TPU v7x, 32 devices: a whole 2x2x4 slice. The times are simulated.
32 devices in a mesh: section: 4 (over y, x), space: 8 (over z, core).
Axes of the slice: x: 2, y: 2, z: 4, core: 2. Of those that a mesh axis runs over, the one named last changes fastest.
Arguments:
- video_clips: bfloat16 [4, 4, 32, 8, 512], P(None, None, 'space'), may hold values from -48 to 48
- code_bits: int32 [4, 1, 8, 2, 18], P(None, None, 'space'), may hold values 0 or 1
- recon_grad: bfloat16 [4, 4, 32, 8, 512], P(None, None, 'space'), may hold values from -14 to 14
- enc_convs: bfloat16 [2, 13824, 512], P(None, 'space'), may hold values from -0.0546875 to 0.0546875
- enc_gains: bfloat16 [2, 512], P(None, 'space'), may hold values from 0.099609375 to 1.8984375
- enc_shifts: bfloat16 [4, 512], P(None, 'space'), may hold values from -2.390625 to 2.390625
- down_weight: bfloat16 [32768, 512], P('space'), may hold values from -0.03125 to 0.03125
- down_bias: bfloat16 [512], P('space'), may hold values from -3 to 3
- down_proj: bfloat16 [512, 18], P('space'), may hold values from -0.25 to 0.25
- up_proj: bfloat16 [512, 18], P('space'), may hold values from -1.5 to 1.5
- up_bias: bfloat16 [512], P('space'), may hold values from -3 to 3
- up_weight: bfloat16 [32768, 512], P('space'), may hold values from -0.25 to 0.25
- upsample_bias: bfloat16 [32768], P('space'), may hold values from -3 to 3
- dec_convs: bfloat16 [2, 13824, 512], P(None, 'space'), may hold values from -0.0546875 to 0.0546875
- dec_gains: bfloat16 [2, 512], P(None, 'space'), may hold values from 0.099609375 to 1.8984375
- dec_shifts: bfloat16 [4, 512], P(None, 'space'), may hold values from -2.390625 to 2.390625
Outputs:
- reconstruction: bfloat16 [4, 4, 32, 8, 512], P(None, None, 'space', None, 'section')
- video_grad: bfloat16 [4, 4, 32, 8, 512], P(None, None, 'space', None, 'section')
- enc_convs_grad: float32 [2, 13824, 512], P(None, 'space')
- enc_gains_grad: float32 [2, 512], P(None, 'space')
- enc_shifts_grad: float32 [4, 512], P(None, 'space')
- down_weight_grad: float32 [32768, 512], P('space')
- down_bias_grad: float32 [512], P('space')
- down_proj_grad: float32 [512, 18], P('space')
- up_proj_grad: float32 [512, 18], P('space')
- up_bias_grad: float32 [512], P('space')
- up_weight_grad: float32 [32768, 512], P('space')
- upsample_bias_grad: float32 [32768], P('space')
- dec_convs_grad: float32 [2, 13824, 512], P(None, 'space')
- dec_gains_grad: float32 [2, 512], P(None, 'space')
- dec_shifts_grad: float32 [4, 512], P(None, 'space')
All inputs are finite; a program needn't handle non-finite values. No bound on the sum of `code_bits` on one device may be relied on, other than what follows from the above.
Results may differ from a plain program's by a relative error of at most 0.014.
Values may be sent and summed in bfloat16 or wider, within the bound.
No kernel may reach another device: no remote copies, remote signals or barrier semaphores. Data moves between devices by JAX's collectives and lax.ppermute only.
A program may use at most 512 MiB of HBM per device.

v0:
```python
from functools import partial

import jax
import jax.numpy as jnp
from jax import lax
from jax.sharding import PartitionSpec as P

GROUPS = 32


def padded_2(block, sides, width):
    for axis, dim in sides:
        count = lax.axis_size(axis)
        forward = [(i, i + 1) for i in range(count - 1)]
        backward = [(target, source) for source, target in forward]
        low = lax.ppermute(
            lax.slice_in_dim(block, block.shape[dim] - width, None, axis=dim), axis, forward
        )
        high = lax.ppermute(lax.slice_in_dim(block, 0, width, axis=dim), axis, backward)
        block = jnp.concatenate([low, block, high], axis=dim)
    return block


def passed_along(block, axis, distance):
    devices = range(lax.axis_size(axis))
    route = [(i - distance, i) for i in devices if i - distance in devices]
    return lax.ppermute(block, axis, route)


def swish_of(values):
    return values * jax.nn.sigmoid(values)


def swish_slope(values):
    logistic = jax.nn.sigmoid(values)
    return logistic * (1.0 + values * (1.0 - logistic))


def group_view(values, groups):
    return values.reshape(values.shape[0], -1, groups, values.shape[-1] // groups)


def norm_forward(values, gain_row, shift_row, groups):
    grouped = group_view(values, groups)
    totals, squares = lax.psum(
        (jnp.sum(grouped, axis=(1, 3)), jnp.sum(grouped * grouped, axis=(1, 3))), "space"
    )
    members = grouped.shape[1] * grouped.shape[3] * lax.axis_size("space")
    average = totals / members
    inv_spread = lax.rsqrt(squares / members - average * average + 1e-06)
    flat_norm = ((grouped - average[:, None, :, None]) * inv_spread[:, None, :, None]).reshape(
        values.shape
    )
    return (flat_norm * gain_row + shift_row, flat_norm, inv_spread)


def norm_backward(gradient, flat_norm, inv_spread, gain_row, groups):
    scaled = group_view(gradient * gain_row, groups)
    grouped = group_view(flat_norm, groups)
    totals, aligned = lax.psum(
        (jnp.sum(scaled, axis=(1, 3)), jnp.sum(scaled * grouped, axis=(1, 3))), "space"
    )
    members = grouped.shape[1] * grouped.shape[3] * lax.axis_size("space")
    result = inv_spread[:, None, :, None] * (
        scaled
        - (totals / members)[:, None, :, None]
        - grouped * (aligned / members)[:, None, :, None]
    )
    return result.reshape(gradient.shape)


def rimmed(full_field):
    padded = padded_2(full_field, (("space", 2),), 1)
    return jnp.pad(padded, ((0, 0), (1, 1), (0, 0), (1, 1), (0, 0)))


def windows(padded, extent, forward):
    frames, height, across = (extent[1], extent[2], extent[3])
    pieces = []
    for tap_index in range(27):
        anchor = (tap_index // 9, tap_index // 3 % 3, tap_index % 3)
        if not forward:
            anchor = (2 - anchor[0], 2 - anchor[1], 2 - anchor[2])
        pieces.append(
            padded[
                :,
                anchor[0] : anchor[0] + frames,
                anchor[1] : anchor[1] + height,
                anchor[2] : anchor[2] + across,
                :,
            ]
        )
    return jnp.stack(pieces, axis=4).reshape(-1, 27 * padded.shape[-1])


def when_busy(active, compute, extents, *operands):

    def resting(*unused):
        return tuple((jnp.zeros(extent_of, jnp.float32) for extent_of in extents))

    return lax.cond(active, compute, resting, *operands)


def conv_ahead(padded, weight_rows, extent):
    return (
        jnp.dot(windows(padded, extent, True), weight_rows, preferred_element_type=jnp.float32),
    )


def conv_behind(padded, grad_low, weight_rows, extent):
    channels = extent[4]
    act_patch = windows(padded[..., :channels], extent, True)
    grad_patch = windows(padded[..., channels:], extent, False)
    weight_grad = lax.dot_general(
        act_patch,
        grad_low.reshape(-1, channels),
        (((0,), (0,)), ((), ())),
        preferred_element_type=jnp.float32,
    )
    spread_back = lax.dot_general(
        grad_patch.reshape(-1, 27, channels),
        weight_rows.reshape(27, channels, channels),
        (((1, 2), (0, 2)), ((), ())),
        preferred_element_type=jnp.float32,
    )
    return (weight_grad, spread_back)


def block_forward(inputs, conv_weights, gains_wide, shifts_wide, active):
    extent = inputs.shape
    channels = extent[4]
    row_total = extent[0] * extent[1] * extent[2] * extent[3]
    normed_one, flat_one, spread_one = norm_forward(inputs, gains_wide[0], shifts_wide[0], GROUPS)
    act_one = swish_of(normed_one).astype(jnp.bfloat16)
    middle = when_busy(
        active,
        partial(conv_ahead, extent=extent),
        ((row_total, channels),),
        rimmed(act_one),
        conv_weights[0],
    )[0]
    middle = (middle + shifts_wide[2]).reshape(extent)
    normed_two, flat_two, spread_two = norm_forward(middle, gains_wide[1], shifts_wide[1], GROUPS)
    act_two = swish_of(normed_two).astype(jnp.bfloat16)
    branch = when_busy(
        active,
        partial(conv_ahead, extent=extent),
        ((row_total, channels),),
        rimmed(act_two),
        conv_weights[1],
    )[0]
    branch = (branch + shifts_wide[3]).reshape(extent)
    return (inputs + branch, (flat_one, spread_one, act_one, flat_two, spread_two, act_two))


def block_backward(cotangent, saved_state, conv_weights, gains_wide, shifts_wide, active):
    flat_one, spread_one, act_one, flat_two, spread_two, act_two = saved_state
    extent = cotangent.shape
    channels = extent[4]
    row_total = extent[0] * extent[1] * extent[2] * extent[3]
    result_extents = ((27 * channels, channels), (row_total, channels))
    normed_one = flat_one * gains_wide[0] + shifts_wide[0]
    normed_two = flat_two * gains_wide[1] + shifts_wide[1]
    outer_low = cotangent.astype(jnp.bfloat16)
    joined_two = rimmed(jnp.concatenate([act_two, outer_low], axis=4))
    conv_two_grad, back_two = when_busy(
        active,
        partial(conv_behind, extent=extent),
        result_extents,
        joined_two,
        outer_low,
        conv_weights[1],
    )
    pre_two = back_two.reshape(extent) * swish_slope(normed_two)
    inner_low = norm_backward(pre_two, flat_two, spread_two, gains_wide[1], GROUPS).astype(
        jnp.bfloat16
    )
    joined_one = rimmed(jnp.concatenate([act_one, inner_low], axis=4))
    conv_one_grad, back_one = when_busy(
        active,
        partial(conv_behind, extent=extent),
        result_extents,
        joined_one,
        inner_low,
        conv_weights[0],
    )
    pre_one = back_one.reshape(extent) * swish_slope(normed_one)
    input_grad = cotangent + norm_backward(pre_one, flat_one, spread_one, gains_wide[0], GROUPS)
    every_axis = (0, 1, 2, 3)
    gain_grads = jnp.stack(
        [jnp.sum(pre_one * flat_one, axis=every_axis), jnp.sum(pre_two * flat_two, axis=every_axis)]
    )
    shift_grads = jnp.stack(
        [
            jnp.sum(pre_one, axis=every_axis),
            jnp.sum(pre_two, axis=every_axis),
            jnp.sum(inner_low.astype(jnp.float32), axis=every_axis),
            jnp.sum(outer_low.astype(jnp.float32), axis=every_axis),
        ]
    )
    return (input_grad, conv_one_grad, conv_two_grad, gain_grads, shift_grads)


def to_latent(full_field):
    extent = full_field.shape
    cubes = full_field.reshape(
        extent[0], extent[1] // 4, 4, extent[2] // 4, 4, extent[3] // 4, 4, extent[4]
    )
    return cubes.transpose(0, 1, 3, 5, 2, 4, 6, 7).reshape(-1, 64 * extent[4])


def from_latent(latent_rows, extent):
    cubes = latent_rows.reshape(
        extent[0], extent[1] // 4, extent[2] // 4, extent[3] // 4, 4, 4, 4, extent[4]
    )
    return cubes.transpose(0, 1, 4, 2, 5, 3, 6, 7).reshape(extent)


def spread_in(row_block, weight_shard):
    offset_parts = lax.all_to_all(row_block, "space", split_axis=1, concat_axis=0, tiled=True)
    return (
        lax.psum_scatter(
            jnp.dot(offset_parts, weight_shard, preferred_element_type=jnp.float32),
            "space",
            scatter_dimension=0,
            tiled=True,
        ),
        offset_parts,
    )


def spread_out(row_block, weight_shard, bias_row):
    gathered = lax.all_gather(row_block, "space", axis=0, tiled=True)
    wide_part = (
        lax.dot_general(
            gathered, weight_shard, (((1,), (1,)), ((), ())), preferred_element_type=jnp.float32
        )
        + bias_row
    )
    return (
        lax.all_to_all(
            wide_part.astype(jnp.bfloat16), "space", split_axis=0, concat_axis=1, tiled=True
        ),
        gathered,
    )


def picked(buffer, index):
    return lax.dynamic_index_in_dim(buffer, index, 0, keepdims=True)


def placed(buffer, value, index, valid):
    previous = lax.dynamic_index_in_dim(buffer, index, 0, keepdims=True)
    return lax.dynamic_update_index_in_dim(buffer, jnp.where(valid, value, previous), index, 0)


def body(
    video_clips,
    code_bits,
    recon_grad,
    enc_convs,
    enc_gains,
    enc_shifts,
    down_weight,
    down_bias,
    down_proj,
    up_proj,
    up_bias,
    up_weight,
    upsample_bias,
    dec_convs,
    dec_gains,
    dec_shifts,
):
    section_index = lax.axis_index("section")
    at_encoder = section_index == 0
    at_down = section_index == 1
    at_up = section_index == 2
    at_decoder = section_index == 3
    local_convs = jnp.where(at_decoder, dec_convs, enc_convs)
    local_gains = jnp.where(at_decoder, dec_gains, enc_gains)
    local_shifts = jnp.where(at_decoder, dec_shifts, enc_shifts)
    mid_weight = jnp.where(at_up, up_weight, down_weight)
    mid_proj = jnp.where(at_up, up_proj, down_proj)
    mid_bias = jnp.where(at_up, up_bias, down_bias)
    fetched = (
        lax.all_gather(local_convs, "space", axis=1, tiled=True),
        lax.all_gather(local_gains, "space", axis=1, tiled=True),
        lax.all_gather(local_shifts, "space", axis=1, tiled=True),
        lax.all_gather(mid_proj, "space", axis=0, tiled=True),
        lax.all_gather(mid_bias, "space", axis=0, tiled=True),
    )
    conv_full = fetched[0]
    gains_wide = fetched[1].astype(jnp.float32)
    shifts_wide = fetched[2].astype(jnp.float32)
    proj_full = fetched[3]
    bias_full = fetched[4].astype(jnp.float32)
    micro_count = video_clips.shape[0]
    extent = (1,) + video_clips.shape[1:]
    channels = extent[4]
    spaces = lax.axis_size("space")
    bit_count = code_bits.shape[4]
    lat_local = code_bits.shape[1] * code_bits.shape[2] * code_bits.shape[3]
    wide_cols = mid_weight.shape[0]
    conv_rows = conv_full.shape[1]
    sign_all = (2 * code_bits - 1).astype(jnp.bfloat16)
    up_shift = jnp.where(at_up, upsample_bias.astype(jnp.float32), 0.0)
    tick_count = micro_count + 4
    block_acc = (
        jnp.zeros((2, conv_rows, channels), jnp.float32),
        jnp.zeros((2, channels), jnp.float32),
        jnp.zeros((4, channels), jnp.float32),
        jnp.zeros((channels, bit_count), jnp.float32),
        jnp.zeros((channels,), jnp.float32),
    )
    mid_acc = (jnp.zeros((wide_cols, channels), jnp.float32), jnp.zeros((wide_cols,), jnp.float32))
    field_stack = (micro_count,) + extent[1:]
    kept_block = (
        jnp.zeros(field_stack, jnp.float32),
        jnp.zeros((micro_count, GROUPS), jnp.float32),
        jnp.zeros(field_stack, jnp.bfloat16),
        jnp.zeros(field_stack, jnp.float32),
        jnp.zeros((micro_count, GROUPS), jnp.float32),
        jnp.zeros(field_stack, jnp.bfloat16),
    )
    kept_parts = jnp.zeros((micro_count, lat_local * spaces, wide_cols), jnp.bfloat16)
    kept_inner = jnp.zeros((micro_count, lat_local, channels), jnp.bfloat16)
    kept_rows = jnp.zeros((micro_count, lat_local * spaces, channels), jnp.bfloat16)
    recon_kept = jnp.zeros(field_stack, jnp.bfloat16)
    video_kept = jnp.zeros(field_stack, jnp.bfloat16)
    ahead_start = jnp.zeros(extent, jnp.bfloat16)
    back_start = jnp.zeros(extent, jnp.bfloat16)
    rows_start = jnp.zeros((lat_local, bit_count), jnp.bfloat16)

    def advance(tick_now, state_now):
        (
            ahead_in,
            back_field,
            back_rows,
            kept_block,
            kept_parts,
            kept_inner,
            kept_rows,
            block_acc,
            mid_acc,
            recon_kept,
            video_kept,
        ) = state_now
        enc_live = tick_now < micro_count
        first_mb = jnp.minimum(tick_now, micro_count - 1)
        dec_live = (tick_now >= 1) & (tick_now <= micro_count)
        dec_mb = jnp.clip(tick_now - 1, 0, micro_count - 1)
        down_live = (tick_now >= 3) & (tick_now <= micro_count + 2)
        down_mb = jnp.clip(tick_now - 3, 0, micro_count - 1)
        up_live = (tick_now >= 2) & (tick_now <= micro_count + 1)
        up_mb = jnp.clip(tick_now - 2, 0, micro_count - 1)
        enc_back_live = tick_now >= 4
        enc_back_mb = jnp.clip(tick_now - 4, 0, micro_count - 1)
        video_now = picked(video_clips, first_mb).astype(jnp.float32)
        block_in = jnp.where(at_encoder, video_now, ahead_in.astype(jnp.float32))
        ahead_live = at_encoder & enc_live | at_decoder & dec_live
        block_out, fresh = block_forward(block_in, conv_full, gains_wide, shifts_wide, ahead_live)
        saved_state = tuple(
            (
                jnp.where(at_decoder, fresh_part, picked(stored_part, enc_back_mb))
                for fresh_part, stored_part in zip(fresh, kept_block)
            )
        )
        recon_now = picked(recon_grad, dec_mb).astype(jnp.float32)
        block_cot = jnp.where(at_decoder, recon_now, back_field.astype(jnp.float32))
        behind_live = at_encoder & enc_back_live | at_decoder & dec_live
        block_grad_in, conv_one_grad, conv_two_grad, gain_grads, shift_grads = block_backward(
            block_cot, saved_state, conv_full, gains_wide, shifts_wide, behind_live
        )
        kept_block = tuple(
            (
                placed(stored_part, fresh_part, first_mb, at_encoder & enc_live)
                for fresh_part, stored_part in zip(fresh, kept_block)
            )
        )
        recon_kept = placed(
            recon_kept, block_out.astype(jnp.bfloat16), dec_mb, at_decoder & dec_live
        )
        video_kept = placed(
            video_kept, block_grad_in.astype(jnp.bfloat16), enc_back_mb, at_encoder & enc_back_live
        )
        sign_now = picked(sign_all, first_mb).reshape(-1, bit_count)
        hidden_low = (
            lax.dot_general(
                sign_now, proj_full, (((1,), (1,)), ((), ())), preferred_element_type=jnp.float32
            )
            + bias_full
        ).astype(jnp.bfloat16)
        inner_grad = lax.dot_general(
            back_rows, proj_full, (((1,), (1,)), ((), ())), preferred_element_type=jnp.float32
        ).astype(jnp.bfloat16)
        grown_rows, gathered = spread_out(
            jnp.where(at_up, hidden_low, inner_grad), mid_weight, up_shift
        )
        in_sum, in_parts = spread_in(
            to_latent(jnp.where(at_down, ahead_in, back_field)), mid_weight
        )
        inner_low = (in_sum + bias_full).astype(jnp.bfloat16)
        hidden_grad = in_sum.astype(jnp.bfloat16)
        parts_then = picked(kept_parts, down_mb)[0]
        inner_then = picked(kept_inner, down_mb)[0]
        rows_then = picked(kept_rows, up_mb)[0]
        sign_then = picked(sign_all, up_mb).reshape(-1, bit_count)
        mid_live = at_up & up_live | at_down & down_live
        weight_part = lax.dot_general(
            jnp.where(at_up, in_parts, parts_then),
            jnp.where(at_up, rows_then, gathered),
            (((0,), (0,)), ((), ())),
            preferred_element_type=jnp.float32,
        )
        upsample_part = jnp.sum(in_parts.astype(jnp.float32), axis=0)
        up_proj_part = lax.dot_general(
            hidden_grad, sign_then, (((0,), (0,)), ((), ())), preferred_element_type=jnp.float32
        )
        down_proj_part = lax.dot_general(
            inner_then, back_rows, (((0,), (0,)), ((), ())), preferred_element_type=jnp.float32
        )
        proj_part = jnp.where(mid_live, jnp.where(at_up, up_proj_part, down_proj_part), 0.0)
        bias_part = jnp.where(
            mid_live,
            jnp.where(
                at_up,
                jnp.sum(hidden_grad.astype(jnp.float32), axis=0),
                jnp.sum(inner_grad.astype(jnp.float32), axis=0),
            ),
            0.0,
        )
        mid_acc = (
            mid_acc[0] + jnp.where(mid_live, weight_part, 0.0),
            mid_acc[1] + jnp.where(at_up & up_live, upsample_part, 0.0),
        )
        sign_grad = jnp.dot(hidden_grad, proj_full, preferred_element_type=jnp.float32).astype(
            jnp.bfloat16
        )
        kept_parts = placed(kept_parts, in_parts[None], dec_mb, at_down & dec_live)
        kept_inner = placed(kept_inner, inner_low[None], dec_mb, at_down & dec_live)
        kept_rows = placed(kept_rows, gathered[None], first_mb, at_up & enc_live)
        grown_field = from_latent(grown_rows, extent)
        ahead_send = jnp.where(at_encoder, block_out.astype(jnp.bfloat16), grown_field)
        back_send = jnp.where(at_decoder, block_grad_in.astype(jnp.bfloat16), grown_field)
        ahead_in = passed_along(ahead_send, "section", 1)
        back_field, back_rows = passed_along((back_send, sign_grad), "section", -1)
        gain_grads = jnp.where(behind_live, gain_grads, 0.0)
        shift_grads = jnp.where(behind_live, shift_grads, 0.0)
        one_share, two_share, gain_share, shift_share, proj_share, bias_share = (
            conv_one_grad,
            conv_two_grad,
            gain_grads,
            shift_grads,
            proj_part,
            bias_part,
        )
        block_acc = (
            block_acc[0].at[0].add(one_share).at[1].add(two_share),
            block_acc[1] + gain_share,
            block_acc[2] + shift_share,
            block_acc[3] + proj_share,
            block_acc[4] + bias_share,
        )
        return (
            ahead_in,
            back_field,
            back_rows,
            kept_block,
            kept_parts,
            kept_inner,
            kept_rows,
            block_acc,
            mid_acc,
            recon_kept,
            video_kept,
        )

    start_state = (
        ahead_start,
        back_start,
        rows_start,
        kept_block,
        kept_parts,
        kept_inner,
        kept_rows,
        block_acc,
        mid_acc,
        recon_kept,
        video_kept,
    )
    final_state = lax.fori_loop(0, tick_count, advance, start_state)
    block_acc, mid_acc, recon_kept, video_kept = (
        final_state[7],
        final_state[8],
        final_state[9],
        final_state[10],
    )
    conv_share, gain_share, shift_share, proj_share, bias_share = (
        lax.psum_scatter(block_acc[0], "space", scatter_dimension=1, tiled=True),
        lax.psum_scatter(block_acc[1], "space", scatter_dimension=1, tiled=True),
        lax.psum_scatter(block_acc[2], "space", scatter_dimension=1, tiled=True),
        lax.psum_scatter(block_acc[3], "space", scatter_dimension=0, tiled=True),
        lax.psum_scatter(block_acc[4], "space", scatter_dimension=0, tiled=True),
    )
    mid_weight_grad, upsample_grad = mid_acc
    encoder_mask = at_encoder.astype(jnp.float32)
    down_mask = at_down.astype(jnp.float32)
    up_mask = at_up.astype(jnp.float32)
    decoder_mask = at_decoder.astype(jnp.float32)
    gathered_grads = (
        lax.psum((conv_share * encoder_mask).astype(jnp.bfloat16), "section").astype(jnp.float32),
        lax.psum((gain_share * encoder_mask).astype(jnp.bfloat16), "section").astype(jnp.float32),
        lax.psum((shift_share * encoder_mask).astype(jnp.bfloat16), "section").astype(jnp.float32),
        lax.psum((mid_weight_grad * down_mask).astype(jnp.bfloat16), "section").astype(jnp.float32),
        lax.psum((bias_share * down_mask).astype(jnp.bfloat16), "section").astype(jnp.float32),
        lax.psum((proj_share * down_mask).astype(jnp.bfloat16), "section").astype(jnp.float32),
        lax.psum((proj_share * up_mask).astype(jnp.bfloat16), "section").astype(jnp.float32),
        lax.psum((bias_share * up_mask).astype(jnp.bfloat16), "section").astype(jnp.float32),
        lax.psum((mid_weight_grad * up_mask).astype(jnp.bfloat16), "section").astype(jnp.float32),
        lax.psum((upsample_grad * up_mask).astype(jnp.bfloat16), "section").astype(jnp.float32),
        lax.psum((conv_share * decoder_mask).astype(jnp.bfloat16), "section").astype(jnp.float32),
        lax.psum((gain_share * decoder_mask).astype(jnp.bfloat16), "section").astype(jnp.float32),
        lax.psum((shift_share * decoder_mask).astype(jnp.bfloat16), "section").astype(jnp.float32),
    )
    recon_home, video_home = (
        lax.psum_scatter(
            jnp.where(at_decoder, recon_kept.astype(jnp.float32), 0.0).astype(jnp.bfloat16),
            "section",
            scatter_dimension=4,
            tiled=True,
        ).astype(jnp.float32),
        lax.psum_scatter(
            jnp.where(at_encoder, video_kept.astype(jnp.float32), 0.0).astype(jnp.bfloat16),
            "section",
            scatter_dimension=4,
            tiled=True,
        ).astype(jnp.float32),
    )
    return (recon_home.astype(jnp.bfloat16), video_home.astype(jnp.bfloat16)) + tuple(
        gathered_grads
    )


def solution(mesh):
    return jax.shard_map(
        body,
        mesh=mesh,
        in_specs=(
            P(None, None, "space", None, None),
            P(None, None, "space", None, None),
            P(None, None, "space", None, None),
            P(None, "space", None),
            P(None, "space"),
            P(None, "space"),
            P("space", None),
            P("space"),
            P("space", None),
            P("space", None),
            P("space"),
            P("space", None),
            P("space"),
            P(None, "space", None),
            P(None, "space"),
            P(None, "space"),
        ),
        out_specs=(
            P(None, None, "space", None, "section"),
            P(None, None, "space", None, "section"),
            P(None, "space", None),
            P(None, "space"),
            P(None, "space"),
            P("space", None),
            P("space"),
            P("space", None),
            P("space", None),
            P("space"),
            P("space", None),
            P("space"),
            P(None, "space", None),
            P(None, "space"),
            P(None, "space"),
        ),
        check_vma=False,
    )
```

profile of v0, /device:TPU:0, one launch (start us, length us, event | category | flops | bytes accessed | tf_op | source)
XLA Modules:
  0.0 3926.8 jit_solution(16633062066635960689)
XLA Ops:
  93.3 167.2 %all-gather.9.cloned.1.call-done = bf16[2,13824,512]{2,1,0:T(8,128)(2,1)} async-done(((bf16[2,1728,512]{2,1,0:T(8,128)(2,1)}), bf16[2,13824,512]{2,1,0:T(8,128)(2,1)}) %all-gather.9.cloned.1.call-update) | async-done | bytes 28311568 | tf_op jit(solution)/shard_map/all_gather | solution.py:287
  284.9 2634.8 %while.58 = (s32[]{:T(128)}, bf16[1,4,4,8,512]{4,3,2,1,0:T(8,128)(2,1)S(1)}, bf16[1,4,4,8,512]{4,3,2,1,0:T(8,128)(2,1)S(1)}, bf16[2,18]{1,0:T(2,128)(2,1)S(1)}, ...) while((s32[]{:T(128)}, ...), condition=%wide.region_43.44_spmd.clone, body=%wide.region_0.43_spmd.clone.sunk | while | flops 11105680384 | bytes 535503936 | solution.py:492
  493.3 29.3 fusion.410
  776.3 29.3 fusion.410
  1061.8 29.3 fusion.410
  1138.8 33.2 collective-permute-start.8
  1376.7 29.3 fusion.410
  1453.6 69.9 %collective-permute-start.8 = (bf16[1,4,4,8,512]{4,3,2,1,0:T(8,128)(2,1)S(1)}, bf16[1,4,4,8,512]{4,3,2,1,0:T(8,128)(2,1)S(1)}, u32[]{:S(2)}, u32[]{:S(2)}) collective-permute-start(bf16[1,4,4,8,512]{4,3,2,1,0:T(8,128)(2,1)S(1)} %get-tuple-element.1649), channel_id=1, source_target_pairs={{0,8},{8,16},{16,24},{1,9},{9,17},{17,25},{2,10},{10,18},{18,26},{... | collective-permute-start | bytes 393224 | tf_op jit(solution)/shard_map/while/body/eval_jaxpr/ppermute | solution.py:27
  1635.9 43.2 %conditional.13 = (f32[1,4,4,8,512]{4,3,2,1,0:T(8,128)}, f32[1,13824,512]{2,1,0:T(8,128)}) conditional(s32[]{:T(128)} %convert_element_type.574, () %tuple.208, (bf16[1,4,6,8,1024]{4,3,2,1,0:T(8,128)(2,1)S(1)}, bf16[1,13824,512]{2,1,0:T(8,128)(2,1)}, bf16[1,4,4,8,512]{4,3,2,1,0:T(8,128)(2,1)S(1)}) %tuple.211), branch_computations={%region_17.17_spmd, %region_18.18_spmd} | conditional | flops 3623878656 | bytes 84279344 | solution.py:101
  1706.2 43.2 %conditional.14 = (f32[1,4,4,8,512]{4,3,2,1,0:T(8,128)}, f32[1,13824,512]{2,1,0:T(8,128)}) conditional(s32[]{:T(128)} %convert_element_type.574, () %tuple.207, (bf16[1,4,6,8,1024]{4,3,2,1,0:T(8,128)(2,1)S(1)}, bf16[1,13824,512]{2,1,0:T(8,128)(2,1)}, bf16[1,4,4,8,512]{4,3,2,1,0:T(8,128)(2,1)S(1)}) %tuple.212), branch_computations={%region_25.25_spmd, %region_26.26_spmd} | conditional | flops 3623878656 | bytes 84279344 | solution.py:101
  1778.5 29.3 fusion.410
  1987.4 43.2 %conditional.13 = (f32[1,4,4,8,512]{4,3,2,1,0:T(8,128)}, f32[1,13824,512]{2,1,0:T(8,128)}) conditional(s32[]{:T(128)} %convert_element_type.574, () %tuple.208, (bf16[1,4,6,8,1024]{4,3,2,1,0:T(8,128)(2,1)S(1)}, bf16[1,13824,512]{2,1,0:T(8,128)(2,1)}, bf16[1,4,4,8,512]{4,3,2,1,0:T(8,128)(2,1)S(1)}) %tuple.211), branch_computations={%region_17.17_spmd, %region_18.18_spmd} | conditional | flops 3623878656 | bytes 84279344 | solution.py:101
  2057.8 43.2 %conditional.14 = (f32[1,4,4,8,512]{4,3,2,1,0:T(8,128)}, f32[1,13824,512]{2,1,0:T(8,128)}) conditional(s32[]{:T(128)} %convert_element_type.574, () %tuple.207, (bf16[1,4,6,8,1024]{4,3,2,1,0:T(8,128)(2,1)S(1)}, bf16[1,13824,512]{2,1,0:T(8,128)(2,1)}, bf16[1,4,4,8,512]{4,3,2,1,0:T(8,128)(2,1)S(1)}) %tuple.212), branch_computations={%region_25.25_spmd, %region_26.26_spmd} | conditional | flops 3623878656 | bytes 84279344 | solution.py:101
  2130.0 29.3 fusion.410
  2339.0 43.2 %conditional.13 = (f32[1,4,4,8,512]{4,3,2,1,0:T(8,128)}, f32[1,13824,512]{2,1,0:T(8,128)}) conditional(s32[]{:T(128)} %convert_element_type.574, () %tuple.208, (bf16[1,4,6,8,1024]{4,3,2,1,0:T(8,128)(2,1)S(1)}, bf16[1,13824,512]{2,1,0:T(8,128)(2,1)}, bf16[1,4,4,8,512]{4,3,2,1,0:T(8,128)(2,1)S(1)}) %tuple.211), branch_computations={%region_17.17_spmd, %region_18.18_spmd} | conditional | flops 3623878656 | bytes 84279344 | solution.py:101
  2409.3 43.2 %conditional.14 = (f32[1,4,4,8,512]{4,3,2,1,0:T(8,128)}, f32[1,13824,512]{2,1,0:T(8,128)}) conditional(s32[]{:T(128)} %convert_element_type.574, () %tuple.207, (bf16[1,4,6,8,1024]{4,3,2,1,0:T(8,128)(2,1)S(1)}, bf16[1,13824,512]{2,1,0:T(8,128)(2,1)}, bf16[1,4,4,8,512]{4,3,2,1,0:T(8,128)(2,1)S(1)}) %tuple.212), branch_computations={%region_25.25_spmd, %region_26.26_spmd} | conditional | flops 3623878656 | bytes 84279344 | solution.py:101
  2481.6 29.3 fusion.410
  2674.7 43.2 %conditional.13 = (f32[1,4,4,8,512]{4,3,2,1,0:T(8,128)}, f32[1,13824,512]{2,1,0:T(8,128)}) conditional(s32[]{:T(128)} %convert_element_type.574, () %tuple.208, (bf16[1,4,6,8,1024]{4,3,2,1,0:T(8,128)(2,1)S(1)}, bf16[1,13824,512]{2,1,0:T(8,128)(2,1)}, bf16[1,4,4,8,512]{4,3,2,1,0:T(8,128)(2,1)S(1)}) %tuple.211), branch_computations={%region_17.17_spmd, %region_18.18_spmd} | conditional | flops 3623878656 | bytes 84279344 | solution.py:101
  2745.1 43.2 %conditional.14 = (f32[1,4,4,8,512]{4,3,2,1,0:T(8,128)}, f32[1,13824,512]{2,1,0:T(8,128)}) conditional(s32[]{:T(128)} %convert_element_type.574, () %tuple.207, (bf16[1,4,6,8,1024]{4,3,2,1,0:T(8,128)(2,1)S(1)}, bf16[1,13824,512]{2,1,0:T(8,128)(2,1)}, bf16[1,4,4,8,512]{4,3,2,1,0:T(8,128)(2,1)S(1)}) %tuple.212), branch_computations={%region_25.25_spmd, %region_26.26_spmd} | conditional | flops 3623878656 | bytes 84279344 | solution.py:101
  2817.3 29.3 fusion.410
  2979.1 481.5 %reduce-scatter.17.cloned.1.call-done = f32[2,1728,512]{2,1,0:T(8,128)} async-done(((f32[2,13824,512]{2,1,0:T(8,128)}), f32[2,1728,512]{2,1,0:T(8,128)}) %reduce-scatter.17.cloned.1.call-update) | async-done | bytes 7077904 | tf_op jit(solution)/shard_map/reduce_scatter | solution.py:500
  3492.5 29.8 reduce-scatter.25.cloned.1.call-done
  3523.1 29.9 reduce-scatter.27.cloned.1.call-done
  3612.7 287.8 %all-reduce.23.cloned.1.call-done = (bf16[2,1728,512]{2,1,0:T(8,128)(2,1)}, bf16[4096,512]{1,0:T(8,128)(2,1)}, bf16[4096,512]{1,0:T(8,128)(2,1)}, bf16[2,1728,512]{2,1,0:T(8,128)(2,1)}) async-done(((bf16[2,1728,512]{2,1,0:T(8,128)(2,1)}, bf16[4096,512]{1,0:T(8,128)(2,1)}, bf16[4096,512]{1,0:T(8,128)(2,1)}, bf16[2,1728,512]{2,1,0:T(8,128)(2,1)}), (bf16[2,1728,512]{2,1,0:T(8,128)(2,1)}, ...) | async-done | bytes 15466512 | tf_op jit(solution)/shard_map/psum | solution.py:512
  (2963 shorter events, 2679.3 us)
Async XLA Ops:
  7.2 253.3 %all-gather.9.cloned.1.call-start = ((), (), s32[]{:S(2)}) async-start(), calls=%async_computation.8 | async-start | bytes 31850496 | tf_op jit(solution)/shard_map/all_gather | solution.py:287
  11.5 3449.0 %reduce-scatter.17.cloned.1.call-start = ((), (), s32[]{:S(2)}) async-start(), calls=%async_computation.9 | async-start | bytes 63700992 | tf_op jit(solution)/shard_map/reduce_scatter | solution.py:500
  323.3 200.7 %all-to-all-start = ((bf16[2,8,4096]{2,0,1:T(2,128)(2,1)}), bf16[2,8,4096]{2,0,1:T(2,128)(2,1)}, u32[]{:S(2)}, u32[]{:S(2)}) async-start(bf16[2,8,4096]{2,0,1:T(2,128)(2,1)} %copy.732), calls=%async_computation | async-start | bytes 262144 | tf_op jit(solution)/shard_map/while/body/eval_jaxpr/all_to_all | solution.py:220
  327.3 45.9 %collective-permute-start = (bf16[1,4,1,8,512]{4,3,2,1,0:T(8,128)(2,1)S(1)}, bf16[1,4,1,8,512]{4,3,2,1,0:T(8,128)(2,1)S(1)}, u32[]{:S(2)}, u32[]{:S(2)}) collective-permute-start(bf16[1,4,1,8,512]{4,3,2,1,0:T(8,128)(2,1)S(1)} %get-tuple-element.1610), channel_id=1, source_target_pairs={{1,0},{2,1},{3,2},{4,3},{5,4},{6,5},{7,6},{9,8},{10,9},{11,10},{12... | collective-permute-start | bytes 98312 | tf_op jit(solution)/shard_map/while/body/eval_jaxpr/ppermute | solution.py:19
  606.3 200.7 %all-to-all-start = ((bf16[2,8,4096]{2,0,1:T(2,128)(2,1)}), bf16[2,8,4096]{2,0,1:T(2,128)(2,1)}, u32[]{:S(2)}, u32[]{:S(2)}) async-start(bf16[2,8,4096]{2,0,1:T(2,128)(2,1)} %copy.732), calls=%async_computation | async-start | bytes 262144 | tf_op jit(solution)/shard_map/while/body/eval_jaxpr/all_to_all | solution.py:220
  610.3 45.9 %collective-permute-start = (bf16[1,4,1,8,512]{4,3,2,1,0:T(8,128)(2,1)S(1)}, bf16[1,4,1,8,512]{4,3,2,1,0:T(8,128)(2,1)S(1)}, u32[]{:S(2)}, u32[]{:S(2)}) collective-permute-start(bf16[1,4,1,8,512]{4,3,2,1,0:T(8,128)(2,1)S(1)} %get-tuple-element.1610), channel_id=1, source_target_pairs={{1,0},{2,1},{3,2},{4,3},{5,4},{6,5},{7,6},{9,8},{10,9},{11,10},{12... | collective-permute-start | bytes 98312 | tf_op jit(solution)/shard_map/while/body/eval_jaxpr/ppermute | solution.py:19
  891.8 200.7 %all-to-all-start = ((bf16[2,8,4096]{2,0,1:T(2,128)(2,1)}), bf16[2,8,4096]{2,0,1:T(2,128)(2,1)}, u32[]{:S(2)}, u32[]{:S(2)}) async-start(bf16[2,8,4096]{2,0,1:T(2,128)(2,1)} %copy.732), calls=%async_computation | async-start | bytes 262144 | tf_op jit(solution)/shard_map/while/body/eval_jaxpr/all_to_all | solution.py:220
  895.8 45.9 %collective-permute-start = (bf16[1,4,1,8,512]{4,3,2,1,0:T(8,128)(2,1)S(1)}, bf16[1,4,1,8,512]{4,3,2,1,0:T(8,128)(2,1)S(1)}, u32[]{:S(2)}, u32[]{:S(2)}) collective-permute-start(bf16[1,4,1,8,512]{4,3,2,1,0:T(8,128)(2,1)S(1)} %get-tuple-element.1610), channel_id=1, source_target_pairs={{1,0},{2,1},{3,2},{4,3},{5,4},{6,5},{7,6},{9,8},{10,9},{11,10},{12... | collective-permute-start | bytes 98312 | tf_op jit(solution)/shard_map/while/body/eval_jaxpr/ppermute | solution.py:19
  1134.6 51.5 %collective-permute-start.10 = (bf16[2,18]{1,0:T(2,128)(2,1)}, bf16[2,18]{1,0:T(2,128)(2,1)}, u32[]{:S(2)}, u32[]{:S(2)}) collective-permute-start(bf16[2,18]{1,0:T(2,128)(2,1)} %convolution_convert_fusion.3), channel_id=1, source_target_pairs={{8,0},{16,8},{24,16},{9,1},{17,9},{25,17},{10,2},{18,10},{26,18},{... | collective-permute-start | bytes 224 | tf_op jit(solution)/shard_map/while/body/eval_jaxpr/ppermute | solution.py:27
  1138.8 48.0 %collective-permute-start.8 = (bf16[1,4,4,8,512]{4,3,2,1,0:T(8,128)(2,1)S(1)}, bf16[1,4,4,8,512]{4,3,2,1,0:T(8,128)(2,1)S(1)}, u32[]{:S(2)}, u32[]{:S(2)}) collective-permute-start(bf16[1,4,4,8,512]{4,3,2,1,0:T(8,128)(2,1)S(1)} %get-tuple-element.1649), channel_id=1, source_target_pairs={{0,8},{8,16},{16,24},{1,9},{9,17},{17,25},{2,10},{10,18},{18,26},{... | collective-permute-start | bytes 393224 | tf_op jit(solution)/shard_map/while/body/eval_jaxpr/ppermute | solution.py:27
  1206.7 200.6 %all-to-all-start = ((bf16[2,8,4096]{2,0,1:T(2,128)(2,1)}), bf16[2,8,4096]{2,0,1:T(2,128)(2,1)}, u32[]{:S(2)}, u32[]{:S(2)}) async-start(bf16[2,8,4096]{2,0,1:T(2,128)(2,1)} %copy.732), calls=%async_computation | async-start | bytes 262144 | tf_op jit(solution)/shard_map/while/body/eval_jaxpr/all_to_all | solution.py:220
  1210.7 45.9 %collective-permute-start = (bf16[1,4,1,8,512]{4,3,2,1,0:T(8,128)(2,1)S(1)}, bf16[1,4,1,8,512]{4,3,2,1,0:T(8,128)(2,1)S(1)}, u32[]{:S(2)}, u32[]{:S(2)}) collective-permute-start(bf16[1,4,1,8,512]{4,3,2,1,0:T(8,128)(2,1)S(1)} %get-tuple-element.1610), channel_id=1, source_target_pairs={{1,0},{2,1},{3,2},{4,3},{5,4},{6,5},{7,6},{9,8},{10,9},{11,10},{12... | collective-permute-start | bytes 98312 | tf_op jit(solution)/shard_map/while/body/eval_jaxpr/ppermute | solution.py:19
  1449.4 88.2 %collective-permute-start.10 = (bf16[2,18]{1,0:T(2,128)(2,1)}, bf16[2,18]{1,0:T(2,128)(2,1)}, u32[]{:S(2)}, u32[]{:S(2)}) collective-permute-start(bf16[2,18]{1,0:T(2,128)(2,1)} %convolution_convert_fusion.3), channel_id=1, source_target_pairs={{8,0},{16,8},{24,16},{9,1},{17,9},{25,17},{10,2},{18,10},{26,18},{... | collective-permute-start | bytes 224 | tf_op jit(solution)/shard_map/while/body/eval_jaxpr/ppermute | solution.py:27
  1453.6 84.7 %collective-permute-start.8 = (bf16[1,4,4,8,512]{4,3,2,1,0:T(8,128)(2,1)S(1)}, bf16[1,4,4,8,512]{4,3,2,1,0:T(8,128)(2,1)S(1)}, u32[]{:S(2)}, u32[]{:S(2)}) collective-permute-start(bf16[1,4,4,8,512]{4,3,2,1,0:T(8,128)(2,1)S(1)} %get-tuple-element.1649), channel_id=1, source_target_pairs={{0,8},{8,16},{16,24},{1,9},{9,17},{17,25},{2,10},{10,18},{18,26},{... | collective-permute-start | bytes 393224 | tf_op jit(solution)/shard_map/while/body/eval_jaxpr/ppermute | solution.py:27
  1558.2 250.9 %all-to-all-start = ((bf16[2,8,4096]{2,0,1:T(2,128)(2,1)}), bf16[2,8,4096]{2,0,1:T(2,128)(2,1)}, u32[]{:S(2)}, u32[]{:S(2)}) async-start(bf16[2,8,4096]{2,0,1:T(2,128)(2,1)} %copy.732), calls=%async_computation | async-start | bytes 262144 | tf_op jit(solution)/shard_map/while/body/eval_jaxpr/all_to_all | solution.py:220
  1909.7 250.9 %all-to-all-start = ((bf16[2,8,4096]{2,0,1:T(2,128)(2,1)}), bf16[2,8,4096]{2,0,1:T(2,128)(2,1)}, u32[]{:S(2)}, u32[]{:S(2)}) async-start(bf16[2,8,4096]{2,0,1:T(2,128)(2,1)} %copy.732), calls=%async_computation | async-start | bytes 262144 | tf_op jit(solution)/shard_map/while/body/eval_jaxpr/all_to_all | solution.py:220
  2261.3 250.9 %all-to-all-start = ((bf16[2,8,4096]{2,0,1:T(2,128)(2,1)}), bf16[2,8,4096]{2,0,1:T(2,128)(2,1)}, u32[]{:S(2)}, u32[]{:S(2)}) async-start(bf16[2,8,4096]{2,0,1:T(2,128)(2,1)} %copy.732), calls=%async_computation | async-start | bytes 262144 | tf_op jit(solution)/shard_map/while/body/eval_jaxpr/all_to_all | solution.py:220
  2597.1 250.9 %all-to-all-start = ((bf16[2,8,4096]{2,0,1:T(2,128)(2,1)}), bf16[2,8,4096]{2,0,1:T(2,128)(2,1)}, u32[]{:S(2)}, u32[]{:S(2)}) async-start(bf16[2,8,4096]{2,0,1:T(2,128)(2,1)} %copy.732), calls=%async_computation | async-start | bytes 262144 | tf_op jit(solution)/shard_map/while/body/eval_jaxpr/all_to_all | solution.py:220
  2919.8 571.9 %reduce-scatter.23.cloned.1.call-start = ((), (), s32[]{:S(2)}) async-start(), calls=%async_computation.12 | async-start | bytes 294912
  2921.3 601.0 %reduce-scatter.25.cloned.1.call-start = ((), (), s32[]{:S(2)}) async-start(), calls=%async_computation.13 | async-start | bytes 294912
  2922.2 630.9 %reduce-scatter.27.cloned.1.call-start = ((), (), s32[]{:S(2)}) async-start(), calls=%async_computation.14 | async-start | bytes 294912
  2923.2 655.6 %reduce-scatter.21.cloned.1.call-start = ((), (), s32[]{:S(2)}) async-start(), calls=%async_computation.11 | async-start | bytes 655360
  2947.0 659.7 %reduce-scatter.19.cloned.1.call-start = ((), (), s32[]{:S(2)}) async-start(), calls=%async_computation.10 | async-start | bytes 655360
  2970.5 930.0 %all-reduce.23.cloned.1.call-start = ((), (), s32[]{:S(2)}) async-start(), calls=%async_computation.15 | async-start | bytes 30932992 | tf_op jit(solution)/shard_map/psum | solution.py:512
  (613 other events, 14959.4 us)
Sparse Core Ops, SparseCore 0:
  11.7 248.7 all-gather.8
  2919.9 540.6 reduce-scatter.16
  3462.9 28.6 reduce-scatter.22
  3493.7 28.5 reduce-scatter.24
  3524.5 28.5 reduce-scatter.26
  3555.8 23.0 reduce-scatter.20
  3581.9 24.7 reduce-scatter.18
  3611.8 288.5 all-reduce.22
where the time goes:
time: 3940 us; the launch traced here: 3930 us
  waiting for transfers between devices  1060 us (27%)
  blocking collectives  779 us (20%)
  other arithmetic  671 us (17%)
  local copies, waits for them, and re-layouts  605 us (15%)
  starting transfers between devices  380 us (10%)
  matrix products  366 us (9%)
  loops' own time  44.6 us (1%)
    reduce_scatter x1, waiting for transfers between devices, body(): lax.psum_scatter(block_acc[0], 'space', scatter_dimension=1, tiled=True)  482 us
    scatter-add x16, other arithmetic, advance(): block_acc[0].at[0].add(one_share).at[1].add(two_share)  466 us
    psum x16, blocking collectives, norm_backward(): lax.psum((jnp.sum(scaled, axis=(1, 3)), jnp.sum(scaled * grouped, axis=(1...  335 us
    psum x1, waiting for transfers between devices, body(): lax.psum((conv_share * encoder_mask).astype(jnp.bfloat16), 'section')  288 us
    psum x16, blocking collectives, norm_forward(): lax.psum((jnp.sum(grouped, axis=(1, 3)), jnp.sum(grouped * grouped, axis=...  236 us
    ppermute x24, starting transfers between devices, passed_along(): return lax.ppermute(block, axis, route)  181 us
    slice x8, local copies, waits for them, and re-layouts, block_forward(): conv_weights[1]  169 us
    all_gather x1, waiting for transfers between devices, body(): lax.all_gather(local_convs, 'space', axis=1, tiled=True)  167 us
  transfers between devices with their start and end apart: 112, of which 16 were waited for; matrix products, arithmetic and copies ran while one was open for 38% of the time, Pallas kernels for 0%

commit v1 on v0

v1 whole, which is shorter than its diff:
```python
from functools import partial

import jax
import jax.numpy as jnp
from jax import lax
from jax.experimental import pallas as pl
from jax.experimental.pallas import tpu as pltpu
from jax.sharding import PartitionSpec as P

GROUPS = 32
CUBE = 4
LANES = 128
BF16 = jnp.bfloat16
F32 = jnp.float32


def swish_slope(values, logistic):
    return logistic * (1.0 + values * (1.0 - logistic))


def chips_of():
    return lax.axis_size("space") // 2


def along_chips(value, step):
    chips = chips_of()
    route = [(i, (i // 2 + step) % chips * 2 + i % 2) for i in range(2 * chips)]
    return lax.ppermute(value, "space", route)


def to_twin(value):
    return lax.ppermute(value, "space", [(i, i ^ 1) for i in range(lax.axis_size("space"))])


def here():
    index = lax.axis_index("space")
    return index // 2, index % 2


def ring_is_short():
    return chips_of() <= 4


def picked(value, index, axis=0):
    return lax.dynamic_index_in_dim(value, index, axis, keepdims=False)


def gathered(value):
    chips = chips_of()
    if not ring_is_short():
        return lax.all_gather(value, "space", axis=0).reshape((chips, 2) + value.shape)
    z, core = here()
    pieces = [value] + [along_chips(value, step) for step in range(1, chips)]
    stack = jnp.zeros((chips,) + value.shape, value.dtype)
    for step, piece in enumerate(pieces):
        stack = lax.dynamic_update_index_in_dim(stack, piece, (z - step) % chips, 0)
    other = to_twin(stack)
    first = jnp.where(core == 0, stack, other)
    second = jnp.where(core == 0, other, stack)
    return jnp.stack([first, second], axis=1)


def scattered(parts):
    chips = chips_of()
    if not ring_is_short():
        flat = parts.reshape((2 * chips,) + parts.shape[2:])
        return lax.psum_scatter(flat, "space", scatter_dimension=0, tiled=False)
    z, core = here()
    mine = picked(parts, core, 1)
    mine = mine + to_twin(picked(parts, 1 - core, 1).astype(BF16)).astype(F32)
    total = picked(mine, z)
    for step in range(1, chips):
        sent = picked(mine, (z + step) % chips).astype(BF16)
        total = total + along_chips(sent, step).astype(F32)
    return total


def summed(value):
    if not ring_is_short():
        return lax.psum(value, "space")
    total = value
    for step in range(1, chips_of()):
        total = total + along_chips(value, step)
    return total + to_twin(total)


def pair_summed(value):
    return value + to_twin(value)


def to_blocks(field):
    chips = chips_of()
    cubes, rows, channels = field.shape
    split = field.reshape(2, cubes // 2, rows, chips, channels // chips)
    return split.transpose(3, 0, 1, 2, 4)


def from_blocks(blocks):
    chips, _, half, rows, width = blocks.shape
    return blocks.transpose(1, 2, 3, 0, 4).reshape(2 * half, rows, chips * width)


def own_block(field):
    z, core = here()
    cubes, rows, channels = field.shape
    width = channels // chips_of()
    return lax.dynamic_slice(field, (core * (cubes // 2), 0, z * width), (cubes // 2, rows, width))


def own_lanes(row):
    z, _ = here()
    width = row.shape[-1] // chips_of()
    return lax.dynamic_slice_in_dim(row, z * width, width, row.ndim - 1)


def cubes_of(slab):
    frames, height, across, channels = slab.shape
    split = slab.reshape(frames, height, across // CUBE, CUBE, channels)
    return split.transpose(0, 1, 3, 2, 4).reshape(-1, across // CUBE, channels)


def slab_of(cubes, extent):
    frames, height, across, channels = extent
    split = cubes.reshape(frames, height, CUBE, across // CUBE, channels)
    return split.transpose(0, 1, 3, 2, 4).reshape(extent)


def field_of(slabs):
    chips, _, cubes, across, channels = slabs.shape
    flat = slabs.reshape(2 * chips, cubes, across, channels)
    return flat.transpose(1, 0, 2, 3).reshape(cubes, 2 * chips * across, channels)


def group_means(sums, width, members):
    groups = sums.reshape(sums.shape[:-1] + (-1, width))
    wide = jnp.broadcast_to(jnp.sum(groups, axis=-1, keepdims=True), groups.shape)
    return wide.reshape(sums.shape) / members


def rimmed(field, across):
    cubes, rows, channels = field.shape
    view = field.reshape(CUBE, CUBE, CUBE, rows // across, across, channels)
    none = (0, 0)
    above = jnp.pad(view[:, -1:, :, :-1], (none, none, none, (1, 0), none, none))
    below = jnp.pad(view[:, :1, :, 1:], (none, none, none, (0, 1), none, none))
    view = jnp.concatenate([above, view, below], axis=1)
    left = jnp.pad(view[:, :, -1:, :, :-1], (none, none, none, none, (1, 0), none))
    right = jnp.pad(view[:, :, :1, :, 1:], (none, none, none, none, (0, 1), none))
    view = jnp.concatenate([left, view, right], axis=2)
    view = jnp.pad(view, ((1, 1), none, none, none, none, none))
    return view.reshape(CUBE + 2, CUBE + 2, CUBE + 2, rows, channels)


def rows_here(weights):
    count = weights.shape[-2]
    start = count * lax.axis_index("space")
    return start // LANES, start % LANES


def block_count(count):
    worst = max(count * s % LANES for s in range(lax.axis_size("space")))
    return -(-(worst + count) // LANES)


def aligned(weights):
    _, offset = rows_here(weights)
    total = block_count(weights.shape[-2]) * LANES
    wide = jnp.zeros(weights.shape[:-2] + (total, weights.shape[-1]), weights.dtype)
    return lax.dynamic_update_slice_in_dim(wide, weights, offset, wide.ndim - 2)


def patches(field, first, count, across):
    cubes, rows, channels = field.shape
    wide = rimmed(field, across)
    per_tap = channels // LANES
    pieces = []
    for j in range(count):
        block = first + j
        tap, lane = jnp.minimum(block // per_tap, 26), block % per_tap
        piece = lax.dynamic_slice(
            wide,
            (tap // 9, tap // 3 % 3, tap % 3, 0, lane * LANES),
            (CUBE, CUBE, CUBE, rows, LANES),
        )
        pieces.append(piece.reshape(cubes * rows, LANES))
    return jnp.concatenate(pieces, axis=1)


def conv_part(field, weights, first, across):
    patch = patches(field, first, weights.shape[0] // LANES, across)
    out = jnp.dot(patch, weights, preferred_element_type=F32)
    return out.reshape(field.shape[:2] + (-1,)), patch


def convt_part(field, weights, first, across):
    cubes, rows, channels = field.shape
    spread = lax.dot_general(
        field.reshape(-1, channels),
        weights,
        (((1,), (1,)), ((), ())),
        preferred_element_type=F32,
    )
    count = weights.shape[0] // LANES
    fold = jax.linear_transpose(
        lambda v: patches(v, first, count, across),
        jax.ShapeDtypeStruct((cubes, rows, channels), F32),
    )
    return fold(spread)[0]


def kernel_grad(patch, field):
    return lax.dot_general(
        patch,
        field.reshape(-1, field.shape[-1]),
        (((0,), (0,)), ((), ())),
        preferred_element_type=F32,
    )


VMEM_BYTES = 56 * 1024 * 1024


def kernels_fit(channels):
    return chips_of() * LANES == channels


def shifted(slabs, rows, valid):
    wide = pltpu.roll(slabs.astype(F32), rows % slabs.shape[1], 1)
    return jnp.where(valid, wide, 0.0)


def row_marks(shape, across):
    row = lax.broadcasted_iota(jnp.int32, shape, len(shape) - 2)
    return row, row % across


def fill_rim(field, rim, across):
    rows, channels = field.shape[1:]
    tiles = channels // LANES
    blank = jnp.zeros((CUBE + 2, CUBE + 2, rows, LANES), rim.dtype)
    for q in range(tiles):
        rim[q, 0] = blank
        rim[q, CUBE + 1] = blank

    def frame(f, carry):
        base = f * CUBE * CUBE
        row, column = row_marks((CUBE, rows, LANES), across)
        row6, column6 = row_marks((CUBE + 2, rows, LANES), across)
        for q in range(tiles):
            lanes = slice(q * LANES, (q + 1) * LANES)
            for h in range(CUBE):
                rim[q, f + 1, h + 1, 1 : CUBE + 1] = field[pl.ds(base + CUBE * h, CUBE), :, lanes]
            above = field[pl.ds(base + CUBE * (CUBE - 1), CUBE), :, lanes]
            rim[q, f + 1, 0, 1 : CUBE + 1] = shifted(above, across, row >= across).astype(rim.dtype)
            below = field[pl.ds(base, CUBE), :, lanes]
            rim[q, f + 1, CUBE + 1, 1 : CUBE + 1] = shifted(
                below, -across, row < rows - across
            ).astype(rim.dtype)
            left = rim[q, f + 1, :, CUBE]
            rim[q, f + 1, :, 0] = shifted(left, 1, column6 >= 1).astype(rim.dtype)
            right = rim[q, f + 1, :, 1]
            rim[q, f + 1, :, CUBE + 1] = shifted(right, -1, column6 < across - 1).astype(rim.dtype)
        return carry

    lax.fori_loop(0, CUBE, frame, 0)


def fold_rim(rim, across):
    tiles, rows = rim.shape[0], rim.shape[4]

    def frame(f, carry):
        row, _ = row_marks((CUBE, rows, LANES), across)
        _, column6 = row_marks((CUBE + 2, rows, LANES), across)
        for q in range(tiles):
            left = shifted(rim[q, f + 1, :, 0], -1, column6 < across - 1)
            rim[q, f + 1, :, CUBE] += left
            right = shifted(rim[q, f + 1, :, CUBE + 1], 1, column6 >= 1)
            rim[q, f + 1, :, 1] += right
            above = shifted(rim[q, f + 1, 0, 1 : CUBE + 1], -across, row < rows - across)
            rim[q, f + 1, CUBE, 1 : CUBE + 1] += above
            below = shifted(rim[q, f + 1, CUBE + 1, 1 : CUBE + 1], across, row >= across)
            rim[q, f + 1, 1, 1 : CUBE + 1] += below
        return carry

    lax.fori_loop(0, CUBE, frame, 0)


def tap_of(block, per_tap):
    tap = jnp.minimum(block // per_tap, 26)
    return block % per_tap, tap // 9, tap // 3 % 3, tap % 3


def fill_patch(rim, patch, first, count, start, size):
    rows = rim.shape[4]
    for j in range(count):
        q, f, h, w = tap_of(first + j, rim.shape[0])
        window = rim[
            q,
            pl.ds(f + start[0], size[0]),
            pl.ds(h + start[1], size[1]),
            pl.ds(w, CUBE),
        ]
        patch[:, j * LANES : (j + 1) * LANES] = window.reshape(
            size[0] * size[1] * CUBE * rows, LANES
        )


def conv_kernel(by_cube, across, where, field, weights, keep, send, rim, patch):
    first, core = where[0], where[1]
    rows, channels = field.shape[1:]
    tiles = channels // LANES
    count = weights.shape[0] // LANES
    half = CUBE // 2
    fill_rim(field, rim, across)

    def part(which):
        start, size = ((0, half * which), (CUBE, half)) if by_cube else ((half * which, 0), (half, CUBE))
        fill_patch(rim, patch, first, count, start, size)
        return jnp.dot(patch[...], weights[...], preferred_element_type=F32)

    for target, which in ((send, 1 - core), (keep, core)):
        total = part(which).astype(target.dtype)
        if by_cube:
            target[...] = total.reshape(target.shape)
        else:
            for q in range(tiles):
                target[q] = total[:, q * LANES : (q + 1) * LANES].reshape(target.shape[1:])


def whole_spec():
    return pl.BlockSpec(memory_space=pltpu.VMEM)


def kernel_params():
    return pltpu.CompilerParams(vmem_limit_bytes=VMEM_BYTES)


def here_scalars(first):
    return jnp.stack([first, lax.axis_index("space") % 2]).astype(jnp.int32)


def conv_shares(field, weights, first, across, by_cube):
    cubes, rows, channels = field.shape
    count = weights.shape[0] // LANES
    tiles = channels // LANES
    if by_cube:
        shape = (CUBE, cubes // (2 * CUBE), rows, channels)
    else:
        shape = (tiles, cubes // 2, rows, LANES)
    work = cubes * rows * channels * weights.shape[0]
    return pl.pallas_call(
        partial(conv_kernel, by_cube, across),
        out_shape=(jax.ShapeDtypeStruct(shape, F32), jax.ShapeDtypeStruct(shape, BF16)),
        in_specs=[pl.BlockSpec(memory_space=pltpu.SMEM), whole_spec(), whole_spec()],
        out_specs=(whole_spec(), whole_spec()),
        scratch_shapes=[
            pltpu.VMEM((tiles, CUBE + 2, CUBE + 2, CUBE + 2, rows, LANES), BF16),
            pltpu.VMEM((cubes // 2 * rows, count * LANES), BF16),
        ],
        compiler_params=kernel_params(),
        cost_estimate=pl.CostEstimate(flops=2 * work, bytes_accessed=8 << 20, transcendentals=0),
        name="conv_part",
    )(here_scalars(first), field, weights)


def add_taps(field, weights, rim, first):
    rows, channels = field.shape[1:]
    tiles = channels // LANES
    count = weights.shape[0] // LANES
    blank = jnp.zeros((CUBE + 2, CUBE + 2, rows, LANES), F32)

    def clear(f, carry):
        for q in range(tiles):
            rim[q, f] = blank
        return carry

    lax.fori_loop(0, CUBE + 2, clear, 0)
    spread_rows = CUBE * CUBE * rows

    def frame(f, carry):
        source = field[pl.ds(f * CUBE * CUBE, CUBE * CUBE)].reshape(spread_rows, channels)
        for j in range(0, count, 2):
            wide = min(2, count - j)
            spread = lax.dot_general(
                source,
                weights[j * LANES : (j + wide) * LANES, :],
                (((1,), (1,)), ((), ())),
                preferred_element_type=F32,
            )
            for i in range(wide):
                q, tf, th, tw = tap_of(first + j + i, tiles)
                rim[q, f + tf, pl.ds(th, CUBE), pl.ds(tw, CUBE)] += spread[
                    :, i * LANES : (i + 1) * LANES
                ].reshape(CUBE, CUBE, rows, LANES)
        return carry

    lax.fori_loop(0, CUBE, frame, 0)


def convt_kernel(across, where, field, weights, keep, send, rim):
    first, core = where[0], where[1]
    add_taps(field, weights, rim, first)
    fold_rim(rim, across)
    half = CUBE // 2
    for q in range(rim.shape[0]):
        for target, which in ((send, 1 - core), (keep, core)):
            for f in range(half):
                target[q, pl.ds(f * CUBE * CUBE, CUBE * CUBE)] = (
                    rim[q, half * which + 1 + f, 1 : CUBE + 1, 1 : CUBE + 1]
                    .reshape((CUBE * CUBE,) + target.shape[2:])
                    .astype(target.dtype)
                )


def convt_whole_kernel(across, where, field, weights, out, rim):
    add_taps(field, weights, rim, where[0])
    fold_rim(rim, across)
    for q in range(rim.shape[0]):
        for f in range(CUBE):
            out[pl.ds(f * CUBE * CUBE, CUBE * CUBE), :, q * LANES : (q + 1) * LANES] = rim[
                q, 1 + f, 1 : CUBE + 1, 1 : CUBE + 1
            ].reshape((CUBE * CUBE,) + out.shape[1:2] + (LANES,))


def convt_shares(field, weights, first, across, whole):
    cubes, rows, channels = field.shape
    tiles = channels // LANES
    shape = (tiles, cubes // 2, rows, LANES)
    if whole:
        out_shape = (jax.ShapeDtypeStruct(field.shape, F32),)
    else:
        out_shape = (jax.ShapeDtypeStruct(shape, F32), jax.ShapeDtypeStruct(shape, BF16))
    work = cubes * rows * channels * weights.shape[0]
    return pl.pallas_call(
        partial(convt_whole_kernel if whole else convt_kernel, across),
        out_shape=out_shape,
        in_specs=[pl.BlockSpec(memory_space=pltpu.SMEM), whole_spec(), whole_spec()],
        out_specs=tuple(whole_spec() for _ in out_shape),
        scratch_shapes=[pltpu.VMEM((tiles, CUBE + 2, CUBE + 2, CUBE + 2, rows, LANES), F32)],
        compiler_params=kernel_params(),
        cost_estimate=pl.CostEstimate(flops=2 * work, bytes_accessed=8 << 20, transcendentals=0),
        name="conv_back_part",
    )(here_scalars(first), field, weights)


def grad_kernel(across, where, field, cotangent, out, rim, patch, wide):
    rows, channels = field.shape[1:]
    count = patch.shape[1] // LANES
    fill_rim(field, rim, across)
    fill_patch(rim, patch, where[0], count, (0, 0), (CUBE, CUBE))
    source = cotangent[...].reshape(-1, channels)
    for j in range(0, count, 2):
        lanes = slice(j * LANES, min(j + 2, count) * LANES)
        wide[lanes, :] = lax.dot_general(
            patch[:, lanes], source, (((0,), (0,)), ((), ())), preferred_element_type=F32
        )
    start = pl.multiple_of(where[1], 8)
    out[...] = wide[pl.ds(start, out.shape[0]), :].astype(out.dtype)


def kernel_grad_here(field, cotangent, first, offset, row_count, across):
    cubes, rows, channels = field.shape
    tiles = channels // LANES
    count = block_count(row_count)
    work = cubes * rows * channels * count * LANES
    return pl.pallas_call(
        partial(grad_kernel, across),
        out_shape=jax.ShapeDtypeStruct((row_count, channels), BF16),
        in_specs=[pl.BlockSpec(memory_space=pltpu.SMEM), whole_spec(), whole_spec()],
        out_specs=whole_spec(),
        scratch_shapes=[
            pltpu.VMEM((tiles, CUBE + 2, CUBE + 2, CUBE + 2, rows, LANES), BF16),
            pltpu.VMEM((cubes * rows, count * LANES), BF16),
            pltpu.VMEM((count * LANES, channels), F32),
        ],
        compiler_params=kernel_params(),
        cost_estimate=pl.CostEstimate(flops=2 * work, bytes_accessed=8 << 20, transcendentals=0),
        name="kernel_grad",
    )(jnp.stack([first, offset]).astype(jnp.int32), field, cotangent)


def chips_summed(mine):
    chips = chips_of()
    z, _ = here()
    total = picked(mine, z)
    for step in range(1, chips):
        sent = picked(mine, (z + step) % chips).astype(BF16)
        total = total + along_chips(sent, step).astype(F32)
    return total


def conv_scattered(field, weights, first, across, by_cube=False):
    if kernels_fit(field.shape[-1]):
        keep, send = conv_shares(field, weights, first, across, by_cube)
        return chips_summed(keep + to_twin(send).astype(F32))
    part, _ = conv_part(field, weights, first, across)
    if by_cube:
        cubes, rows, channels = part.shape
        return scattered(part.reshape(chips_of(), 2, -1, rows, channels))
    return scattered(to_blocks(part))


def convt_scattered(field, weights, first, across):
    if kernels_fit(field.shape[-1]):
        keep, send = convt_shares(field, weights, first, across, False)
        return chips_summed(keep + to_twin(send).astype(F32))
    return scattered(to_blocks(convt_part(field, weights, first, across)))


def convt_whole(field, weights, first, across):
    if kernels_fit(field.shape[-1]):
        return convt_shares(field, weights, first, across, True)[0]
    return convt_part(field, weights, first, across)


def kernel_grads(field, cotangent, first, offset, row_count, across):
    if kernels_fit(field.shape[-1]):
        return kernel_grad_here(field, cotangent, first, offset, row_count, across)
    patch = patches(field, first, block_count(row_count), across)
    grad = kernel_grad(patch, cotangent)
    return lax.dynamic_slice_in_dim(grad, offset, row_count, 0).astype(BF16)


def normed(values, sums, squares, width, members):
    average = group_means(sums, width, members)
    square = group_means(squares, width, members)
    spread = lax.rsqrt(square - average * average + 1e-06)
    return (values - average) * spread, spread


def channel_sums(values):
    return jnp.sum(values, axis=tuple(range(values.ndim - 1)))


def body(
    video_clips,
    code_bits,
    recon_grad,
    enc_convs,
    enc_gains,
    enc_shifts,
    down_weight,
    down_bias,
    down_proj,
    up_proj,
    up_bias,
    up_weight,
    upsample_bias,
    dec_convs,
    dec_gains,
    dec_shifts,
):
    section = lax.axis_index("section")
    space = lax.axis_index("space")
    sections = lax.axis_size("section")
    spaces = lax.axis_size("space")
    chips = chips_of()
    clips, frames, height, width, channels = video_clips.shape
    extent = (frames, height, width, channels)
    across = width // CUBE
    bits = code_bits.shape[-1]
    rows = spaces * across
    cubes = CUBE**3
    own_cubes = cubes // spaces
    members = float(cubes * rows * (channels // GROUPS))
    group = channels // GROUPS
    first_space = (space == 0).astype(F32)

    lanes = down_bias.shape[0]
    code = code_bits.reshape(-1).astype(BF16)
    code = jnp.pad(code, (0, -code.shape[0] % lanes)).reshape(-1, lanes)
    small = jnp.concatenate(
        [
            enc_gains,
            dec_gains,
            enc_shifts,
            dec_shifts,
            up_bias[None],
            down_bias[None],
            up_proj.T,
            down_proj.T,
            code,
        ],
        axis=0,
    )
    small = gathered(small).reshape(spaces, small.shape[0], lanes)
    heads = 14 + 2 * bits
    table = small[:, :heads].transpose(1, 0, 2).reshape(heads, channels)
    wide_table = table.astype(F32)
    e_gains, d_gains = wide_table[0:2], wide_table[2:4]
    e_shifts, d_shifts = wide_table[4:8], wide_table[8:12]
    up_row, down_row = wide_table[12], wide_table[13]
    up_cols, down_cols = table[14 : 14 + bits], table[14 + bits :]
    count = clips * across * bits
    code_all = small[:, heads:].reshape(spaces, -1)[:, :count].reshape(spaces, clips, across, bits)
    signs = (2 * code_all - 1).transpose(1, 0, 2, 3).reshape(clips * rows, bits)

    slabs = jnp.stack(
        [cubes_of(picked(video_clips, section)), cubes_of(picked(recon_grad, section))]
    )
    hidden = (jnp.dot(signs, up_cols, preferred_element_type=F32) + up_row).astype(BF16)
    hidden_own = lax.dynamic_slice_in_dim(hidden, section * rows, rows, 0)
    grown = lax.dot_general(
        hidden_own, up_weight, (((1,), (1,)), ((), ())), preferred_element_type=F32
    )
    grown = (grown + upsample_bias.astype(F32)).astype(BF16)
    grown = grown.reshape(rows, own_cubes, channels).transpose(1, 0, 2)
    decoded_in = gathered(grown).reshape(cubes, rows, channels)
    both = gathered(slabs)
    video = field_of(both[:, :, 0])
    recon_cot = field_of(both[:, :, 1])

    maps = jnp.stack(
        [
            lax.dot_general(
                up_cols, up_weight, (((1,), (1,)), ((), ())), preferred_element_type=F32
            ),
            lax.dot_general(
                down_cols, down_weight, (((1,), (1,)), ((), ())), preferred_element_type=F32
            ),
        ]
    ).astype(BF16)
    maps = gathered(maps).reshape(spaces, 2, bits, own_cubes, channels)
    up_map, down_map = maps[:, 0], maps[:, 1]

    first, offset = rows_here(enc_convs)
    enc_w, dec_w = aligned(enc_convs), aligned(dec_convs)
    half_members = members

    def ahead(inputs, weights, gains, shifts, by_cube):
        wide = inputs.astype(F32)
        flat_one, spread_one = normed(
            wide, channel_sums(wide), channel_sums(wide * wide), group, members
        )
        norm_one = flat_one * gains[0] + shifts[0]
        logistic = jax.nn.sigmoid(norm_one)
        act_one = (norm_one * logistic).astype(BF16)
        middle = conv_scattered(act_one, weights[0], first, across) + own_lanes(shifts[2])
        sums = pair_summed(jnp.stack([channel_sums(middle), channel_sums(middle * middle)]))
        flat_two, spread_two = normed(middle, sums[0], sums[1], group, half_members)
        norm_two = flat_two * own_lanes(gains[1]) + own_lanes(shifts[1])
        act_two = (norm_two * jax.nn.sigmoid(norm_two)).astype(BF16)
        act_two = from_blocks(gathered(act_two))
        branch = conv_scattered(act_two, weights[1], first, across, by_cube)
        return (
            branch,
            (flat_one, spread_one, norm_one, act_one),
            (flat_two, spread_two, norm_two, act_two),
        )

    def grads_two(raw, state, gains):
        flat, spread, norm, _ = state
        pre = raw * swish_slope(norm, jax.nn.sigmoid(norm))
        sums = pair_summed(jnp.stack([channel_sums(pre), channel_sums(pre * flat)]))
        gain = own_lanes(gains[1])
        total = group_means(sums[0] * gain, group, members)
        lined = group_means(sums[1] * gain, group, members)
        inner = (spread * (pre * gain - total - flat * lined)).astype(BF16)
        return inner, sums

    z, core = here()

    def spread_lanes(block_row):
        full = jnp.zeros(block_row.shape[:-1] + (channels,), F32)
        placed = lax.dynamic_update_slice_in_dim(
            full, block_row, z * block_row.shape[-1], full.ndim - 1
        )
        return jnp.where(core == 0, placed, 0.0)

    dec_branch, dec_one, dec_two = ahead(decoded_in, dec_w, d_gains, d_shifts, False)
    dec_inner, dec_sums_two = grads_two(
        convt_scattered(recon_cot, dec_w[1], first, across), dec_two, d_gains
    )
    dec_inner = from_blocks(gathered(dec_inner))
    back = convt_whole(dec_inner, dec_w[0], first, across)
    flat_one, spread_one, norm_one, _ = dec_one
    pre = back * swish_slope(norm_one, jax.nn.sigmoid(norm_one))
    dec_sums_one = jnp.stack([channel_sums(pre), channel_sums(pre * flat_one)])
    total = group_means(dec_sums_one[0] * d_gains[0], group, members)
    lined = group_means(dec_sums_one[1] * d_gains[0], group, members)
    grad_part = spread_one * (pre * d_gains[0] - total - flat_one * lined)
    grad_part = grad_part + recon_cot.astype(F32) * first_space
    sign_part = jnp.einsum(
        "sorc,skoc->rk",
        grad_part.reshape(spaces, own_cubes, rows, channels).astype(BF16),
        up_map,
        preferred_element_type=F32,
    )
    sign_grad = summed(sign_part).astype(BF16)
    enc_cot = jnp.einsum("rk,skoc->sorc", sign_grad, down_map, preferred_element_type=F32)
    enc_cot = enc_cot.astype(BF16).reshape(cubes, rows, channels)

    enc_branch, enc_one, enc_two = ahead(video, enc_w, e_gains, e_shifts, True)
    enc_inner, enc_sums_two = grads_two(
        convt_scattered(enc_cot, enc_w[1], first, across), enc_two, e_gains
    )
    enc_inner = from_blocks(gathered(enc_inner))
    back = convt_scattered(enc_inner, enc_w[0], first, across)
    flat, norm = own_block(enc_one[0]), own_block(enc_one[2])
    pre = back * swish_slope(norm, jax.nn.sigmoid(norm))
    enc_sums_one = pair_summed(jnp.stack([channel_sums(pre), channel_sums(pre * flat)]))
    gain = own_lanes(e_gains[0])
    total = group_means(enc_sums_one[0] * gain, group, members)
    lined = group_means(enc_sums_one[1] * gain, group, members)
    video_back = own_lanes(enc_one[1]) * (pre * gain - total - flat * lined)
    video_back = (own_block(enc_cot).astype(F32) + video_back).astype(BF16)
    recon = dec_branch + own_lanes(d_shifts[3])
    recon = (recon + own_block(decoded_in).astype(F32)).astype(BF16)

    def to_output(block):
        half, _, lane_count = block.shape
        pieces = block.reshape(half, spaces, across, lane_count).transpose(1, 0, 2, 3)
        swapped = lax.all_to_all(pieces, "space", 0, 0, tiled=True)
        slab = swapped.reshape(chips, 2, half, across, lane_count).transpose(1, 2, 3, 0, 4)
        slab = slab_of(slab.reshape(cubes, across, channels), extent)
        parted = slab.reshape(frames, height, width, sections, channels // sections)
        return lax.all_to_all(parted.transpose(3, 0, 1, 2, 4), "section", 0, 0, tiled=True)

    row_count = enc_convs.shape[1]
    grads = [
        lax.psum(kernel_grads(act, cot, first, offset, row_count, across), "section").astype(F32)
        for act, cot in (
            (enc_one[3], enc_inner),
            (enc_two[3], enc_cot),
            (dec_one[3], dec_inner),
            (dec_two[3], recon_cot),
        )
    ]

    encoded = enc_branch
    own = lambda v: lax.dynamic_slice_in_dim(v, space * own_cubes, own_cubes, 0).astype(F32)
    encoded = (encoded + e_shifts[3] + own(video)).astype(BF16)
    decoded_grad = scattered(grad_part.reshape(chips, 2, own_cubes, rows, channels)).astype(BF16)
    both = lax.all_gather(jnp.stack([encoded, decoded_grad]), "section", axis=0)
    both = both.transpose(1, 0, 3, 2, 4).reshape(2, clips * rows, own_cubes * channels)
    enc_rows, dec_rows = both[0], both[1]
    sign_all = lax.all_gather(sign_grad, "section", axis=0, tiled=True)
    inner_grad = jnp.dot(sign_all, down_cols, preferred_element_type=F32).astype(BF16)

    def outer(left, right):
        return lax.dot_general(left, right, (((0,), (0,)), ((), ())), preferred_element_type=F32)

    down_weight_grad = outer(enc_rows, inner_grad)
    up_weight_grad = outer(dec_rows, hidden)
    upsample_grad = jnp.sum(dec_rows.astype(F32), axis=0)
    parts = jnp.stack(
        [
            jnp.dot(enc_rows, down_weight, preferred_element_type=F32),
            jnp.dot(dec_rows, up_weight, preferred_element_type=F32),
        ]
    )
    shares = lax.psum_scatter(parts, "space", scatter_dimension=2, tiled=True)
    inner_low = (shares[0] + down_bias.astype(F32)).astype(BF16)
    hidden_grad = shares[1].astype(BF16)
    down_proj_grad = outer(inner_low, sign_all)
    up_proj_grad = outer(hidden_grad, signs)
    up_bias_grad = jnp.sum(hidden_grad.astype(F32), axis=0)
    inner_share = lax.dynamic_slice_in_dim(inner_grad, space * lanes, lanes, 1)
    down_bias_grad = jnp.sum(inner_share.astype(F32), axis=0)

    one = lambda v: channel_sums(v.astype(F32))[None] * first_space
    small_grads = jnp.concatenate(
        [
            spread_lanes(enc_sums_one[1:]),
            spread_lanes(enc_sums_two[1:]),
            spread_lanes(enc_sums_one[:1]),
            spread_lanes(enc_sums_two[:1]),
            one(enc_inner),
            one(enc_cot),
            dec_sums_one[1:],
            spread_lanes(dec_sums_two[1:]),
            dec_sums_one[:1],
            spread_lanes(dec_sums_two[:1]),
            one(dec_inner),
            one(recon_cot),
        ],
        axis=0,
    )
    small_grads = lax.psum(small_grads, ("section", "space"))
    small_grads = lax.dynamic_slice_in_dim(small_grads, space * lanes, lanes, 1)

    return (
        to_output(recon),
        to_output(video_back),
        jnp.stack(grads[:2]),
        small_grads[0:2],
        small_grads[2:6],
        down_weight_grad,
        down_bias_grad,
        down_proj_grad,
        up_proj_grad,
        up_bias_grad,
        up_weight_grad,
        upsample_grad,
        jnp.stack(grads[2:]),
        small_grads[6:8],
        small_grads[8:12],
    )


def solution(mesh):
    lead, second, third = P("space"), P(None, "space"), P(None, None, "space")
    field = P(None, None, "space", None, "section")
    return jax.shard_map(
        body,
        mesh=mesh,
        in_specs=(
            third,
            third,
            third,
            second,
            second,
            second,
            lead,
            lead,
            lead,
            lead,
            lead,
            lead,
            lead,
            second,
            second,
            second,
        ),
        out_specs=(
            field,
            field,
            second,
            second,
            second,
            lead,
            lead,
            lead,
            lead,
            lead,
            lead,
            lead,
            second,
            second,
            second,
        ),
        check_vma=False,
    )
```

time: 3940 us -> 586 us (0.15)
  waiting for transfers between devices: 1060 us -> 146 us
  blocking collectives: 779 us -> 48.8 us
  other arithmetic: 671 us -> 68 us
  local copies, waits for them, and re-layouts: 605 us -> 95.4 us
  matrix products: 366 us -> 23.7 us
  starting transfers between devices: 380 us -> 105 us
  Pallas kernels: 0 us -> 74.8 us
  loops' own time: 44.6 us -> 0 us
    psum x33 -> x1, blocking collectives: 587 us -> 40.5 us  [body(): small_grads = lax.psum(small_grads, ('section', 'space'))]
    reduce_scatter x1 -> x0, waiting for transfers between devices: 482 us -> none  [body(): lax.psum_scatter(block_acc[0], 'space', scatter_dimension=1, tiled=True)]
    scatter-add x16 -> x0, other arithmetic: 466 us -> none  [advance(): block_acc[0].at[0].add(one_share).at[1].add(two_share)]
    dot_general x88 -> x13, matrix products: 366 us -> 23.7 us  [the longest x4 11.3 us: outer(): lax.dot_general(left, right, (((0,), (0,)), ((), ())), preferred_element_...]
    psum x1, waiting for transfers between devices: 288 us -> 36.5 us  [body(): lax.psum(kernel_grads(act, cot, first, offset, row_count, across), 'secti...]
    ppermute x88 -> x73, starting transfers between devices: 320 us -> 89.5 us  [the longest x51 85.2 us: along_chips(): return lax.ppermute(value, 'space', route)]
    slice x32 -> x22, local copies, waits for them, and re-layouts: 176 us -> 4.65 us  [the longest x1 1.75 us: body(): up_map, down_map = (maps[:, 0], maps[:, 1])]
    all_gather x1, waiting for transfers between devices: 167 us -> 8.65 us  [body(): both = lax.all_gather(jnp.stack([encoded, decoded_grad]), 'section', axis=0)]
  transfers between devices with their start and end apart: 112 -> 80, of which waited for: 16 -> 26; matrix products, arithmetic and copies ran while one was open for 38% -> 29% of each run, Pallas kernels for 0% -> 13%
where the time goes in v1:
time: 586 us; the launch traced here: 577 us
  waiting for transfers between devices  146 us (25%)
  starting transfers between devices  105 us (18%)
  local copies, waits for them, and re-layouts  95.4 us (16%)
  Pallas kernels  74.8 us (13%)
  other arithmetic  68 us (12%)
  blocking collectives  48.8 us (8%)
  matrix products  23.7 us (4%)
  between operations  15.9 us (3%)
    ppermute x51, waiting for transfers between devices, along_chips(): return lax.ppermute(value, 'space', route)  93.3 us
    ppermute x51, starting transfers between devices, along_chips(): return lax.ppermute(value, 'space', route)  85.2 us
    psum x1, blocking collectives, body(): small_grads = lax.psum(small_grads, ('section', 'space'))  40.5 us
    psum x1, waiting for transfers between devices, body(): lax.psum(kernel_grads(act, cot, first, offset, row_count, across), 'secti...  36.5 us
    pallas_call x4, Pallas kernels, convt_shares(): pl.pallas_call(partial(convt_whole_kernel if whole else convt_kernel, acr...  28.2 us
    pallas_call x4, Pallas kernels, conv_shares(): pl.pallas_call(partial(conv_kernel, by_cube, across), out_shape=(jax.Shap...  23.4 us
    pallas_call x4, Pallas kernels, kernel_grad_here(): pl.pallas_call(partial(grad_kernel, across), out_shape=jax.ShapeDtypeStru...  23.1 us
    dynamic_update_slice x28, local copies, waits for them, and re-layouts, gathered(): stack = lax.dynamic_update_index_in_dim(stack, piece, (z - step) % chips, 0)  17 us
  transfers between devices with their start and end apart: 80, of which 26 were waited for; matrix products, arithmetic and copies ran while one was open for 29% of the time, Pallas kernels for 13%

profile of v1, /device:TPU:0, one launch (start us, length us, event | category | flops | bytes accessed | tf_op | source)
XLA Modules:
  0.0 577.4 jit_solution(12155658675717879274)
XLA Ops:
  73.6 17.5 %collective-permute-done.21 = bf16[2,18,4096]{2,1,0:T(8,128)(2,1)S(1)} collective-permute-done((bf16[2,18,4096]{2,1,0:T(8,128)(2,1)}, bf16[2,18,4096]{2,1,0:T(8,128)(2,1)S(1)}, u32[]{:S(2)}, u32[]{:S(2)}) %collective-permute-start.21) | collective-permute-done | bytes 294944 | tf_op jit(solution)/shard_map/ppermute | solution.py:28
  91.4 8.3 %collective-permute-done.22 = bf16[2,18,4096]{2,1,0:T(8,128)(2,1)S(1)} collective-permute-done((bf16[2,18,4096]{2,1,0:T(8,128)(2,1)}, bf16[2,18,4096]{2,1,0:T(8,128)(2,1)S(1)}, u32[]{:S(2)}, u32[]{:S(2)}) %collective-permute-start.22) | collective-permute-done | bytes 294944 | tf_op jit(solution)/shard_map/ppermute | solution.py:28
  103.1 5.8 %conv_part.4 = (f32[4,32,16,128]{3,2,1,0:T(8,128)}, bf16[4,32,16,128]{3,2,1,0:T(8,128)(2,1)}) custom-call(s32[2]{0:T(128)} %get-tuple-element.216.where, bf16[64,16,512]{2,1,0:T(8,128)(2,1)} %multiply_convert_fusion.1.field, bf16[1792,512]{1,0:T(8,128)(2,1)} %get-tuple-element.139.weights), custom_call_target="tpu_custom_call" | custom-call | flops 1879048192 | bytes 8388608 | tf_op jit(solution)/shard_map/conv_part/pallas_call | solution.py:351
  138.8 6.9 %conv_back_part.4 = (f32[4,32,16,128]{3,2,1,0:T(8,128)}, bf16[4,32,16,128]{3,2,1,0:T(8,128)(2,1)}) custom-call(s32[2]{0:T(128)} %get-tuple-element.216.where, bf16[64,16,512]{2,1,0:T(8,128)(2,1)} %reshape.505.field.cotangent, bf16[1792,512]{1,0:T(8,128)(2,1)} %get-tuple-element.138.weights), custom_call_target="tpu_custom_call" | custom-call | flops 1879048192 | bytes 8388608 | tf_op jit(solution)/shard_map/conv_back_part/pallas_call | solution.py:434
  155.1 5.8 %conv_part.6 = (f32[4,32,16,128]{3,2,1,0:T(8,128)}, bf16[4,32,16,128]{3,2,1,0:T(8,128)(2,1)}) custom-call(s32[2]{0:T(128)} %get-tuple-element.216.where, bf16[64,16,512]{2,1,0:T(8,128)(2,1)} %get-tuple-element.148.field, bf16[1792,512]{1,0:T(8,128)(2,1)} %get-tuple-element.137.weights), custom_call_target="tpu_custom_call" | custom-call | flops 1879048192 | bytes 8388608 | tf_op jit(solution)/shard_map/conv_part/pallas_call | solution.py:351
  204.0 6.4 %collective-permute-done.31 = bf16[32,16,128]{2,1,0:T(8,128)(2,1)S(1)} collective-permute-done((bf16[32,16,128]{2,1,0:T(8,128)(2,1)S(1)}, bf16[32,16,128]{2,1,0:T(8,128)(2,1)S(1)}, u32[]{:S(2)}, u32[]{:S(2)}) %collective-permute-start.31) | collective-permute-done | bytes 131104 | tf_op jit(solution)/shard_map/ppermute | solution.py:28
  210.7 7.8 %collective-permute-done.44 = bf16[32,16,128]{2,1,0:T(8,128)(2,1)S(1)} collective-permute-done((bf16[32,16,128]{2,1,0:T(8,128)(2,1)S(1)}, bf16[32,16,128]{2,1,0:T(8,128)(2,1)S(1)}, u32[]{:S(2)}, u32[]{:S(2)}) %collective-permute-start.44) | collective-permute-done | bytes 131104 | tf_op jit(solution)/shard_map/ppermute | solution.py:28
  232.7 5.8 %kernel_grad.7 = bf16[1728,512]{1,0:T(8,128)(2,1)} custom-call(s32[2]{0:T(128)} %get-tuple-element.217.where, bf16[64,16,512]{2,1,0:T(8,128)(2,1)} %reshape.499.field, bf16[64,16,512]{2,1,0:T(8,128)(2,1)} %reshape.505.field.cotangent), custom_call_target="tpu_custom_call" | custom-call | flops 1879048192 | bytes 8388608 | tf_op jit(solution)/shard_map/kernel_grad/pallas_call | solution.py:466
  253.3 7.2 %conv_back_part.5 = f32[64,16,512]{2,1,0:T(8,128)} custom-call(s32[2]{0:T(128)} %get-tuple-element.216.where, bf16[64,16,512]{2,1,0:T(8,128)(2,1)} %reshape.506.field.cotangent, bf16[1792,512]{1,0:T(8,128)(2,1)} %get-tuple-element.139.weights), custom_call_target="tpu_custom_call" | custom-call | flops 1879048192 | bytes 8388608 | tf_op jit(solution)/shard_map/conv_back_part/pallas_call | solution.py:434
  270.4 5.8 %kernel_grad.6 = bf16[1728,512]{1,0:T(8,128)(2,1)} custom-call(s32[2]{0:T(128)} %get-tuple-element.217.where, bf16[64,16,512]{2,1,0:T(8,128)(2,1)} %multiply_convert_fusion.1.field, bf16[64,16,512]{2,1,0:T(8,128)(2,1)} %reshape.506.field.cotangent), custom_call_target="tpu_custom_call" | custom-call | flops 1879048192 | bytes 8388608 | tf_op jit(solution)/shard_map/kernel_grad/pallas_call | solution.py:466
  280.7 5.9 %conv_part.7 = (f32[4,8,16,512]{3,2,1,0:T(8,128)}, bf16[4,8,16,512]{3,2,1,0:T(8,128)(2,1)}) custom-call(s32[2]{0:T(128)} %get-tuple-element.216.where, bf16[64,16,512]{2,1,0:T(8,128)(2,1)} %reshape.514.field, bf16[1792,512]{1,0:T(8,128)(2,1)} %get-tuple-element.136.weights), custom_call_target="tpu_custom_call" | custom-call | flops 1879048192 | bytes 8388608 | tf_op jit(solution)/shard_map/conv_part/pallas_call | solution.py:351
  288.3 7.1 %conv_back_part.6 = (f32[4,32,16,128]{3,2,1,0:T(8,128)}, bf16[4,32,16,128]{3,2,1,0:T(8,128)(2,1)}) custom-call(s32[2]{0:T(128)} %get-tuple-element.216.where, bf16[64,16,512]{2,1,0:T(8,128)(2,1)} %bitcast.470, bf16[1792,512]{1,0:T(8,128)(2,1)} %get-tuple-element.136.weights), custom_call_target="tpu_custom_call" | custom-call | flops 1879048192 | bytes 8388608 | tf_op jit(solution)/shard_map/conv_back_part/pallas_call | solution.py:434
  311.1 8.1 %collective-permute-start.71 = (bf16[8,16,512]{2,1,0:T(8,128)(2,1)S(1)}, bf16[8,16,512]{2,1,0:T(8,128)(2,1)S(1)}, u32[]{:S(2)}, u32[]{:S(2)}) collective-permute-start(bf16[8,16,512]{2,1,0:T(8,128)(2,1)S(1)} %get-tuple-element.158), channel_id=1, source_target_pairs={{0,4},{1,5},{2,6},{3,7},{4,0},{5,1},{6,2},{7,3},{8,12},{9,13},{10,... | collective-permute-start | bytes 393224 | tf_op jit(solution)/shard_map/ppermute | solution.py:28
  329.9 5.6 collective-permute-done.49
  338.6 5.8 kernel_grad.5
  348.2 6.2 %collective-permute-done.53 = bf16[32,16,128]{2,1,0:T(8,128)(2,1)S(1)} collective-permute-done((bf16[32,16,128]{2,1,0:T(8,128)(2,1)S(1)}, bf16[32,16,128]{2,1,0:T(8,128)(2,1)S(1)}, u32[]{:S(2)}, u32[]{:S(2)}) %collective-permute-start.53) | collective-permute-done | bytes 131104 | tf_op jit(solution)/shard_map/ppermute | solution.py:28
  354.5 8.7 %all-gather.3.cloned.1.call-done = bf16[8,8,16,512]{3,2,1,0:T(8,128)(2,1)} async-done(((bf16[2,8,16,512]{3,2,1,0:T(8,128)(2,1)}), bf16[8,8,16,512]{3,2,1,0:T(8,128)(2,1)}) %all-gather.3.cloned.1.call-update) | async-done | bytes 1048592 | tf_op jit(solution)/shard_map/all_gather | solution.py:734
  376.7 5.8 kernel_grad.4
  383.3 5.9 %conv_part.5 = (f32[4,32,16,128]{3,2,1,0:T(8,128)}, bf16[4,32,16,128]{3,2,1,0:T(8,128)(2,1)}) custom-call(s32[2]{0:T(128)} %get-tuple-element.216.where, bf16[64,16,512]{2,1,0:T(8,128)(2,1)} %reshape.499.field, bf16[1792,512]{1,0:T(8,128)(2,1)} %get-tuple-element.138.weights), custom_call_target="tpu_custom_call" | custom-call | flops 1879048192 | bytes 8388608 | tf_op jit(solution)/shard_map/conv_part/pallas_call | solution.py:351
  402.8 6.2 %collective-permute-done.19 = bf16[32,16,128]{2,1,0:T(8,128)(2,1)S(1)} collective-permute-done((bf16[32,16,128]{2,1,0:T(8,128)(2,1)S(1)}, bf16[32,16,128]{2,1,0:T(8,128)(2,1)S(1)}, u32[]{:S(2)}, u32[]{:S(2)}) %collective-permute-start.19) | collective-permute-done | bytes 131104 | tf_op jit(solution)/shard_map/ppermute | solution.py:28
  413.2 6.9 %conv_back_part.7 = (f32[4,32,16,128]{3,2,1,0:T(8,128)}, bf16[4,32,16,128]{3,2,1,0:T(8,128)(2,1)}) custom-call(s32[2]{0:T(128)} %get-tuple-element.216.where, bf16[64,16,512]{2,1,0:T(8,128)(2,1)} %reshape.511.field.cotangent, bf16[1792,512]{1,0:T(8,128)(2,1)} %get-tuple-element.137.weights), custom_call_target="tpu_custom_call" | custom-call | flops 1879048192 | bytes 8388608 | tf_op jit(solution)/shard_map/conv_back_part/pallas_call | solution.py:434
  420.5 8.3 %all_gather.11 = bf16[64,18]{1,0:T(8,128)(2,1)S(1)} all-gather(bf16[16,18]{1,0:T(8,128)(2,1)S(1)} %add_convert_fusion.1), channel_id=1, replica_groups=mesh['section'=4,'space'=8] {'section'}, dimensions={0}, use_global_device_ids=true | all-gather | bytes 2880 | tf_op jit(solution)/shard_map/all_gather | solution.py:737
  462.9 40.5 %psum.37 = f32[12,512]{1,0:T(8,128)S(1)} all-reduce(f32[12,512]{1,0:T(8,128)S(1)} %concatenate.15), channel_id=1, replica_groups=mesh['section'=4,'space'=8] {'section','space'}, use_global_device_ids=true, to_apply=%region_38.39 | all-reduce | flops 6144 | bytes 49152 | tf_op jit(solution)/shard_map/psum | solution.py:779
  523.8 36.5 %all-reduce.4.cloned.1.call-done = (bf16[1,1728,512]{2,1,0:T(8,128)(2,1)}, bf16[1,1728,512]{2,1,0:T(8,128)(2,1)}, bf16[1,1728,512]{2,1,0:T(8,128)(2,1)}, bf16[1,1728,512]{2,1,0:T(8,128)(2,1)}) async-done(((bf16[1,1728,512]{2,1,0:T(8,128)(2,1)}, bf16[1,1728,512]{2,1,0:T(8,128)(2,1)}, bf16[1,1728,512]{2,1,0:T(8,128)(2,1)}, bf16[1,1728,512]{2,1,0:T(8,128)(2,1)}), (bf16[1,1728,512]{2,1,0:T(8,128)(2,1)}, ...) | async-done | bytes 7077904 | tf_op jit(solution)/shard_map/psum | solution.py:721
  (651 shorter events, 326.7 us)
Async XLA Ops:
  7.2 356.0 %all-gather.3.cloned.1.call-start = ((), (), s32[]{:S(2)}) async-start(), calls=%async_computation.5 | async-start | bytes 1310720 | tf_op jit(solution)/shard_map/all_gather | solution.py:734
  11.1 26.1 %collective-permute-start.2 = (bf16[53,64]{1,0:T(8,128)(2,1)S(1)}, bf16[53,64]{1,0:T(8,128)(2,1)}, u32[]{:S(2)}, u32[]{:S(2)}) collective-permute-start(bf16[53,64]{1,0:T(8,128)(2,1)S(1)} %concatenate.14), channel_id=1, source_target_pairs={{0,6},{1,7},{2,0},{3,1},{4,2},{5,3},{6,4},{7,5},{8,14},{9,15},{10,... | collective-permute-start | bytes 20360 | tf_op jit(solution)/shard_map/ppermute | solution.py:28
  20.1 51.8 %collective-permute-start.26 = (bf16[2,64,2,512]{3,2,1,0:T(2,128)(2,1)}, bf16[2,64,2,512]{3,2,1,0:T(2,128)(2,1)}, u32[]{:S(2)}, u32[]{:S(2)}) collective-permute-start(bf16[2,64,2,512]{3,2,1,0:T(2,128)(2,1)} %pad_maximum_fusion.5), channel_id=1, source_target_pairs={{0,4},{1,5},{2,6},{3,7},{4,0},{5,1},{6,2},{7,3},{8,12},{9,13},{10,... | collective-permute-start | bytes 786440 | tf_op jit(solution)/shard_map/ppermute | solution.py:28
  22.0 45.0 %collective-permute-start.25 = (bf16[2,64,2,512]{3,2,1,0:T(2,128)(2,1)}, bf16[2,64,2,512]{3,2,1,0:T(2,128)(2,1)}, u32[]{:S(2)}, u32[]{:S(2)}) collective-permute-start(bf16[2,64,2,512]{3,2,1,0:T(2,128)(2,1)} %pad_maximum_fusion.5), channel_id=1, source_target_pairs={{0,2},{1,3},{2,4},{3,5},{4,6},{5,7},{6,0},{7,1},{8,10},{9,11},{10,... | collective-permute-start | bytes 786440 | tf_op jit(solution)/shard_map/ppermute | solution.py:28
  33.3 39.6 %collective-permute-start.27 = (bf16[2,64,2,512]{3,2,1,0:T(2,128)(2,1)}, bf16[2,64,2,512]{3,2,1,0:T(2,128)(2,1)S(1)}, u32[]{:S(2)}, u32[]{:S(2)}) collective-permute-start(bf16[2,64,2,512]{3,2,1,0:T(2,128)(2,1)} %pad_maximum_fusion.5), channel_id=1, source_target_pairs={{0,6},{1,7},{2,0},{3,1},{4,2},{5,3},{6,4},{7,5},{8,14},{9,15},{10,... | collective-permute-start | bytes 786440 | tf_op jit(solution)/shard_map/ppermute | solution.py:28
  62.6 46.4 %collective-permute-start.23 = (bf16[2,18,4096]{2,1,0:T(8,128)(2,1)}, bf16[2,18,4096]{2,1,0:T(8,128)(2,1)}, u32[]{:S(2)}, u32[]{:S(2)}) collective-permute-start(bf16[2,18,4096]{2,1,0:T(8,128)(2,1)} %pad_maximum_fusion.4), channel_id=1, source_target_pairs={{0,6},{1,7},{2,0},{3,1},{4,2},{5,3},{6,4},{7,5},{8,14},{9,15},{10,... | collective-permute-start | bytes 884744 | tf_op jit(solution)/shard_map/ppermute | solution.py:28
  65.9 33.8 %collective-permute-start.22 = (bf16[2,18,4096]{2,1,0:T(8,128)(2,1)}, bf16[2,18,4096]{2,1,0:T(8,128)(2,1)S(1)}, u32[]{:S(2)}, u32[]{:S(2)}) collective-permute-start(bf16[2,18,4096]{2,1,0:T(8,128)(2,1)} %pad_maximum_fusion.4), channel_id=1, source_target_pairs={{0,4},{1,5},{2,6},{3,7},{4,0},{5,1},{6,2},{7,3},{8,12},{9,13},{10,... | collective-permute-start | bytes 884744 | tf_op jit(solution)/shard_map/ppermute | solution.py:28
  67.1 24.0 %collective-permute-start.21 = (bf16[2,18,4096]{2,1,0:T(8,128)(2,1)}, bf16[2,18,4096]{2,1,0:T(8,128)(2,1)S(1)}, u32[]{:S(2)}, u32[]{:S(2)}) collective-permute-start(bf16[2,18,4096]{2,1,0:T(8,128)(2,1)} %pad_maximum_fusion.4), channel_id=1, source_target_pairs={{0,2},{1,3},{2,4},{3,5},{4,6},{5,7},{6,0},{7,1},{8,10},{9,11},{10,... | collective-permute-start | bytes 884744 | tf_op jit(solution)/shard_map/ppermute | solution.py:28
  71.9 28.1 %collective-permute-start.7 = (bf16[4,8,16,512]{3,2,1,0:T(8,128)(2,1)S(1)}, bf16[4,8,16,512]{3,2,1,0:T(8,128)(2,1)S(1)}, u32[]{:S(2)}, u32[]{:S(2)}) collective-permute-start(bf16[4,8,16,512]{3,2,1,0:T(8,128)(2,1)S(1)} %bitcast_dynamic-update-slice_fusion.16), channel_id=1, source_target_pairs={{0,1},{1,0},{2,3},{3,2},{4,5},{5,4},{6,7},{7,6},{8,9},{9,8},{10,11... | collective-permute-start | bytes 1572872 | tf_op jit(solution)/shard_map/ppermute | solution.py:32
  73.0 45.0 %collective-permute-start.28 = (bf16[4,2,64,2,512]{4,2,3,1,0:T(8,128)(2,1)S(1)}, bf16[4,2,64,2,512]{4,2,3,1,0:T(8,128)(2,1)}, u32[]{:S(2)}, u32[]{:S(2)}) collective-permute-start(bf16[4,2,64,2,512]{4,2,3,1,0:T(8,128)(2,1)S(1)} %copy_dynamic-update-slice_fusion.4), channel_id=1, source_target_pairs={{0,1},{1,0},{2,3},{3,2},{4,5},{5,4},{6,7},{7,6},{8,9},{9,8},{10,11... | collective-permute-start | bytes 3145736 | tf_op jit(solution)/shard_map/ppermute | solution.py:32
  110.3 62.1 %collective-permute-start.24 = (bf16[4,2,18,4096]{3,1,2,0:T(2,128)(2,1)S(1)}, bf16[4,2,18,4096]{3,1,2,0:T(2,128)(2,1)}, u32[]{:S(2)}, u32[]{:S(2)}) collective-permute-start(bf16[4,2,18,4096]{3,1,2,0:T(2,128)(2,1)S(1)} %copy_dynamic-update-slice_fusion), channel_id=1, source_target_pairs={{0,1},{1,0},{2,3},{3,2},{4,5},{5,4},{6,7},{7,6},{8,9},{9,8},{10,11... | collective-permute-start | bytes 3538952 | tf_op jit(solution)/shard_map/ppermute | solution.py:32
  113.3 32.5 %collective-permute-start.9 = (bf16[32,16,128]{2,1,0:T(8,128)(2,1)}, bf16[32,16,128]{2,1,0:T(8,128)(2,1)S(1)}, u32[]{:S(2)}, u32[]{:S(2)}) collective-permute-start(bf16[32,16,128]{2,1,0:T(8,128)(2,1)} %get-tuple-element.182), channel_id=1, source_target_pairs={{0,2},{1,3},{2,4},{3,5},{4,6},{5,7},{6,0},{7,1},{8,10},{9,11},{10,... | collective-permute-start | bytes 393224 | tf_op jit(solution)/shard_map/ppermute | solution.py:28
  114.0 31.8 %collective-permute-start.11 = (bf16[32,16,128]{2,1,0:T(8,128)(2,1)}, bf16[32,16,128]{2,1,0:T(8,128)(2,1)S(1)}, u32[]{:S(2)}, u32[]{:S(2)}) collective-permute-start(bf16[32,16,128]{2,1,0:T(8,128)(2,1)} %get-tuple-element.183), channel_id=1, source_target_pairs={{0,6},{1,7},{2,0},{3,1},{4,2},{5,3},{6,4},{7,5},{8,14},{9,15},{10,... | collective-permute-start | bytes 393224 | tf_op jit(solution)/shard_map/ppermute | solution.py:28
  117.4 29.7 %collective-permute-start.10 = (bf16[32,16,128]{2,1,0:T(8,128)(2,1)}, bf16[32,16,128]{2,1,0:T(8,128)(2,1)}, u32[]{:S(2)}, u32[]{:S(2)}) collective-permute-start(bf16[32,16,128]{2,1,0:T(8,128)(2,1)} %get-tuple-element.184), channel_id=1, source_target_pairs={{0,4},{1,5},{2,6},{3,7},{4,0},{5,1},{6,2},{7,3},{8,12},{9,13},{10,... | collective-permute-start | bytes 393224 | tf_op jit(solution)/shard_map/ppermute | solution.py:28
  145.7 42.0 %collective-permute-start.29 = (bf16[4,32,16,128]{3,2,1,0:T(8,128)(2,1)}, bf16[4,32,16,128]{3,2,1,0:T(8,128)(2,1)}, u32[]{:S(2)}, u32[]{:S(2)}) collective-permute-start(bf16[4,32,16,128]{3,2,1,0:T(8,128)(2,1)} %get-tuple-element.34), channel_id=1, source_target_pairs={{0,1},{1,0},{2,3},{3,2},{4,5},{5,4},{6,7},{7,6},{8,9},{9,8},{10,11... | collective-permute-start | bytes 1572872 | tf_op jit(solution)/shard_map/ppermute | solution.py:32
  160.9 34.4 %collective-permute-start.42 = (bf16[4,32,16,128]{3,2,1,0:T(8,128)(2,1)}, bf16[4,32,16,128]{3,2,1,0:T(8,128)(2,1)}, u32[]{:S(2)}, u32[]{:S(2)}) collective-permute-start(bf16[4,32,16,128]{3,2,1,0:T(8,128)(2,1)} %get-tuple-element.36), channel_id=1, source_target_pairs={{0,1},{1,0},{2,3},{3,2},{4,5},{5,4},{6,7},{7,6},{8,9},{9,8},{10,11... | collective-permute-start | bytes 1572872 | tf_op jit(solution)/shard_map/ppermute | solution.py:32
  172.4 56.0 %collective-permute-start.16 = (bf16[4,32,16,128]{3,2,1,0:T(8,128)(2,1)}, bf16[4,32,16,128]{3,2,1,0:T(8,128)(2,1)}, u32[]{:S(2)}, u32[]{:S(2)}) collective-permute-start(bf16[4,32,16,128]{3,2,1,0:T(8,128)(2,1)} %bitcast_dynamic-update-slice_fusion.12), channel_id=1, source_target_pairs={{0,1},{1,0},{2,3},{3,2},{4,5},{5,4},{6,7},{7,6},{8,9},{9,8},{10,11... | collective-permute-start | bytes 1572872 | tf_op jit(solution)/shard_map/ppermute | solution.py:32
  249.1 27.1 %collective-permute-start.64 = (bf16[4,32,16,128]{3,2,1,0:T(8,128)(2,1)}, bf16[4,32,16,128]{3,2,1,0:T(8,128)(2,1)}, u32[]{:S(2)}, u32[]{:S(2)}) collective-permute-start(bf16[4,32,16,128]{3,2,1,0:T(8,128)(2,1)} %bitcast_dynamic-update-slice_fusion), channel_id=1, source_target_pairs={{0,1},{1,0},{2,3},{3,2},{4,5},{5,4},{6,7},{7,6},{8,9},{9,8},{10,11... | collective-permute-start | bytes 1572872 | tf_op jit(solution)/shard_map/ppermute | solution.py:32
  270.4 25.6 %collective-permute-start.69 = (bf16[4,8,16,512]{3,2,1,0:T(8,128)(2,1)}, bf16[4,8,16,512]{3,2,1,0:T(8,128)(2,1)}, u32[]{:S(2)}, u32[]{:S(2)}) collective-permute-start(bf16[4,8,16,512]{3,2,1,0:T(8,128)(2,1)} %fusion.12), channel_id=1, source_target_pairs={{0,1},{1,0},{2,3},{3,2},{4,5},{5,4},{6,7},{7,6},{8,9},{9,8},{10,11... | collective-permute-start | bytes 1572872 | tf_op jit(solution)/shard_map/ppermute | solution.py:32
  297.2 26.8 %collective-permute-start.70 = (bf16[8,16,512]{2,1,0:T(8,128)(2,1)S(1)}, bf16[8,16,512]{2,1,0:T(8,128)(2,1)S(1)}, u32[]{:S(2)}, u32[]{:S(2)}) collective-permute-start(bf16[8,16,512]{2,1,0:T(8,128)(2,1)S(1)} %get-tuple-element.156), channel_id=1, source_target_pairs={{0,2},{1,3},{2,4},{3,5},{4,6},{5,7},{6,0},{7,1},{8,10},{9,11},{10,... | collective-permute-start | bytes 393224 | tf_op jit(solution)/shard_map/ppermute | solution.py:28
  298.9 25.2 %collective-permute-start.72 = (bf16[8,16,512]{2,1,0:T(8,128)(2,1)S(1)}, bf16[8,16,512]{2,1,0:T(8,128)(2,1)S(1)}, u32[]{:S(2)}, u32[]{:S(2)}) collective-permute-start(bf16[8,16,512]{2,1,0:T(8,128)(2,1)S(1)} %get-tuple-element.157), channel_id=1, source_target_pairs={{0,6},{1,7},{2,0},{3,1},{4,2},{5,3},{6,4},{7,5},{8,14},{9,15},{10,... | collective-permute-start | bytes 393224 | tf_op jit(solution)/shard_map/ppermute | solution.py:28
  336.6 183.9 %reduce-scatter.4.cloned.1.call-start = ((), (), s32[]{:S(2)}) async-start(), calls=%async_computation.6 | async-start | bytes 294912
  370.5 189.8 %all-reduce.4.cloned.1.call-start = ((), (), s32[]{:S(2)}) async-start(), calls=%async_computation.7 | async-start | bytes 14155776 | tf_op jit(solution)/shard_map/psum | solution.py:721
  459.2 45.5 %all-to-all-start.2 = ((bf16[8,32,2,128]{3,1,2,0:T(8,128)(2,1)}), bf16[8,32,2,128]{3,1,2,0:T(8,128)(2,1)S(1)}, u32[]{:S(2)}, u32[]{:S(2)}) async-start(bf16[8,32,2,128]{3,1,2,0:T(8,128)(2,1)} %bitcast.442), calls=%async_computation.2 | async-start | bytes 262144 | tf_op jit(solution)/shard_map/all_to_all | solution.py:713
  (143 other events, 1502.4 us)
Sparse Core Ops, SparseCore 0:
  336.7 26.4 all-gather.2
  370.6 30.7 reduce-scatter.3
  406.2 154.0 all-reduce.3

commit v2 on v1

--- a/solution.py
+++ b/solution.py
@@ -217,11 +217,26 @@
     )
 
 
+def normed(values, sums, squares, width, members):
+    average = group_means(sums, width, members)
+    square = group_means(squares, width, members)
+    spread = lax.rsqrt(square - average * average + 1e-06)
+    return (values - average) * spread, spread
+
+
+def channel_sums(values):
+    return jnp.sum(values, axis=tuple(range(values.ndim - 1)))
+
+
 VMEM_BYTES = 56 * 1024 * 1024
 
 
 def kernels_fit(channels):
     return chips_of() * LANES == channels
+
+
+def kernel_params():
+    return pltpu.CompilerParams(vmem_limit_bytes=VMEM_BYTES)
 
 
 def shifted(slabs, rows, valid):
@@ -305,64 +320,6 @@
         )
 
 
-def conv_kernel(by_cube, across, where, field, weights, keep, send, rim, patch):
-    first, core = where[0], where[1]
-    rows, channels = field.shape[1:]
-    tiles = channels // LANES
-    count = weights.shape[0] // LANES
-    half = CUBE // 2
-    fill_rim(field, rim, across)
-
-    def part(which):
-        start, size = ((0, half * which), (CUBE, half)) if by_cube else ((half * which, 0), (half, CUBE))
-        fill_patch(rim, patch, first, count, start, size)
-        return jnp.dot(patch[...], weights[...], preferred_element_type=F32)
-
-    for target, which in ((send, 1 - core), (keep, core)):
-        total = part(which).astype(target.dtype)
-        if by_cube:
-            target[...] = total.reshape(target.shape)
-        else:
-            for q in range(tiles):
-                target[q] = total[:, q * LANES : (q + 1) * LANES].reshape(target.shape[1:])
-
-
-def whole_spec():
-    return pl.BlockSpec(memory_space=pltpu.VMEM)
-
-
-def kernel_params():
-    return pltpu.CompilerParams(vmem_limit_bytes=VMEM_BYTES)
-
-
-def here_scalars(first):
-    return jnp.stack([first, lax.axis_index("space") % 2]).astype(jnp.int32)
-
-
-def conv_shares(field, weights, first, across, by_cube):
-    cubes, rows, channels = field.shape
-    count = weights.shape[0] // LANES
-    tiles = channels // LANES
-    if by_cube:
-        shape = (CUBE, cubes // (2 * CUBE), rows, channels)
-    else:
-        shape = (tiles, cubes // 2, rows, LANES)
-    work = cubes * rows * channels * weights.shape[0]
-    return pl.pallas_call(
-        partial(conv_kernel, by_cube, across),
-        out_shape=(jax.ShapeDtypeStruct(shape, F32), jax.ShapeDtypeStruct(shape, BF16)),
-        in_specs=[pl.BlockSpec(memory_space=pltpu.SMEM), whole_spec(), whole_spec()],
-        out_specs=(whole_spec(), whole_spec()),
-        scratch_shapes=[
-            pltpu.VMEM((tiles, CUBE + 2, CUBE + 2, CUBE + 2, rows, LANES), BF16),
-            pltpu.VMEM((cubes // 2 * rows, count * LANES), BF16),
-        ],
-        compiler_params=kernel_params(),
-        cost_estimate=pl.CostEstimate(flops=2 * work, bytes_accessed=8 << 20, transcendentals=0),
-        name="conv_part",
-    )(here_scalars(first), field, weights)
-
-
 def add_taps(field, weights, rim, first):
     rows, channels = field.shape[1:]
     tiles = channels // LANES
@@ -397,142 +354,1007 @@
     lax.fori_loop(0, CUBE, frame, 0)
 
 
-def convt_kernel(across, where, field, weights, keep, send, rim):
-    first, core = where[0], where[1]
-    add_taps(field, weights, rim, first)
-    fold_rim(rim, across)
-    half = CUBE // 2
-    for q in range(rim.shape[0]):
-        for target, which in ((send, 1 - core), (keep, core)):
-            for f in range(half):
-                target[q, pl.ds(f * CUBE * CUBE, CUBE * CUBE)] = (
-                    rim[q, half * which + 1 + f, 1 : CUBE + 1, 1 : CUBE + 1]
-                    .reshape((CUBE * CUBE,) + target.shape[2:])
-                    .astype(target.dtype)
-                )
-
-
-def convt_whole_kernel(across, where, field, weights, out, rim):
-    add_taps(field, weights, rim, where[0])
-    fold_rim(rim, across)
-    for q in range(rim.shape[0]):
-        for f in range(CUBE):
-            out[pl.ds(f * CUBE * CUBE, CUBE * CUBE), :, q * LANES : (q + 1) * LANES] = rim[
-                q, 1 + f, 1 : CUBE + 1, 1 : CUBE + 1
-            ].reshape((CUBE * CUBE,) + out.shape[1:2] + (LANES,))
-
-
-def convt_shares(field, weights, first, across, whole):
+def group_totals(row, width):
+    lanes = row.shape[1]
+    lane = lax.broadcasted_iota(jnp.int32, row.shape, 1)
+    step = 1
+    while step < width:
+        before = pltpu.roll(row, step, 1)
+        after = pltpu.roll(row, lanes - step, 1)
+        row = row + jnp.where(lane // step % 2 == 1, before, after)
+        step *= 2
+    return row
+
+
+def row_sum(values):
+    return jnp.sum(values.reshape(-1, values.shape[-1]), axis=0, keepdims=True)
+
+
+def logistic_of(values):
+    return 0.5 + 0.5 * jnp.tanh(0.5 * values)
+
+
+def both_halves(row):
+    return row + pltpu.roll(row, LANES // 2, 1)
+
+
+def pack_pair(near, far, core):
+    axis = near.ndim - 1
+    lane = lax.broadcasted_iota(jnp.int32, near.shape, axis)
+    low = lane < LANES // 2
+    first = jnp.where(low, near, pltpu.roll(far, LANES // 2, axis))
+    second = jnp.where(low, pltpu.roll(near, LANES // 2, axis), far)
+    lead = lane * 0 + core == 0
+    return jnp.where(lead, first, second), jnp.where(lead, second, first)
+
+
+def unpack_pair(own, other, core):
+    axis = own.ndim - 1
+    lane = lax.broadcasted_iota(jnp.int32, own.shape, axis)
+    low = lane < LANES // 2
+    lead = lane * 0 + core == 0
+    first, second = jnp.where(lead, own, other), jnp.where(lead, other, own)
+    near = jnp.where(low, first, pltpu.roll(second, LANES // 2, axis))
+    far = jnp.where(low, pltpu.roll(first, LANES // 2, axis), second)
+    return near, far
+
+
+def own_row(table, index, z, core):
+    lanes = pl.ds(pl.multiple_of(z * LANES, LANES), LANES)
+    row = table[index : index + 1, lanes]
+    mine, _ = pack_pair(row, row, core)
+    return mine
+
+
+def pack_own(field, out, z, core):
+    lanes = pl.ds(pl.multiple_of(z * LANES, LANES), LANES)
+    half = field.shape[0] // 2
+
+    def some(i, carry):
+        near = field[pl.ds(8 * i, 8), :, lanes].astype(F32)
+        far = field[pl.ds(half + 8 * i, 8), :, lanes].astype(F32)
+        out[pl.ds(8 * i, 8)] = pack_pair(near, far, core)[0].astype(out.dtype)
+        return carry
+
+    lax.fori_loop(0, half // 8, some, 0)
+
+
+def unpack_stacks(own, other, field, z, core, relative):
+    chips, half = own.shape[:2]
+    for hop in range(chips):
+        place = lax.rem(z + chips - hop, chips) if relative else hop
+        lanes = pl.ds(pl.multiple_of(place * LANES, LANES), LANES)
+
+        def some(i, carry, hop=hop, lanes=lanes):
+            mine = own[hop, pl.ds(8 * i, 8)].astype(F32)
+            twin = other[hop, pl.ds(8 * i, 8)].astype(F32)
+            near, far = unpack_pair(mine, twin, core)
+            field[pl.ds(8 * i, 8), :, lanes] = near.astype(field.dtype)
+            field[pl.ds(half + 8 * i, 8), :, lanes] = far.astype(field.dtype)
+            return carry
+
+        lax.fori_loop(0, half // 8, some, 0)
+
+
+class Rows:
+    def __init__(self, weights, index, offset, wide, sem):
+        count = weights.shape[1]
+        slack = wide.shape[0] - count
+        blank = jnp.zeros((slack, wide.shape[1]), wide.dtype)
+        wide[0:slack, :] = blank
+        wide[count : count + slack, :] = blank
+        target = wide.at[pl.ds(pl.multiple_of(offset, 64), count), :]
+        self.copy = pltpu.make_async_copy(weights.at[index], target, sem)
+        self.copy.start()
+
+    def ready(self):
+        self.copy.wait()
+
+
+def norm_in(field, act, table, gain, shift, stats, group, members):
     cubes, rows, channels = field.shape
-    tiles = channels // LANES
-    shape = (tiles, cubes // 2, rows, LANES)
-    if whole:
-        out_shape = (jax.ShapeDtypeStruct(field.shape, F32),)
+
+    def add(i, carry):
+        values = field[pl.ds(4 * i, 4)].astype(F32)
+        folded = values.reshape(-1, 8, channels)
+        return (carry[0] + jnp.sum(folded, 0), carry[1] + jnp.sum(folded * folded, 0))
+
+    blank = jnp.zeros((8, channels), F32)
+    totals, squares = lax.fori_loop(0, cubes // 4, add, (blank, blank))
+    sums = jnp.concatenate(
+        [jnp.sum(totals, 0, keepdims=True), jnp.sum(squares, 0, keepdims=True)], axis=0
+    )
+    means = group_totals(sums, group) / members
+    average = means[0:1]
+    spread = lax.rsqrt(means[1:2] - average * average + 1e-06)
+    stats[0:1, :] = average
+    stats[1:2, :] = spread
+    scale, start = table[gain : gain + 1, :], table[shift : shift + 1, :]
+
+    def apply(i, carry):
+        values = field[pl.ds(4 * i, 4)].astype(F32)
+        flat = (values - average[None]) * spread[None]
+        normal = flat * scale[None] + start[None]
+        act[pl.ds(4 * i, 4)] = (normal * logistic_of(normal)).astype(act.dtype)
+        return carry
+
+    lax.fori_loop(0, cubes // 4, apply, 0)
+
+
+def multiply(patch, wide, product):
+    size = product.shape[1]
+
+    for f in range(product.shape[0]):
+        rows = slice(f * size, (f + 1) * size)
+        product[f] = jnp.dot(patch[rows, :], wide[...], preferred_element_type=F32)
+
+
+def share_blocks(frame_block, keep, send, core):
+    tiles, cubes = keep.shape[0], CUBE * CUBE
+
+    def pair(i, carry):
+        for q in range(tiles):
+            mine, twin = pack_pair(frame_block(i, q), frame_block(i + CUBE // 2, q), core)
+            keep[q, pl.ds(i * cubes, cubes)] = mine
+            send[q, pl.ds(i * cubes, cubes)] = twin.astype(send.dtype)
+        return carry
+
+    lax.fori_loop(0, CUBE // 2, pair, 0)
+
+
+def of_product(product, rows):
+    def block(f, q):
+        return product[f, :, q * LANES : (q + 1) * LANES].reshape(CUBE * CUBE, rows, LANES)
+
+    return block
+
+
+def of_rim(rim):
+    rows = rim.shape[4]
+
+    def block(f, q):
+        inner = rim[q, f + 1, 1 : CUBE + 1, 1 : CUBE + 1]
+        return inner.reshape(CUBE * CUBE, rows, LANES)
+
+    return block
+
+
+def first_conv_kernel(settings, where, *refs):
+    stacked, across, group, members, gain, shift, index = settings
+    if stacked:
+        own, other, table, weights, keep, send, act, stats, mine, field = refs[:10]
+        rim, patch, wide, product, sem = refs[10:]
     else:
-        out_shape = (jax.ShapeDtypeStruct(shape, F32), jax.ShapeDtypeStruct(shape, BF16))
-    work = cubes * rows * channels * weights.shape[0]
-    return pl.pallas_call(
-        partial(convt_whole_kernel if whole else convt_kernel, across),
-        out_shape=out_shape,
-        in_specs=[pl.BlockSpec(memory_space=pltpu.SMEM), whole_spec(), whole_spec()],
-        out_specs=tuple(whole_spec() for _ in out_shape),
-        scratch_shapes=[pltpu.VMEM((tiles, CUBE + 2, CUBE + 2, CUBE + 2, rows, LANES), F32)],
-        compiler_params=kernel_params(),
-        cost_estimate=pl.CostEstimate(flops=2 * work, bytes_accessed=8 << 20, transcendentals=0),
-        name="conv_back_part",
-    )(here_scalars(first), field, weights)
-
-
-def grad_kernel(across, where, field, cotangent, out, rim, patch, wide):
-    rows, channels = field.shape[1:]
-    count = patch.shape[1] // LANES
-    fill_rim(field, rim, across)
-    fill_patch(rim, patch, where[0], count, (0, 0), (CUBE, CUBE))
-    source = cotangent[...].reshape(-1, channels)
-    for j in range(0, count, 2):
-        lanes = slice(j * LANES, min(j + 2, count) * LANES)
-        wide[lanes, :] = lax.dot_general(
+        field, table, weights, keep, send, act, stats, mine = refs[:8]
+        rim, patch, wide, product, sem = refs[8:]
+    first, offset, z, core = where[0], where[1], where[2], where[3]
+    coming = Rows(weights, index, offset, wide, sem)
+    if stacked:
+        chips, count = own.shape[:2]
+        for hop in range(chips):
+            place = lax.rem(z + chips - hop, chips) * 2
+            field[pl.ds((place + core) * count, count)] = own[hop]
+            field[pl.ds((place + 1 - core) * count, count)] = other[hop]
+    rows = field.shape[1]
+    norm_in(field, act, table, gain, shift, stats, group, members)
+    fill_rim(act, rim, across)
+    fill_patch(rim, patch, first, patch.shape[1] // LANES, (0, 0), (CUBE, CUBE))
+    coming.ready()
+    multiply(patch, wide, product)
+    share_blocks(of_product(product, rows), keep, send, core)
+    pack_own(field, mine, z, core)
+
+
+def fill_grad(patch, source, offset, grad, out):
+    count = patch.shape[1]
+    for j in range(0, count, 2 * LANES):
+        lanes = slice(j, min(j + 2 * LANES, count))
+        grad[lanes, :] = lax.dot_general(
             patch[:, lanes], source, (((0,), (0,)), ((), ())), preferred_element_type=F32
         )
-    start = pl.multiple_of(where[1], 8)
-    out[...] = wide[pl.ds(start, out.shape[0]), :].astype(out.dtype)
-
-
-def kernel_grad_here(field, cotangent, first, offset, row_count, across):
-    cubes, rows, channels = field.shape
+    start = pl.multiple_of(offset, 64)
+    out[...] = grad[pl.ds(start, out.shape[0]), :].astype(out.dtype)
+
+
+def second_conv_kernel(across, with_grad, index, where, *refs):
+    if with_grad:
+        own, other, weights, cotangent, keep, send, out, field = refs[:8]
+        rim, patch, wide, product, sem, grad = refs[8:]
+    else:
+        own, other, weights, keep, send, field = refs[:6]
+        rim, patch, wide, product, sem = refs[6:]
+    first, offset, z, core = where[0], where[1], where[2], where[3]
+    rows, channels = field.shape[1:]
+    coming = Rows(weights, index, offset, wide, sem)
+    unpack_stacks(own, other, field, z, core, False)
+    fill_rim(field, rim, across)
+    fill_patch(rim, patch, first, patch.shape[1] // LANES, (0, 0), (CUBE, CUBE))
+    coming.ready()
+    multiply(patch, wide, product)
+    if with_grad:
+        share_blocks(of_product(product, rows), keep, send, core)
+        fill_grad(patch, cotangent[...].reshape(-1, channels), offset, grad, out)
+    else:
+
+        def frame(f, carry):
+            low = product[f, : CUBE * CUBE * rows // 2]
+            high = product[f, CUBE * CUBE * rows // 2 :]
+            lead = lax.broadcasted_iota(jnp.int32, low.shape, 1) * 0 + core == 0
+            keep[f] = jnp.where(lead, low, high).reshape(keep.shape[1:])
+            send[f] = jnp.where(lead, high, low).reshape(send.shape[1:]).astype(send.dtype)
+            return carry
+
+        lax.fori_loop(0, CUBE, frame, 0)
+
+
+def grad_only_kernel(across, where, field, cotangent, out, rim, patch, grad):
+    channels = field.shape[2]
+    fill_rim(field, rim, across)
+    fill_patch(rim, patch, where[0], patch.shape[1] // LANES, (0, 0), (CUBE, CUBE))
+    fill_grad(patch, cotangent[...].reshape(-1, channels), where[1], grad, out)
+
+
+def twin_add_kernel(where, keep, received, own, *sends):
+    chips, z = keep.shape[0], where[2]
+    own[...] = keep[z] + received[z].astype(F32)
+    for hop, send in enumerate(sends):
+        target = lax.rem(z + 1 + hop, chips)
+        send[...] = (keep[target] + received[target].astype(F32)).astype(send.dtype)
+
+
+def twin_sums_kernel(count, where, *refs):
+    out = refs[2 * count]
+    lanes = out.shape[-1]
+    for i in range(count):
+        keep, received = refs[2 * i], refs[2 * i + 1]
+        for target in range(out.shape[0]):
+            total = (keep[target] + received[target].astype(F32)).astype(out.dtype)
+            if total.shape[-1] == lanes:
+                out[target, i] = total
+            else:
+                parts = total.shape[-1] // lanes
+                for cube in range(total.shape[0]):
+                    for q in range(parts):
+                        out[target, i, cube * parts + q] = total[cube, :, q * lanes : (q + 1) * lanes]
+
+
+def total_of(pieces):
+    if len(pieces) == 1:
+        return jnp.sum(pieces[0][...].astype(F32), axis=0)
+    total = pieces[0][...]
+    for piece in pieces[1:]:
+        total = total + piece[...].astype(F32)
+    return total
+
+
+def mid_norm(middle, table, gain, shift, z, core, group, members):
+    sums = jnp.concatenate([row_sum(middle), row_sum(middle * middle)], axis=0)
+    means = group_totals(both_halves(sums), group) / members
+    average = means[0:1]
+    spread = lax.rsqrt(means[1:2] - average * average + 1e-06)
+    flat = (middle - average[None]) * spread[None]
+    scale = own_row(table, gain, z, core)
+    normal = flat * scale[None] + own_row(table, shift, z, core)[None]
+    return flat, spread, normal, logistic_of(normal), scale
+
+
+def mid_back(raw, normed_state, group, members):
+    flat, spread, normal, logistic, scale = normed_state
+    pre = raw * (logistic * (1.0 + normal * (1.0 - logistic)))
+    sums = jnp.concatenate([row_sum(pre), row_sum(pre * flat)], axis=0)
+    sums = both_halves(sums)
+    means = group_totals(sums * scale, group) / members
+    back = spread[None] * (pre * scale[None] - means[0:1][None] - flat * means[1:2][None])
+    return back, sums
+
+
+def mid_ahead_kernel(settings, where, *refs):
+    group, members, gain, shift, bias, chips = settings
+    pieces, table, act, kept = refs[:chips], refs[chips], refs[chips + 1], refs[chips + 2]
+    z, core = where[2], where[3]
+    middle = total_of(pieces) + own_row(table, bias, z, core)[None]
+    kept[...] = middle
+    state = mid_norm(middle, table, gain, shift, z, core, group, members)
+    act[...] = (state[2] * state[3]).astype(act.dtype)
+
+
+def mid_back_kernel(settings, where, *refs):
+    group, members, gain, shift, chips = settings
+    pieces, kept, table, inner, sums = refs[:chips], *refs[chips:]
+    z, core = where[2], where[3]
+    state = mid_norm(kept[...], table, gain, shift, z, core, group, members)
+    back, rows = mid_back(total_of(pieces), state, group, members)
+    inner[...] = back.astype(inner.dtype)
+    sums[...] = rows
+
+
+def mid_both_kernel(settings, where, *refs):
+    group, members, gain, shift, bias, chips = settings
+    ahead, behind = refs[:chips], refs[chips : chips + 1]
+    table, act, inner, sums = refs[chips + 1 :]
+    z, core = where[2], where[3]
+    middle = total_of(ahead) + own_row(table, bias, z, core)[None]
+    state = mid_norm(middle, table, gain, shift, z, core, group, members)
+    act[...] = (state[2] * state[3]).astype(act.dtype)
+    back, rows = mid_back(total_of(behind), state, group, members)
+    inner[...] = back.astype(inner.dtype)
+    sums[...] = rows
+
+
+def last_back_kernel(settings, where, *refs):
+    group, members, gain, shift, chips = settings
+    pieces = refs[:chips]
+    inputs, cotangent, stats, table, out, sums = refs[chips:]
+    z, core = where[2], where[3]
+    average, spread = own_row(stats, 0, z, core), own_row(stats, 1, z, core)
+    flat = (inputs[...].astype(F32) - average[None]) * spread[None]
+    scale = own_row(table, gain, z, core)
+    normal = flat * scale[None] + own_row(table, shift, z, core)[None]
+    state = (flat, spread, normal, logistic_of(normal), scale)
+    back, rows = mid_back(total_of(pieces), state, group, members)
+    out[...] = (cotangent[...].astype(F32) + back).astype(out.dtype)
+    sums[...] = rows
+
+
+def share_rim(field, coming, where, wide, rim, across, keep, send):
+    coming.ready()
+    add_taps(field, wide, rim, where[0])
+    fold_rim(rim, across)
+    share_blocks(of_rim(rim), keep, send, where[3])
+
+
+def back_kernel(across, index, where, field, weights, keep, send, wide, rim, sem):
+    coming = Rows(weights, index, where[1], wide, sem)
+    share_rim(field, coming, where, wide, rim, across, keep, send)
+
+
+def back_stacked_kernel(across, index, where, own, other, weights, keep, send, field, *work):
+    wide, rim, sem = work
+    coming = Rows(weights, index, where[1], wide, sem)
+    unpack_stacks(own, other, field, where[2], where[3], True)
+    share_rim(field, coming, where, wide, rim, across, keep, send)
+
+
+def back_signs_kernel(settings, where, tiny, maps, weights, keep, send, field, mine, *work):
+    across, bits, index = settings
+    wide, rim, sem = work
+    coming = Rows(weights, index, where[1], wide, sem)
+    rows, channels = field.shape[1:]
+    signs = tiny[0:rows, 0:bits].astype(BF16)
+    parts, slabs = maps.shape[:2]
+    size = field.shape[0] // (slabs * parts)
+
+    def slab(s, carry):
+        for p in range(parts):
+            wave = jnp.dot(signs, maps[p, s], preferred_element_type=F32)
+            for j in range(size):
+                cube = (s * parts + p) * size + j
+                field[cube] = wave[:, j * channels : (j + 1) * channels].astype(BF16)
+        return carry
+
+    lax.fori_loop(0, slabs, slab, 0)
+    share_rim(field, coming, where, wide, rim, across, keep, send)
+    pack_own(field, mine, where[2], where[3])
+
+
+def back_whole_kernel(settings, where, *refs):
+    across, group, members, gain, shift, bits, index = settings
+    own, other, weights, inputs, stats, table, cotangent, maps = refs[:8]
+    keep, send, tiny, field = refs[8:12]
+    wide, rim, sem, pre_ref, low, sums = refs[12:]
+    z, core = where[2], where[3]
+    tiles, rows, channels = rim.shape[0], rim.shape[4], field.shape[2]
+    size = CUBE * CUBE
+    coming = Rows(weights, index, where[1], wide, sem)
+    unpack_stacks(own, other, field, z, core, True)
+    coming.ready()
+    add_taps(field, wide, rim, where[0])
+    fold_rim(rim, across)
+    sums[...] = jnp.zeros(sums.shape, F32)
+    block = of_rim(rim)
+
+    def at(f, q):
+        lanes = slice(q * LANES, (q + 1) * LANES)
+        values = inputs[pl.ds(f * size, size), :, lanes].astype(F32)
+        flat = (values - stats[0:1, lanes][None]) * stats[1:2, lanes][None]
+        return flat, lanes
+
+    def ahead(f, carry):
+        for q in range(tiles):
+            flat, lanes = at(f, q)
+            normal = flat * table[gain : gain + 1, lanes][None] + table[shift : shift + 1, lanes][None]
+            logistic = logistic_of(normal)
+            pre = block(f, q) * (logistic * (1.0 + normal * (1.0 - logistic)))
+            pre_ref[q, pl.ds(f * size, size)] = pre
+            sums[0:1, lanes] += row_sum(pre)
+            sums[1:2, lanes] += row_sum(pre * flat)
+        return carry
+
+    lax.fori_loop(0, CUBE, ahead, 0)
+    means = group_totals(sums[0:2, :] * table[gain : gain + 1, :], group) / members
+    lead_slab = (2 * z + core == 0).astype(F32)
+    half = size // 2
+
+    def behind(f, carry):
+        for q in range(tiles):
+            flat, lanes = at(f, q)
+            scaled = pre_ref[q, pl.ds(f * size, size)] * table[gain : gain + 1, lanes][None]
+            back = stats[1:2, lanes][None] * (
+                scaled - means[0:1, lanes][None] - flat * means[1:2, lanes][None]
+            )
+            back = back + cotangent[pl.ds(f * size, size), :, lanes].astype(F32) * lead_slab
+            low[pl.ds(f * size, size), :, lanes] = back.astype(BF16)
+            lead = lax.broadcasted_iota(jnp.int32, (half, rows, LANES), 2) * 0 + core == 0
+            keep[f, :, :, lanes] = jnp.where(lead, back[:half], back[half:])
+            send[f, :, :, lanes] = jnp.where(lead, back[half:], back[:half]).astype(BF16)
+        return carry
+
+    lax.fori_loop(0, CUBE, behind, 0)
+    parts, slabs = maps.shape[:2]
+    size = field.shape[0] // (slabs * parts)
+
+    def slab(s, total):
+        for p in range(parts):
+            cube = (s * parts + p) * size
+            wave = jnp.concatenate([low[cube + j] for j in range(size)], axis=1)
+            total = total + lax.dot_general(
+                wave, maps[p, s], (((1,), (1,)), ((), ())), preferred_element_type=F32
+            )
+        return total
+
+    signs = lax.fori_loop(0, slabs, slab, jnp.zeros((rows, bits), F32))
+    tiny[...] = jnp.zeros(tiny.shape, F32)
+    tiny[0:rows, 0:bits] = signs
+    for q in range(tiles):
+        lanes = slice(q * LANES, (q + 1) * LANES)
+        tiny[rows + q : rows + q + 1, :] = sums[0:1, lanes]
+        tiny[rows + tiles + q : rows + tiles + q + 1, :] = sums[1:2, lanes]
+
+
+def fast_body(
+    video_clips,
+    code_bits,
+    recon_grad,
+    enc_convs,
+    enc_gains,
+    enc_shifts,
+    down_weight,
+    down_bias,
+    down_proj,
+    up_proj,
+    up_bias,
+    up_weight,
+    upsample_bias,
+    dec_convs,
+    dec_gains,
+    dec_shifts,
+):
+    section = lax.axis_index("section")
+    space = lax.axis_index("space")
+    z, core = here()
+    sections = lax.axis_size("section")
+    spaces = lax.axis_size("space")
+    chips = chips_of()
+    clips, frames, height, width, channels = video_clips.shape
+    across = width // CUBE
+    bits = code_bits.shape[-1]
+    rows = spaces * across
+    cubes = CUBE**3
+    own_cubes = cubes // spaces
+    half = cubes // 2
+    group = channels // GROUPS
+    members = float(cubes * rows * group)
+    lanes = down_bias.shape[0]
+    row_count = enc_convs.shape[1]
+    total_rows = block_count(row_count) * LANES
     tiles = channels // LANES
-    count = block_count(row_count)
-    work = cubes * rows * channels * count * LANES
-    return pl.pallas_call(
-        partial(grad_kernel, across),
-        out_shape=jax.ShapeDtypeStruct((row_count, channels), BF16),
-        in_specs=[pl.BlockSpec(memory_space=pltpu.SMEM), whole_spec(), whole_spec()],
-        out_specs=whole_spec(),
-        scratch_shapes=[
-            pltpu.VMEM((tiles, CUBE + 2, CUBE + 2, CUBE + 2, rows, LANES), BF16),
-            pltpu.VMEM((cubes * rows, count * LANES), BF16),
-            pltpu.VMEM((count * LANES, channels), F32),
-        ],
-        compiler_params=kernel_params(),
-        cost_estimate=pl.CostEstimate(flops=2 * work, bytes_accessed=8 << 20, transcendentals=0),
-        name="kernel_grad",
-    )(jnp.stack([first, offset]).astype(jnp.int32), field, cotangent)
-
-
-def chips_summed(mine):
-    chips = chips_of()
-    z, _ = here()
-    total = picked(mine, z)
-    for step in range(1, chips):
-        sent = picked(mine, (z + step) % chips).astype(BF16)
-        total = total + along_chips(sent, step).astype(F32)
-    return total
-
-
-def conv_scattered(field, weights, first, across, by_cube=False):
-    if kernels_fit(field.shape[-1]):
-        keep, send = conv_shares(field, weights, first, across, by_cube)
-        return chips_summed(keep + to_twin(send).astype(F32))
-    part, _ = conv_part(field, weights, first, across)
-    if by_cube:
-        cubes, rows, channels = part.shape
-        return scattered(part.reshape(chips_of(), 2, -1, rows, channels))
-    return scattered(to_blocks(part))
-
-
-def convt_scattered(field, weights, first, across):
-    if kernels_fit(field.shape[-1]):
-        keep, send = convt_shares(field, weights, first, across, False)
-        return chips_summed(keep + to_twin(send).astype(F32))
-    return scattered(to_blocks(convt_part(field, weights, first, across)))
-
-
-def convt_whole(field, weights, first, across):
-    if kernels_fit(field.shape[-1]):
-        return convt_shares(field, weights, first, across, True)[0]
-    return convt_part(field, weights, first, across)
-
-
-def kernel_grads(field, cotangent, first, offset, row_count, across):
-    if kernels_fit(field.shape[-1]):
-        return kernel_grad_here(field, cotangent, first, offset, row_count, across)
-    patch = patches(field, first, block_count(row_count), across)
-    grad = kernel_grad(patch, cotangent)
-    return lax.dynamic_slice_in_dim(grad, offset, row_count, 0).astype(BF16)
-
-
-def normed(values, sums, squares, width, members):
-    average = group_means(sums, width, members)
-    square = group_means(squares, width, members)
-    spread = lax.rsqrt(square - average * average + 1e-06)
-    return (values - average) * spread, spread
-
-
-def channel_sums(values):
-    return jnp.sum(values, axis=tuple(range(values.ndim - 1)))
-
-
-def body(
+    first, offset = rows_here(enc_convs)
+    where = jnp.stack([first, offset, z, core]).astype(jnp.int32)
+
+    def arr(shape, dtype):
+        return jax.ShapeDtypeStruct(shape, dtype)
+
+    full = arr((cubes, rows, channels), BF16)
+    piece_b, piece_f = arr((half, rows, LANES), BF16), arr((half, rows, LANES), F32)
+    blocks_f, blocks_b = arr((tiles, half, rows, LANES), F32), arr((tiles, half, rows, LANES), BF16)
+    cubes_f = arr((CUBE, half // CUBE, rows, channels), F32)
+    cubes_b = arr((CUBE, half // CUBE, rows, channels), BF16)
+    stats_f = arr((8, channels), F32)
+    sums_f = arr((2, LANES), F32)
+    grad_b = arr((row_count, channels), BF16)
+    rim_shape = (tiles, CUBE + 2, CUBE + 2, CUBE + 2, rows, LANES)
+    rim_b, rim_f = pltpu.VMEM(rim_shape, BF16), pltpu.VMEM(rim_shape, F32)
+    patch = pltpu.VMEM((cubes * rows, total_rows), BF16)
+    wide = pltpu.VMEM((total_rows, channels), BF16)
+    grad_s = pltpu.VMEM((total_rows, channels), F32)
+    product = pltpu.VMEM((CUBE, cubes * rows // CUBE, channels), F32)
+    spec = pl.BlockSpec(memory_space=pltpu.VMEM)
+    conv_flops = 2 * cubes * rows * channels * total_rows
+
+    hbm = pl.BlockSpec(memory_space=pltpu.HBM)
+    enc_convs, dec_convs = (
+        pltpu.with_memory_space_constraint(w, pltpu.HBM) for w in (enc_convs, dec_convs)
+    )
+    arrival = pltpu.SemaphoreType.DMA
+
+    def piece_spec(index):
+        return pl.BlockSpec((chips, None, half, rows, LANES), lambda i: (0, index, 0, 0, 0))
+
+    order = [where]
+
+    def call(kernel, name, out_shape, scratch, specs, args, flops=conv_flops, mib=28, held=(), after=()):
+        place, anywhere = pl.BlockSpec(memory_space=pltpu.SMEM), pl.BlockSpec(memory_space=pl.ANY)
+        inner, outer = len(args), len(out_shape)
+
+        def ordered(*refs):
+            skip = inner + len(held) + len(after)
+            given, handed = refs[0], refs[1 + skip]
+            for i in range(given.shape[0]):
+                handed[i] = given[i]
+            outs = 2 + skip
+            scratch_refs = refs[outs + outer + len(held) :]
+            kernel(given, *refs[1 : 1 + inner], *refs[outs : outs + outer], *scratch_refs)
+
+        made = pl.pallas_call(
+            ordered,
+            grid=(1,),
+            out_shape=(arr(where.shape, jnp.int32),)
+            + tuple(out_shape)
+            + tuple(arr(h.shape, h.dtype) for h in held),
+            in_specs=[place] + specs + [anywhere] * (len(held) + len(after)),
+            out_specs=(place,) + tuple(spec for _ in out_shape) + (anywhere,) * len(held),
+            scratch_shapes=scratch,
+            input_output_aliases={1 + inner + i: 1 + outer + i for i in range(len(held))},
+            compiler_params=pltpu.CompilerParams(vmem_limit_bytes=mib << 20),
+            cost_estimate=pl.CostEstimate(flops=flops, bytes_accessed=6 << 20, transcendentals=0),
+            name=name,
+        )(order[0], *args, *held, *after)
+        order[0] = made[0]
+        return made[1:]
+
+    def z_hops(value):
+        return [along_chips(value, step) for step in range(1, chips)]
+
+    def gather_stacks(piece, hops=None):
+        stack = jnp.stack([piece] + (hops or z_hops(piece)))
+        return stack, to_twin(stack)
+
+    def scatter_pieces(shares, held=(), after=()):
+        keep, received = shares
+        shape = keep.shape[1:]
+        outs = (arr(shape, F32),) + tuple(arr(shape, BF16) for _ in range(chips - 1))
+        made = call(
+            twin_add_kernel, "twin_add", outs, [], [spec, spec], shares, 1, 8, held, after
+        )
+        hops = [along_chips(s, step) for step, s in zip(range(1, chips), made[1:chips])]
+        return [made[0]] + hops, made[chips:]
+
+    line = [[2 * chip + c for chip in range(chips)] for c in range(2)]
+
+    def swap_chips(value):
+        return lax.all_to_all(value, "space", 0, 0, axis_index_groups=line, tiled=True)
+
+    def scatter_swap(shares, held=(), after=()):
+        flat = [v for pair in shares for v in pair]
+        out = arr((chips, len(shares), half, rows, LANES), BF16)
+        made = call(
+            partial(twin_sums_kernel, len(shares)),
+            "twin_sums",
+            (out,),
+            [],
+            [spec] * len(flat),
+            flat,
+            1,
+            16,
+            held,
+            after,
+        )
+        return swap_chips(made[0]), made[1:]
+
+    def tiny_gather(value):
+        chain = z_hops(value)[::-1] + [value]
+        stack = jnp.stack(chain)
+        twin = to_twin(stack)
+        pair = jnp.where(core == 0, jnp.stack([stack, twin], 1), jnp.stack([twin, stack], 1))
+        return lax.dynamic_slice_in_dim(jnp.concatenate([pair, pair]), chips - 1 - z, chips, 0)
+
+    def to_output(pieces):
+        count, split = pieces.shape[0], LANES // 2
+        parts = pieces.reshape(count, half, spaces, across, LANES).transpose(2, 0, 1, 3, 4)
+        got = lax.all_to_all(parts, "space", 0, 0, tiled=True)
+        got = got.reshape(spaces, count, half, across, 2, split).transpose(1, 4, 2, 3, 0, 5)
+        slab = got.reshape(count, cubes, across, channels)
+        slab = jax.vmap(lambda v: slab_of(v, (frames, height, width, channels)))(slab)
+        slab = slab.reshape(count, frames, height, width, sections, channels // sections)
+        slab = lax.all_to_all(slab.transpose(4, 0, 1, 2, 3, 5), "section", 0, 0, tiled=True)
+        return tuple(slab[:, i] for i in range(count))
+
+    def own_channels(row):
+        return lax.dynamic_slice_in_dim(row, space * lanes, lanes, row.ndim - 1)
+
+    code = code_bits.reshape(-1).astype(BF16)
+    code = jnp.pad(code, (0, -code.shape[0] % lanes)).reshape(-1, lanes)
+    small = jnp.concatenate(
+        [enc_gains, dec_gains, enc_shifts, dec_shifts, up_bias[None], down_bias[None]]
+        + [up_proj.T, down_proj.T, code],
+        axis=0,
+    )
+    recon_slab = cubes_of(picked(recon_grad, section))
+    (small,) = call(lambda where: None, "first", (), [], [], (), 1, 8, (small,), (recon_slab,))
+    small = tiny_gather(small).reshape(spaces, small.shape[0], lanes)
+    heads = 14 + 2 * bits
+    heading = small[:, :heads].transpose(1, 0, 2).reshape(heads, channels)
+    table = jnp.pad(heading[:14].astype(F32), ((0, 2), (0, 0)))
+    up_cols, down_cols = heading[14 : 14 + bits], heading[14 + bits :]
+    count = clips * across * bits
+    code_all = small[:, heads:].reshape(spaces, -1)[:, :count].reshape(spaces, clips, across, bits)
+    signs = (2 * code_all - 1).transpose(1, 0, 2, 3).reshape(clips * rows, bits)
+
+    def cube_map(columns, weight):
+        size = weight.shape[0] // sections
+        part = lax.dynamic_slice_in_dim(weight, section * size, size, 0)
+        made = lax.dot_general(
+            columns, part, (((1,), (1,)), ((), ())), preferred_element_type=F32
+        )
+        return made.astype(BF16).reshape(bits, -1, channels)
+
+    def field_from(every):
+        return every.transpose(1, 0, 2, 3).reshape(cubes, rows, channels)
+
+    recon_cot = field_from(lax.all_gather(recon_slab, "space", axis=0))
+    hidden = (jnp.dot(signs, up_cols, preferred_element_type=F32) + table[12]).astype(BF16)
+    hidden_own = lax.dynamic_slice_in_dim(hidden, section * rows, rows, 0)
+    grown = lax.dot_general(
+        hidden_own, up_weight, (((1,), (1,)), ((), ())), preferred_element_type=F32
+    )
+    grown = (grown + upsample_bias.astype(F32)).astype(BF16)
+    grown = grown.reshape(rows, own_cubes, channels).transpose(1, 0, 2)
+    grown_own, grown_twin = gather_stacks(grown)
+
+    def map_spec(index):
+        shape = (sections, spaces, None, bits, own_cubes * channels // sections)
+        return pl.BlockSpec(shape, lambda i: (0, 0, index, 0, 0))
+
+    def with_twin(keep, send, *rest):
+        return ((keep, to_twin(send)),) + rest
+
+    slabs = cubes_of(picked(video_clips, section))
+    slabs, up_cols, down_cols = call(
+        lambda where: None,
+        "begin",
+        (),
+        [],
+        [],
+        (),
+        1,
+        8,
+        (slabs, up_cols, down_cols),
+        (grown_own, recon_cot),
+    )
+    slabs = jnp.concatenate([slabs, cube_map(up_cols, up_weight), cube_map(down_cols, down_weight)])
+    slabs = lax.all_gather(slabs, "space", axis=0)
+    video = field_from(slabs[:, :cubes])
+    maps = slabs[:, cubes:]
+    (shares,) = with_twin(
+        *call(
+            partial(back_kernel, across, 1),
+            "dec_back_two",
+            (blocks_f, blocks_b),
+            [wide, rim_f, arrival],
+            [spec, hbm],
+            (recon_cot, dec_convs),
+        )
+    )
+    behind, _ = scatter_swap([shares])
+    shares, dec_act, dec_stats, dec_mine, decoded_in = with_twin(
+        *call(
+            partial(first_conv_kernel, (True, across, group, members, 2, 8, 0)),
+            "dec_conv_one",
+            (blocks_f, blocks_b, full, stats_f, piece_b, full),
+            [rim_b, patch, wide, product, arrival],
+            [spec, spec, spec, hbm],
+            (grown_own, grown_twin, table, dec_convs),
+        )
+    )
+    ahead, (maps,) = scatter_pieces(shares, (maps,))
+    maps = lax.all_gather(maps.reshape(spaces, 2, bits, -1), "section", axis=0)
+    enc_keep, enc_send, enc_act, enc_stats, enc_mine = call(
+        partial(first_conv_kernel, (False, across, group, members, 0, 4, 0)),
+        "enc_conv_one",
+        (blocks_f, blocks_b, full, stats_f, piece_b),
+        [rim_b, patch, wide, product, arrival],
+        [spec, spec, hbm],
+        (video, table, enc_convs),
+    )
+    dec_act_two, dec_inner, dec_sums_two, enc_send = call(
+        partial(mid_both_kernel, (group, members, 3, 9, 10, chips)),
+        "dec_mid",
+        (piece_b, piece_b, sums_f),
+        [],
+        [spec] * (chips + 2),
+        (*ahead, behind[:, 0], table),
+        1,
+        8,
+        (enc_send,),
+    )
+    inner_hops = z_hops(dec_inner)
+    enc_pieces, _ = scatter_swap([(enc_keep, to_twin(enc_send))])
+    enc_act_two, enc_kept, dec_inner = call(
+        partial(mid_ahead_kernel, (group, members, 1, 5, 6, 1)),
+        "enc_mid",
+        (piece_b, piece_f),
+        [],
+        [spec] * 2,
+        (enc_pieces[:, 0], table),
+        1,
+        8,
+        (dec_inner,),
+    )
+    inner_own, inner_twin = gather_stacks(dec_inner, inner_hops)
+    acts = jnp.broadcast_to(jnp.stack([dec_act_two, enc_act_two])[None], (chips, 2) + piece_b.shape)
+    acts = swap_chips(acts)
+    tiny_f = arr((rows + 2 * tiles, LANES), F32)
+    grad_shares, tiny, dec_inner_full = with_twin(
+        *call(
+            partial(back_whole_kernel, (across, group, members, 2, 8, bits, 0)),
+            "dec_back_one",
+            (cubes_f, cubes_b, tiny_f, full),
+            [
+                wide,
+                rim_f,
+                arrival,
+                pltpu.VMEM((tiles, cubes, rows, LANES), F32),
+                pltpu.VMEM((cubes, rows, channels), BF16),
+                pltpu.VMEM((8, channels), F32),
+            ],
+            [spec, spec, hbm, spec, spec, spec, spec, map_spec(0)],
+            (inner_own, inner_twin, dec_convs, decoded_in, dec_stats, table, recon_cot, maps),
+            mib=34,
+        )
+    )
+    for hop in z_hops(tiny):
+        tiny = tiny + hop
+    tiny = tiny + to_twin(tiny)
+    sign_grad = tiny[:rows, :bits].astype(BF16)
+
+    def kernel_grad_of(act, cot, name, held=(), after=()):
+        return call(
+            partial(grad_only_kernel, across),
+            name,
+            (grad_b,),
+            [rim_b, patch, grad_s],
+            [spec, spec],
+            (act, cot),
+            held=held,
+            after=after,
+        )
+
+    (dec_grad_one,) = kernel_grad_of(dec_act, dec_inner_full, "dec_grad_one")
+
+    def parts_of(grad):
+        parts = grad.reshape(sections, row_count // sections, channels)
+        parts = lax.all_to_all(parts, "section", 0, 0, tiled=True)
+        return jnp.sum(parts.astype(F32), axis=0).astype(BF16)
+
+    shares, enc_cot, cot_mine, acts, dec_grad_one = with_twin(
+        *call(
+            partial(back_signs_kernel, (across, bits, 1)),
+            "enc_back_two",
+            (blocks_f, blocks_b, full, piece_b),
+            [wide, rim_f, arrival],
+            [spec, map_spec(1), hbm],
+            (tiny, maps, enc_convs),
+            held=(acts, dec_grad_one),
+        )
+    )
+    acts_twin = to_twin(acts)
+    enc_pieces, (dec_grad_one,) = scatter_pieces(shares, (dec_grad_one,))
+    dec_one = parts_of(dec_grad_one)
+    recon_keep, recon_send, dec_grad_two, _ = call(
+        partial(second_conv_kernel, across, True, 1),
+        "dec_conv_two",
+        (blocks_f, blocks_b, grad_b, full),
+        [rim_b, patch, wide, product, arrival, grad_s],
+        [piece_spec(0), piece_spec(0), hbm, spec],
+        (acts, acts_twin, dec_convs, recon_cot),
+        mib=36,
+    )
+    enc_inner, enc_sums_two, recon_send, dec_grad_two = call(
+        partial(mid_back_kernel, (group, members, 1, 5, chips)),
+        "enc_mid_back",
+        (piece_b, sums_f),
+        [],
+        [spec] * (chips + 2),
+        (*enc_pieces, enc_kept, table),
+        1,
+        8,
+        (recon_send, dec_grad_two),
+    )
+    einner_hops = z_hops(enc_inner)
+
+    recon_shares = (recon_keep, to_twin(recon_send))
+    encoded_keep, encoded_send, enc_act_two_full, enc_inner, dec_grad_two, dec_one = call(
+        partial(second_conv_kernel, across, False, 1),
+        "enc_conv_two",
+        (cubes_f, cubes_b, full),
+        [rim_b, patch, wide, product, arrival],
+        [piece_spec(1), piece_spec(1), hbm],
+        (acts, acts_twin, enc_convs),
+        held=(enc_inner, dec_grad_two, dec_one),
+    )
+    dec_one = lax.all_gather(dec_one, "section", axis=0, tiled=True)
+    dec_two = parts_of(dec_grad_two)
+    einner_own, einner_twin = gather_stacks(enc_inner, einner_hops)
+    encoded_shares = (encoded_keep, to_twin(encoded_send))
+    shares, enc_inner_full = with_twin(
+        *call(
+            partial(back_stacked_kernel, across, 0),
+            "enc_back_one",
+            (blocks_f, blocks_b, full),
+            [wide, rim_f, arrival],
+            [spec, spec, hbm],
+            (einner_own, einner_twin, enc_convs),
+        )
+    )
+    enc_pieces, _ = scatter_pieces(shares)
+    (enc_grad_two,) = kernel_grad_of(enc_act_two_full, enc_cot, "enc_grad_two")
+    (enc_grad_one,) = kernel_grad_of(enc_act, enc_inner_full, "enc_grad_one")
+    video_back, enc_sums_one, enc_grad_one = call(
+        partial(last_back_kernel, (group, members, 0, 4, chips)),
+        "enc_last",
+        (piece_b, sums_f),
+        [],
+        [spec] * (chips + 4),
+        (*enc_pieces, enc_mine, cot_mine, enc_stats, table),
+        1,
+        8,
+        (enc_grad_one,),
+        (dec_two,),
+    )
+    dec_two = lax.all_gather(dec_two, "section", axis=0, tiled=True)
+    enc_two = lax.psum(enc_grad_two, "section")
+    swapped, _ = scatter_swap([grad_shares, recon_shares, encoded_shares])
+    totals = jnp.sum(swapped.astype(F32), axis=0)
+    own_bias = own_channels(table[11])
+    recon = totals[1] + jnp.concatenate([own_bias, own_bias]) + dec_mine.astype(F32)
+    pieces = jnp.stack([recon.astype(BF16), video_back])
+
+    def as_cubes(part):
+        split = part.reshape(own_cubes, tiles, rows, LANES).transpose(0, 2, 1, 3)
+        return split.reshape(own_cubes, rows, channels)
+
+    swaps = range(1, sections)
+
+    def section_swap(value, step):
+        return lax.ppermute(value, "section", [(i, i ^ step) for i in range(sections)])
+
+    def quarter_sum(grad):
+        size = row_count // sections
+
+        def part(step):
+            return lax.dynamic_slice_in_dim(grad, (section ^ step) * size, size, 0)
+
+        got = [section_swap(part(step), step) for step in swaps]
+        total = part(0).astype(F32)
+        for value in got:
+            total = total + value.astype(F32)
+        return total.astype(BF16)
+
+    def by_section(value):
+        every = jnp.stack([value] + [section_swap(value, step) for step in swaps])
+        every = every.reshape((sections // 2, 2) + value.shape)
+        every = jnp.where(section % 2 == 1, every[:, ::-1], every)
+        every = jnp.where(section // 2 == 1, every[::-1], every)
+        return every.reshape((sections,) + value.shape)
+
+    enc_one_sum = quarter_sum(enc_grad_one)
+    enc_one = by_section(enc_one_sum).reshape(row_count, channels)
+
+    own = lax.dynamic_slice_in_dim(video, space * own_cubes, own_cubes, 0).astype(F32)
+    encoded = as_cubes(totals[2]) + table[7] + own
+    decoded_grad = as_cubes(totals[0])
+    sign_wide = jnp.pad(sign_grad, ((0, 0), (0, channels - bits)))[None]
+    encoded, decoded_grad = encoded.astype(BF16), decoded_grad.astype(BF16)
+    both = jnp.concatenate([encoded, decoded_grad, sign_wide])
+
+    signs_own = lax.dynamic_slice_in_dim(signs, section * rows, rows, 0)
+    signs_own = jnp.concatenate([signs_own, jnp.ones((rows, 1), BF16)], axis=1)
+
+    def through(bit_rows, field, weight):
+        wave = jnp.einsum("rk,orc->koc", bit_rows, field, preferred_element_type=F32)
+        wave = wave.astype(BF16).reshape(wave.shape[0], -1)
+        return jnp.dot(wave, weight, preferred_element_type=F32)
+
+    projected = jnp.concatenate(
+        [through(sign_grad, encoded, down_weight), through(signs_own, decoded_grad, up_weight)]
+    )
+    both, projected, pieces = call(
+        lambda where: None,
+        "latent",
+        (),
+        [],
+        [],
+        (),
+        1,
+        8,
+        (both, projected, pieces),
+        (enc_one_sum,),
+    )
+    both = by_section(both)
+    recon_out, video_out = to_output(pieces)
+    for hop in z_hops(projected):
+        projected = projected + hop
+    projected = own_channels(projected + to_twin(projected))
+    sign_total = jnp.sum(sign_grad.astype(F32), axis=0)
+    biased = sign_total[:, None] * down_bias.astype(F32)[None]
+    projected = jnp.concatenate([projected[:bits] + biased, projected[bits:]])
+    sign_all = both[:, 2 * own_cubes, :, :bits].reshape(clips * rows, bits)
+
+    def latent_rows(part):
+        return part.transpose(0, 2, 1, 3).reshape(clips * rows, own_cubes * channels)
+
+    enc_rows = latent_rows(both[:, :own_cubes])
+    dec_rows = latent_rows(both[:, own_cubes : 2 * own_cubes])
+    inner_grad = jnp.dot(sign_all, down_cols, preferred_element_type=F32).astype(BF16)
+
+    def outer(left, right):
+        return lax.dot_general(left, right, (((0,), (0,)), ((), ())), preferred_element_type=F32)
+
+    down_weight_grad = outer(enc_rows, inner_grad)
+    up_weight_grad = outer(dec_rows, hidden)
+    upsample_grad = jnp.sum(dec_rows.astype(F32), axis=0)
+    down_bias_grad = jnp.sum(own_channels(inner_grad).astype(F32), axis=0)
+
+    def own_sum(field):
+        return own_channels(channel_sums(field.astype(F32)))[None]
+
+    dec_sums_one = own_channels(tiny[rows:].reshape(2, channels))
+    enc_sums_one, enc_sums_two, dec_sums_two = (
+        s[:, :lanes] for s in (enc_sums_one, enc_sums_two, dec_sums_two)
+    )
+    small_grads = jnp.concatenate(
+        [
+            enc_sums_one[1:],
+            enc_sums_two[1:],
+            enc_sums_one[:1],
+            enc_sums_two[:1],
+            own_sum(enc_inner_full),
+            own_sum(enc_cot),
+            dec_sums_one[1:],
+            dec_sums_two[1:],
+            dec_sums_one[:1],
+            dec_sums_two[:1],
+            own_sum(dec_inner_full),
+            own_sum(recon_cot),
+            projected,
+        ]
+    )
+    step = 1
+    while step < sections:
+        route = [(i, i ^ step) for i in range(sections)]
+        small_grads = small_grads + lax.ppermute(small_grads, "section", route)
+        step *= 2
+
+    return (
+        recon_out,
+        video_out,
+        jnp.stack([enc_one, enc_two]).astype(F32),
+        small_grads[0:2],
+        small_grads[2:6],
+        down_weight_grad,
+        down_bias_grad,
+        small_grads[12 : 12 + bits].T,
+        small_grads[12 + bits : 12 + 2 * bits].T,
+        small_grads[12 + 2 * bits],
+        up_weight_grad,
+        upsample_grad,
+        jnp.stack([dec_one, dec_two]).astype(F32),
+        small_grads[6:8],
+        small_grads[8:12],
+    )
+
+
+def general_body(
     video_clips,
     code_bits,
     recon_grad,
@@ -627,7 +1449,7 @@
     enc_w, dec_w = aligned(enc_convs), aligned(dec_convs)
     half_members = members
 
-    def ahead(inputs, weights, gains, shifts, by_cube):
+    def ahead(inputs, weights, gains, shifts):
         wide = inputs.astype(F32)
         flat_one, spread_one = normed(
             wide, channel_sums(wide), channel_sums(wide * wide), group, members
@@ -635,21 +1457,23 @@
         norm_one = flat_one * gains[0] + shifts[0]
         logistic = jax.nn.sigmoid(norm_one)
         act_one = (norm_one * logistic).astype(BF16)
-        middle = conv_scattered(act_one, weights[0], first, across) + own_lanes(shifts[2])
+        part, patch_one = conv_part(act_one, weights[0], first, across)
+        middle = scattered(to_blocks(part)) + own_lanes(shifts[2])
         sums = pair_summed(jnp.stack([channel_sums(middle), channel_sums(middle * middle)]))
         flat_two, spread_two = normed(middle, sums[0], sums[1], group, half_members)
         norm_two = flat_two * own_lanes(gains[1]) + own_lanes(shifts[1])
         act_two = (norm_two * jax.nn.sigmoid(norm_two)).astype(BF16)
         act_two = from_blocks(gathered(act_two))
-        branch = conv_scattered(act_two, weights[1], first, across, by_cube)
+        branch, patch_two = conv_part(act_two, weights[1], first, across)
         return (
             branch,
-            (flat_one, spread_one, norm_one, act_one),
-            (flat_two, spread_two, norm_two, act_two),
+            (flat_one, spread_one, norm_one, patch_one),
+            (flat_two, spread_two, norm_two, patch_two),
         )
 
-    def grads_two(raw, state, gains):
+    def grads_two(spread_back, state, gains):
         flat, spread, norm, _ = state
+        raw = scattered(to_blocks(spread_back))
         pre = raw * swish_slope(norm, jax.nn.sigmoid(norm))
         sums = pair_summed(jnp.stack([channel_sums(pre), channel_sums(pre * flat)]))
         gain = own_lanes(gains[1])
@@ -667,12 +1491,12 @@
         )
         return jnp.where(core == 0, placed, 0.0)
 
-    dec_branch, dec_one, dec_two = ahead(decoded_in, dec_w, d_gains, d_shifts, False)
+    dec_branch, dec_one, dec_two = ahead(decoded_in, dec_w, d_gains, d_shifts)
     dec_inner, dec_sums_two = grads_two(
-        convt_scattered(recon_cot, dec_w[1], first, across), dec_two, d_gains
+        convt_part(recon_cot, dec_w[1], first, across), dec_two, d_gains
     )
     dec_inner = from_blocks(gathered(dec_inner))
-    back = convt_whole(dec_inner, dec_w[0], first, across)
+    back = convt_part(dec_inner, dec_w[0], first, across)
     flat_one, spread_one, norm_one, _ = dec_one
     pre = back * swish_slope(norm_one, jax.nn.sigmoid(norm_one))
     dec_sums_one = jnp.stack([channel_sums(pre), channel_sums(pre * flat_one)])
@@ -690,12 +1514,12 @@
     enc_cot = jnp.einsum("rk,skoc->sorc", sign_grad, down_map, preferred_element_type=F32)
     enc_cot = enc_cot.astype(BF16).reshape(cubes, rows, channels)
 
-    enc_branch, enc_one, enc_two = ahead(video, enc_w, e_gains, e_shifts, True)
+    enc_branch, enc_one, enc_two = ahead(video, enc_w, e_gains, e_shifts)
     enc_inner, enc_sums_two = grads_two(
-        convt_scattered(enc_cot, enc_w[1], first, across), enc_two, e_gains
+        convt_part(enc_cot, enc_w[1], first, across), enc_two, e_gains
     )
     enc_inner = from_blocks(gathered(enc_inner))
-    back = convt_scattered(enc_inner, enc_w[0], first, across)
+    back = scattered(to_blocks(convt_part(enc_inner, enc_w[0], first, across)))
     flat, norm = own_block(enc_one[0]), own_block(enc_one[2])
     pre = back * swish_slope(norm, jax.nn.sigmoid(norm))
     enc_sums_one = pair_summed(jnp.stack([channel_sums(pre), channel_sums(pre * flat)]))
@@ -704,7 +1528,7 @@
     lined = group_means(enc_sums_one[1] * gain, group, members)
     video_back = own_lanes(enc_one[1]) * (pre * gain - total - flat * lined)
     video_back = (own_block(enc_cot).astype(F32) + video_back).astype(BF16)
-    recon = dec_branch + own_lanes(d_shifts[3])
+    recon = scattered(to_blocks(dec_branch)) + own_lanes(d_shifts[3])
     recon = (recon + own_block(decoded_in).astype(F32)).astype(BF16)
 
     def to_output(block):
@@ -716,18 +1540,21 @@
         parted = slab.reshape(frames, height, width, sections, channels // sections)
         return lax.all_to_all(parted.transpose(3, 0, 1, 2, 4), "section", 0, 0, tiled=True)
 
+    grads = [
+        kernel_grad(enc_one[3], enc_inner),
+        kernel_grad(enc_two[3], enc_cot),
+        kernel_grad(dec_one[3], dec_inner),
+        kernel_grad(dec_two[3], recon_cot),
+    ]
     row_count = enc_convs.shape[1]
     grads = [
-        lax.psum(kernel_grads(act, cot, first, offset, row_count, across), "section").astype(F32)
-        for act, cot in (
-            (enc_one[3], enc_inner),
-            (enc_two[3], enc_cot),
-            (dec_one[3], dec_inner),
-            (dec_two[3], recon_cot),
+        lax.psum(lax.dynamic_slice_in_dim(g, offset, row_count, 0).astype(BF16), "section").astype(
+            F32
         )
+        for g in grads
     ]
 
-    encoded = enc_branch
+    encoded = scattered(enc_branch.reshape(chips, 2, own_cubes, rows, channels))
     own = lambda v: lax.dynamic_slice_in_dim(v, space * own_cubes, own_cubes, 0).astype(F32)
     encoded = (encoded + e_shifts[3] + own(video)).astype(BF16)
     decoded_grad = scattered(grad_part.reshape(chips, 2, own_cubes, rows, channels)).astype(BF16)
@@ -801,8 +1628,9 @@
 def solution(mesh):
     lead, second, third = P("space"), P(None, "space"), P(None, None, "space")
     field = P(None, None, "space", None, "section")
+    short = mesh.shape["space"] == 8 and mesh.shape["section"] == 4
     return jax.shard_map(
-        body,
+        fast_body if short else general_body,
         mesh=mesh,
         in_specs=(
             third,

time: 586 us -> 462 us (0.79)
  blocking collectives: 48.8 us -> 0 us
  local copies, waits for them, and re-layouts: 95.4 us -> 56.1 us
  other arithmetic: 68 us -> 31.1 us
  Pallas kernels: 74.8 us -> 96.4 us
  starting transfers between devices: 105 us -> 93.1 us
    ppermute x0 -> x11, waiting for transfers between devices: none -> 44.6 us  [the longest x9 42.8 us: section_swap(): lax.ppermute(value, 'section', [(i, i ^ step) for i in range(sections)])]
    ppermute x51 -> x27, starting transfers between devices: 85.2 us -> 42.1 us  [along_chips(): return lax.ppermute(value, 'space', route)]
    psum x1 -> x0, blocking collectives: 40.5 us -> none  [body(): small_grads = lax.psum(small_grads, ('section', 'space'))]
    psum x1, waiting for transfers between devices: 36.5 us -> 0.01 us  [fast_body(): enc_two = lax.psum(enc_grad_two, 'section')]
    ppermute x51 -> x27, waiting for transfers between devices: 93.3 us -> 61.8 us  [along_chips(): return lax.ppermute(value, 'space', route)]
    another operation x27 -> x10, other arithmetic: 27.1 us -> 2.57 us  [the longest x2 1.37 us: by_section(): every = jnp.stack([value] + [section_swap(value, step) for step in swaps])]
    pallas_call x12 -> x24, Pallas kernels: 74.8 us -> 96.4 us  [call(): pl.pallas_call(ordered, grid=(1,), out_shape=(arr(where.shape, jnp.int32)...]
    all_to_all x4 -> x8, starting transfers between devices: 14.7 us -> 35.1 us  [the longest x4 17.8 us: swap_chips(): lax.all_to_all(value, 'space', 0, 0, axis_index_groups=line, tiled=True)]
  transfers between devices with their start and end apart: 80 -> 67, of which waited for: 26 -> 33; matrix products, arithmetic and copies ran while one was open for 29% -> 15% of each run, Pallas kernels for 13% -> 15%
where the time goes in v2:
time: 462 us; the launch traced here: 453 us
  waiting for transfers between devices  142 us (31%)
  Pallas kernels  96.4 us (21%)
  starting transfers between devices  93.1 us (20%)
  local copies, waits for them, and re-layouts  56.1 us (12%)
  other arithmetic  31.1 us (7%)
  matrix products  18.1 us (4%)
  between operations  16.2 us (4%)
    pallas_call x24, Pallas kernels, call(): pl.pallas_call(ordered, grid=(1,), out_shape=(arr(where.shape, jnp.int32)...  96.4 us
    ppermute x27, waiting for transfers between devices, along_chips(): return lax.ppermute(value, 'space', route)  61.8 us
    ppermute x9, waiting for transfers between devices, section_swap(): lax.ppermute(value, 'section', [(i, i ^ step) for i in range(sections)])  42.8 us
    ppermute x27, starting transfers between devices, along_chips(): return lax.ppermute(value, 'space', route)  42.1 us
    unnamed x140, local copies, waits for them, and re-layouts  24.5 us
    all_to_all x4, starting transfers between devices, swap_chips(): lax.all_to_all(value, 'space', 0, 0, axis_index_groups=line, tiled=True)  17.8 us
    all_to_all x2, waiting for transfers between devices, parts_of(): parts = lax.all_to_all(parts, 'section', 0, 0, tiled=True)  12.4 us
    ppermute x9, starting transfers between devices, section_swap(): lax.ppermute(value, 'section', [(i, i ^ step) for i in range(sections)])  10.5 us
  transfers between devices with their start and end apart: 67, of which 33 were waited for; matrix products, arithmetic and copies ran while one was open for 15% of the time, Pallas kernels for 15%

profile of v2, /device:TPU:0, one launch (start us, length us, event | category | flops | bytes accessed | tf_op | source)
XLA Modules:
  0.0 452.8 jit_solution(7480482869349015559)
XLA Ops:
  40.7 11.6 %collective-permute-done.5 = bf16[8,16,512]{2,1,0:T(8,128)(2,1)S(1)} collective-permute-done((bf16[8,16,512]{2,1,0:T(8,128)(2,1)S(1)}, bf16[8,16,512]{2,1,0:T(8,128)(2,1)S(1)}, u32[]{:S(2)}, u32[]{:S(2)}) %collective-permute-start.5) | collective-permute-done | bytes 131104 | tf_op jit(solution)/shard_map/ppermute | solution.py:28
  62.4 7.3 %dec_back_two.1 = (s32[4]{0:T(128)S(1)}, f32[4,32,16,128]{3,2,1,0:T(8,128)S(1)}, bf16[4,32,16,128]{3,2,1,0:T(8,128)(2,1)}) custom-call(s32[4]{0:T(128)S(1)} %get-tuple-element.116.refs_0_, bf16[64,16,512]{2,1,0:T(8,128)(2,1)S(1)} %copy.127.refs_5_.refs_1_.refs_7_.refs_4_, bf16[2,1728,512]{2,1,0:T(8,128)(2,1)} %refs_3_.9), custom_call_target="tpu_custom_call" | custom-call | flops 1879048192 | bytes 6291456 | tf_op jit(solution)/shard_map/dec_back_two/pallas_call | solution.py:898
  73.3 7.3 %dec_conv_one.1 = (s32[4]{0:T(128)S(1)}, f32[4,32,16,128]{3,2,1,0:T(8,128)S(1)}, bf16[4,32,16,128]{3,2,1,0:T(8,128)(2,1)S(1)}, bf16[64,16,512]{2,1,0:T(8,128)(2,...) custom-call(s32[4]{0:T(128)S(1)} %get-tuple-element.120.refs_0_, ...), custom_call_target="tpu_custom_call" | custom-call | flops 1879048192 | bytes 6291456 | tf_op jit(solution)/shard_map/dec_conv_one/pallas_call | solution.py:898
  104.8 7.2 %enc_conv_one.1 = (s32[4]{0:T(128)S(1)}, f32[4,32,16,128]{3,2,1,0:T(8,128)S(1)}, bf16[4,32,16,128]{3,2,1,0:T(8,128)(2,1)S(1)}, bf16[64,16,512]{2,1,0:T(8,128)(2,...) custom-call(s32[4]{0:T(128)S(1)} %get-tuple-element.127.refs_0_, ...), custom_call_target="tpu_custom_call" | custom-call | flops 1879048192 | bytes 6291456 | tf_op jit(solution)/shard_map/enc_conv_one/pallas_call | solution.py:898
  127.9 4.8 %all-to-all-start.1 = ((bf16[4,1,32,16,128]{4,3,2,1,0:T(8,128)(2,1)}), bf16[4,1,32,16,128]{4,3,2,1,0:T(8,128)(2,1)S(1)}, u32[]{:S(2)}, u32[]{:S(2)}) async-start(bf16[4,1,32,16,128]{4,3,2,1,0:T(8,128)(2,1)} %get-tuple-element.139), calls=%async_computation.1 | async-start | bytes 1048576 | tf_op jit(solution)/shard_map/all_to_all | solution.py:935
  137.7 7.6 %collective-permute-done.16 = bf16[32,16,128]{2,1,0:T(8,128)(2,1)S(1)} collective-permute-done((bf16[32,16,128]{2,1,0:T(8,128)(2,1)S(1)}, bf16[32,16,128]{2,1,0:T(8,128)(2,1)S(1)}, u32[]{:S(2)}, u32[]{:S(2)}) %collective-permute-start.16) | collective-permute-done | bytes 131104 | tf_op jit(solution)/shard_map/ppermute | solution.py:28
  145.3 13.4 %collective-permute-done.15 = bf16[32,16,128]{2,1,0:T(8,128)(2,1)S(1)} collective-permute-done((bf16[32,16,128]{2,1,0:T(8,128)(2,1)S(1)}, bf16[32,16,128]{2,1,0:T(8,128)(2,1)S(1)}, u32[]{:S(2)}, u32[]{:S(2)}) %collective-permute-start.15) | collective-permute-done | bytes 131104 | tf_op jit(solution)/shard_map/ppermute | solution.py:28
  172.5 11.3 %dec_back_one.1 = (s32[4]{0:T(128)S(1)}, f32[4,8,16,512]{3,2,1,0:T(8,128)S(1)}, bf16[4,8,16,512]{3,2,1,0:T(8,128)(2,1)}, f32[24,128]{1,0:T(8,128)S(1)}, bf16[64,16,512]{2,1,0:T(8,128)(2,1)S(1)}) custom-call(s32[4]{0:T(128)S(1)} %get-tuple-element.141.refs_0_, bf16[4,32,16,128]{3,2,1,0:T(8,128)(2,1)} %pad_maximum_fusion.3.refs_1_, ...), custom_call_target="tpu_custom_call" | custom-call | flops 1879048192 | bytes 6291456 | tf_op jit(solution)/shard_map/dec_back_one/pallas_call | solution.py:898
  199.5 7.3 %enc_back_two.1 = (s32[4]{0:T(128)S(1)}, f32[4,32,16,128]{3,2,1,0:T(8,128)S(1)}, bf16[4,32,16,128]{3,2,1,0:T(8,128)(2,1)S(1)}, bf16[64,16,512]{2,1,0:T(8,128)(2,...) custom-call(s32[4]{0:T(128)S(1)} %get-tuple-element.149.refs_0_, ...), custom_call_target="tpu_custom_call", output_to_operand_aliasing={{5}: (4, {}), {6}: (5, {})} | custom-call | flops 1879048192 | bytes 6291456 | tf_op jit(solution)/shard_map/enc_back_two/pallas_call | solution.py:898
  220.3 10.6 %dec_conv_two.1 = (s32[4]{0:T(128)S(1)}, f32[4,32,16,128]{3,2,1,0:T(8,128)S(1)}, bf16[4,32,16,128]{3,2,1,0:T(8,128)(2,1)}, bf16[1728,512]{1,0:T(8,128)(2,1)}, bf16[64,16,512]{2,1,0:T(8,128)(2,1)}) custom-call(s32[4]{0:T(128)S(1)} %get-tuple-element.158.refs_0_, bf16[4,2,32,16,128]{4,3,2,1,0:T(8,128)(2,1)} %get-tuple-element.159.refs_1_, ...), custom_call_target="tpu_custom_call" | custom-call | flops 1879048192 | bytes 6291456 | tf_op jit(solution)/shard_map/dec_conv_two/pallas_call | solution.py:898
  241.0 6.3 %collective-permute-done.28 = bf16[32,16,128]{2,1,0:T(8,128)(2,1)S(1)} collective-permute-done((bf16[32,16,128]{2,1,0:T(8,128)(2,1)S(1)}, bf16[32,16,128]{2,1,0:T(8,128)(2,1)S(1)}, u32[]{:S(2)}, u32[]{:S(2)}) %collective-permute-start.28) | collective-permute-done | bytes 131104 | tf_op jit(solution)/shard_map/ppermute | solution.py:28
  247.3 6.9 %enc_conv_two.1 = (s32[4]{0:T(128)S(1)}, f32[4,8,16,512]{3,2,1,0:T(8,128)S(1)}, bf16[4,8,16,512]{3,2,1,0:T(8,128)(2,1)}, bf16[64,16,512]{2,1,0:T(8,128)(2,1)S(1)...) custom-call(s32[4]{0:T(128)S(1)} %get-tuple-element.168.refs_0_, ...), custom_call_target="tpu_custom_call", output_to_operand_aliasing={{4}: (4, {}), {5}: (5, {}), {6}: (6, {})} | custom-call | flops 1879048192 | bytes 6291456 | tf_op jit(solution)/shard_map/enc_conv_two/pallas_call | solution.py:898
  256.3 6.7 %enc_back_one.1 = (s32[4]{0:T(128)S(1)}, f32[4,32,16,128]{3,2,1,0:T(8,128)S(1)}, bf16[4,32,16,128]{3,2,1,0:T(8,128)(2,1)S(1)}, bf16[64,16,512]{2,1,0:T(8,128)(2,1)S(1)}) custom-call(s32[4]{0:T(128)S(1)} %get-tuple-element.172.refs_0_, bf16[4,32,16,128]{3,2,1,0:T(8,128)(2,1)S(1)} %pad_maximum_fusion.4.refs_1_, ...), custom_call_target="tpu_custom_call" | custom-call | flops 1879048192 | bytes 6291456 | tf_op jit(solution)/shard_map/enc_back_one/pallas_call | solution.py:898
  266.4 4.7 %enc_grad_two.1 = (s32[4]{0:T(128)S(1)}, bf16[1728,512]{1,0:T(8,128)(2,1)}) custom-call(s32[4]{0:T(128)S(1)} %get-tuple-element.177.refs_0_, bf16[64,16,512]{2,1,0:T(8,128)(2,1)S(1)} %get-tuple-element.178.refs_1_, bf16[64,16,512]{2,1,0:T(8,128)(2,1)S(1)} %copy-done.20), custom_call_target="tpu_custom_call" | custom-call | flops 1879048192 | bytes 6291456 | tf_op jit(solution)/shard_map/enc_grad_two/pallas_call | solution.py:898
  283.6 5.8 %collective-permute-done.32.refs_2_ = bf16[32,16,128]{2,1,0:T(8,128)(2,1)S(1)} collective-permute-done((bf16[32,16,128]{2,1,0:T(8,128)(2,1)S(1)}, bf16[32,16,128]{2,1,0:T(8,128)(2,1)S(1)}, u32[]{:S(2)}, u32[]{:S(2)}) %collective-permute-start.32) | collective-permute-done | bytes 131104 | tf_op jit(solution)/shard_map/ppermute | solution.py:28
  295.5 11.9 %all-to-all-done.4 = bf16[4,432,512]{2,1,0:T(8,128)(2,1)} async-done(((bf16[4,432,512]{2,1,0:T(8,128)(2,1)}), bf16[4,432,512]{2,1,0:T(8,128)(2,1)}, u32[]{:S(2)}, u32[]{:S(2)}) %all-to-all-start.4) | async-done | bytes 1769504 | tf_op jit(solution)/shard_map/all_to_all | solution.py:1136
  320.0 4.7 %all-to-all-start.5 = ((bf16[4,3,32,16,128]{4,3,2,1,0:T(8,128)(2,1)}), bf16[4,3,32,16,128]{4,3,2,1,0:T(8,128)(2,1)}, u32[]{:S(2)}, u32[]{:S(2)}) async-start(bf16[4,3,32,16,128]{4,3,2,1,0:T(8,128)(2,1)} %copy-done.7), calls=%async_computation.5 | async-start | bytes 3145728 | tf_op jit(solution)/shard_map/all_to_all | solution.py:935
  333.7 10.5 %collective-permute-done.38 = bf16[432,512]{1,0:T(8,128)(2,1)S(1)} collective-permute-done((bf16[432,512]{1,0:T(8,128)(2,1)}, bf16[432,512]{1,0:T(8,128)(2,1)S(1)}, u32[]{:S(2)}, u32[]{:S(2)}) %collective-permute-start.38) | collective-permute-done | bytes 442400 | tf_op jit(solution)/shard_map/ppermute | solution.py:1229
  344.2 17.4 %collective-permute-done.40 = bf16[432,512]{1,0:T(8,128)(2,1)S(1)} collective-permute-done((bf16[432,512]{1,0:T(8,128)(2,1)}, bf16[432,512]{1,0:T(8,128)(2,1)S(1)}, u32[]{:S(2)}, u32[]{:S(2)}) %collective-permute-start.40) | collective-permute-done | bytes 442400 | tf_op jit(solution)/shard_map/ppermute | solution.py:1229
  379.4 9.1 %collective-permute-done.42 = bf16[432,512]{1,0:T(8,128)(2,1)S(1)} collective-permute-done((bf16[432,512]{1,0:T(8,128)(2,1)S(1)}, bf16[432,512]{1,0:T(8,128)(2,1)S(1)}, u32[]{:S(2)}, u32[]{:S(2)}) %collective-permute-start.42) | collective-permute-done | bytes 442400 | tf_op jit(solution)/shard_map/ppermute | solution.py:1229
  397.6 5.4 %maximum_convert_fusion = f32[2,1728,512]{2,1,0:T(8,128)} fusion(bf16[1,1728,512]{2,1,0:T(8,128)(2,1)} %all-reduce.6.cloned.1.call-done, bf16[1,1728,512]{2,1,0:T(8,128)(2,1)} %bitcast.203), kind=kLoop, calls=%fused_computation.2 | loop fusion | flops 3538944 | bytes 10616832 | tf_op jit(solution)/shard_map/convert_element_type | solution.py:1341
  414.1 5.1 %collective-permute-done.51 = bf16[17,16,512]{2,1,0:T(8,128)(2,1)S(1)} collective-permute-done((bf16[17,16,512]{2,1,0:T(8,128)(2,1)S(1)}, bf16[17,16,512]{2,1,0:T(8,128)(2,1)S(1)}, u32[]{:S(2)}, u32[]{:S(2)}) %collective-permute-start.51) | collective-permute-done | bytes 278560 | tf_op jit(solution)/shard_map/ppermute | solution.py:1229
  421.2 4.7 %fusion.33 = f32[4096,512]{1,0:T(8,128)} fusion(bf16[64,4096]{1,0:T(8,128)(2,1)S(1)} %bitcast.210, bf16[64,512]{1,0:T(8,128)(2,1)S(1)} %convolution_convert_fusion.2), kind=kOutput, calls=%fused_computation.105 | convolution fusion | flops 268435456 | bytes 8978432 | tf_op jit(solution)/shard_map/dot_general | solution.py:1301
  439.3 5.4 %maximum_convert_fusion.1 = f32[2,1728,512]{2,1,0:T(8,128)} fusion(bf16[1,1728,512]{2,1,0:T(8,128)(2,1)} %bitcast.215, bf16[1,1728,512]{2,1,0:T(8,128)(2,1)} %bitcast.214), kind=kLoop, calls=%fused_computation.3 | loop fusion | flops 3538944 | bytes 10616832 | tf_op jit(solution)/shard_map/convert_element_type | solution.py:1351
  (412 shorter events, 243.4 us)
Async XLA Ops:
  7.2 47.9 %all-gather.7.cloned.1.call-start = ((), (), s32[]{:S(2)}) async-start(), calls=%async_computation.8 | async-start | bytes 1179648 | tf_op jit(solution)/shard_map/all_gather | solution.py:1004
  23.8 63.4 %all-gather.15.cloned.1.call-start = ((), (), s32[]{:S(2)}) async-start(), calls=%async_computation.13 | async-start | bytes 1843200 | tf_op jit(solution)/shard_map/all_gather | solution.py:1035
  62.4 104.6 %all-gather.9.cloned.1.call-start = ((), (), s32[]{:S(2)}) async-start(), calls=%async_computation.9 | async-start | bytes 2949120 | tf_op jit(solution)/shard_map/all_gather | solution.py:1060
  92.6 25.4 %all-to-all-start = ((bf16[4,1,32,16,128]{4,3,2,1,0:T(8,128)(2,1)}), bf16[4,1,32,16,128]{4,3,2,1,0:T(8,128)(2,1)S(1)}, u32[]{:S(2)}, u32[]{:S(2)}) async-start(bf16[4,1,32,16,128]{4,3,2,1,0:T(8,128)(2,1)} %get-tuple-element.133), calls=%async_computation | async-start | bytes 1048576 | tf_op jit(solution)/shard_map/all_to_all | solution.py:935
  101.0 20.0 %collective-permute-start.11 = (bf16[32,16,128]{2,1,0:T(8,128)(2,1)}, bf16[32,16,128]{2,1,0:T(8,128)(2,1)}, u32[]{:S(2)}, u32[]{:S(2)}) collective-permute-start(bf16[32,16,128]{2,1,0:T(8,128)(2,1)} %get-tuple-element.131), channel_id=1, source_target_pairs={{0,4},{1,5},{2,6},{3,7},{4,0},{5,1},{6,2},{7,3},{8,12},{9,13},{10,... | collective-permute-start | bytes 393224 | tf_op jit(solution)/shard_map/ppermute | solution.py:28
  127.9 30.9 %all-to-all-start.1 = ((bf16[4,1,32,16,128]{4,3,2,1,0:T(8,128)(2,1)}), bf16[4,1,32,16,128]{4,3,2,1,0:T(8,128)(2,1)S(1)}, u32[]{:S(2)}, u32[]{:S(2)}) async-start(bf16[4,1,32,16,128]{4,3,2,1,0:T(8,128)(2,1)} %get-tuple-element.139), calls=%async_computation.1 | async-start | bytes 1048576 | tf_op jit(solution)/shard_map/all_to_all | solution.py:935
  136.5 22.2 %collective-permute-start.15 = (bf16[32,16,128]{2,1,0:T(8,128)(2,1)S(1)}, bf16[32,16,128]{2,1,0:T(8,128)(2,1)S(1)}, u32[]{:S(2)}, u32[]{:S(2)}) collective-permute-start(bf16[32,16,128]{2,1,0:T(8,128)(2,1)S(1)} %get-tuple-element.140.refs_3_), channel_id=1, source_target_pairs={{0,4},{1,5},{2,6},{3,7},{4,0},{5,1},{6,2},{7,3},{8,12},{9,13},{10,... | collective-permute-start | bytes 393224 | tf_op jit(solution)/shard_map/ppermute | solution.py:28
  136.5 22.2 %collective-permute-start.14 = (bf16[32,16,128]{2,1,0:T(8,128)(2,1)S(1)}, bf16[32,16,128]{2,1,0:T(8,128)(2,1)S(1)}, u32[]{:S(2)}, u32[]{:S(2)}) collective-permute-start(bf16[32,16,128]{2,1,0:T(8,128)(2,1)S(1)} %get-tuple-element.140.refs_3_), channel_id=1, source_target_pairs={{0,2},{1,3},{2,4},{3,5},{4,6},{5,7},{6,0},{7,1},{8,10},{9,11},{10,... | collective-permute-start | bytes 393224 | tf_op jit(solution)/shard_map/ppermute | solution.py:28
  161.8 36.3 %all-to-all-start.2 = ((bf16[4,2,32,16,128]{4,3,2,1,0:T(8,128)(2,1)}), bf16[4,2,32,16,128]{4,3,2,1,0:T(8,128)(2,1)}, u32[]{:S(2)}, u32[]{:S(2)}) async-start(bf16[4,2,32,16,128]{4,3,2,1,0:T(8,128)(2,1)} %broadcast_in_dim.33), calls=%async_computation.2 | async-start | bytes 2097152 | tf_op jit(solution)/shard_map/all_to_all | solution.py:935
  211.6 26.8 %all-to-all-start.3 = ((bf16[4,432,512]{2,1,0:T(8,128)(2,1)}), bf16[4,432,512]{2,1,0:T(8,128)(2,1)}, u32[]{:S(2)}, u32[]{:S(2)}) async-start(bf16[4,432,512]{2,1,0:T(8,128)(2,1)} %bitcast.187), calls=%async_computation.3 | async-start | bytes 3538944 | tf_op jit(solution)/shard_map/all_to_all | solution.py:1136
  216.1 181.5 %all-reduce.6.cloned.1.call-start = ((), (), s32[]{:S(2)}) async-start(), calls=%async_computation.10 | async-start | bytes 3538944 | tf_op jit(solution)/shard_map/psum | solution.py:1215
  271.8 35.7 %all-to-all-start.4 = ((bf16[4,432,512]{2,1,0:T(8,128)(2,1)}), bf16[4,432,512]{2,1,0:T(8,128)(2,1)}, u32[]{:S(2)}, u32[]{:S(2)}) async-start(bf16[4,432,512]{2,1,0:T(8,128)(2,1)} %bitcast.48), calls=%async_computation.4 | async-start | bytes 3538944 | tf_op jit(solution)/shard_map/all_to_all | solution.py:1136
  276.3 161.3 %all-gather.11.cloned.1.call-start = ((), (), s32[]{:S(2)}) async-start(), calls=%async_computation.11 | async-start | bytes 2211840 | tf_op jit(solution)/shard_map/all_gather | solution.py:1185
  279.6 33.7 %collective-permute-start.35 = (bf16[4,8,16,512]{3,2,1,0:T(8,128)(2,1)}, bf16[4,8,16,512]{3,2,1,0:T(8,128)(2,1)S(1)}, u32[]{:S(2)}, u32[]{:S(2)}) collective-permute-start(bf16[4,8,16,512]{3,2,1,0:T(8,128)(2,1)} %get-tuple-element.195), channel_id=1, source_target_pairs={{0,1},{1,0},{2,3},{3,2},{4,5},{5,4},{6,7},{7,6},{8,9},{9,8},{10,11... | collective-permute-start | bytes 1572872 | tf_op jit(solution)/shard_map/ppermute | solution.py:32
  279.8 33.5 %collective-permute-start.36 = (bf16[4,32,16,128]{3,2,1,0:T(8,128)(2,1)}, bf16[4,32,16,128]{3,2,1,0:T(8,128)(2,1)}, u32[]{:S(2)}, u32[]{:S(2)}) collective-permute-start(bf16[4,32,16,128]{3,2,1,0:T(8,128)(2,1)} %get-tuple-element.197), channel_id=1, source_target_pairs={{0,1},{1,0},{2,3},{3,2},{4,5},{5,4},{6,7},{7,6},{8,9},{9,8},{10,11... | collective-permute-start | bytes 1572872 | tf_op jit(solution)/shard_map/ppermute | solution.py:32
  280.1 33.2 %collective-permute-start.37 = (bf16[4,8,16,512]{3,2,1,0:T(8,128)(2,1)}, bf16[4,8,16,512]{3,2,1,0:T(8,128)(2,1)}, u32[]{:S(2)}, u32[]{:S(2)}) collective-permute-start(bf16[4,8,16,512]{3,2,1,0:T(8,128)(2,1)} %get-tuple-element.199), channel_id=1, source_target_pairs={{0,1},{1,0},{2,3},{3,2},{4,5},{5,4},{6,7},{7,6},{8,9},{9,8},{10,11... | collective-permute-start | bytes 1572872 | tf_op jit(solution)/shard_map/ppermute | solution.py:32
  281.7 27.8 %collective-permute-start.33 = (bf16[32,16,128]{2,1,0:T(8,128)(2,1)}, bf16[32,16,128]{2,1,0:T(8,128)(2,1)}, u32[]{:S(2)}, u32[]{:S(2)}) collective-permute-start(bf16[32,16,128]{2,1,0:T(8,128)(2,1)} %get-tuple-element.186), channel_id=1, source_target_pairs={{0,4},{1,5},{2,6},{3,7},{4,0},{5,1},{6,2},{7,3},{8,12},{9,13},{10,... | collective-permute-start | bytes 393224 | tf_op jit(solution)/shard_map/ppermute | solution.py:28
  320.0 46.4 %all-to-all-start.5 = ((bf16[4,3,32,16,128]{4,3,2,1,0:T(8,128)(2,1)}), bf16[4,3,32,16,128]{4,3,2,1,0:T(8,128)(2,1)}, u32[]{:S(2)}, u32[]{:S(2)}) async-start(bf16[4,3,32,16,128]{4,3,2,1,0:T(8,128)(2,1)} %copy-done.7), calls=%async_computation.5 | async-start | bytes 3145728 | tf_op jit(solution)/shard_map/all_to_all | solution.py:935
  324.7 114.6 %all-gather.13.cloned.1.call-start = ((), (), s32[]{:S(2)}) async-start(), calls=%async_computation.12 | async-start | bytes 2211840 | tf_op jit(solution)/shard_map/all_gather | solution.py:1214
  330.3 31.3 %collective-permute-start.40 = (bf16[432,512]{1,0:T(8,128)(2,1)}, bf16[432,512]{1,0:T(8,128)(2,1)S(1)}, u32[]{:S(2)}, u32[]{:S(2)}) collective-permute-start(bf16[432,512]{1,0:T(8,128)(2,1)} %get-tuple-element.246), channel_id=1, source_target_pairs={{0,24},{8,16},{16,8},{24,0},{1,25},{9,17},{17,9},{25,1},{2,26},{10... | collective-permute-start | bytes 1327112 | tf_op jit(solution)/shard_map/ppermute | solution.py:1229
  331.7 29.9 %collective-permute-start.39 = (bf16[432,512]{1,0:T(8,128)(2,1)S(1)}, bf16[432,512]{1,0:T(8,128)(2,1)}, u32[]{:S(2)}, u32[]{:S(2)}) collective-permute-start(bf16[432,512]{1,0:T(8,128)(2,1)S(1)} %get-tuple-element.247), channel_id=1, source_target_pairs={{0,16},{8,24},{16,0},{24,8},{1,17},{9,25},{17,1},{25,9},{2,18},{10... | collective-permute-start | bytes 1327112 | tf_op jit(solution)/shard_map/ppermute | solution.py:1229
  363.3 25.2 %collective-permute-start.42 = (bf16[432,512]{1,0:T(8,128)(2,1)S(1)}, bf16[432,512]{1,0:T(8,128)(2,1)S(1)}, u32[]{:S(2)}, u32[]{:S(2)}) collective-permute-start(bf16[432,512]{1,0:T(8,128)(2,1)S(1)} %add_convert_fusion.refs_4_), channel_id=1, source_target_pairs={{0,16},{8,24},{16,0},{24,8},{1,17},{9,25},{17,1},{25,9},{2,18},{10... | collective-permute-start | bytes 1327112 | tf_op jit(solution)/shard_map/ppermute | solution.py:1229
  365.0 23.4 %collective-permute-start.41 = (bf16[432,512]{1,0:T(8,128)(2,1)S(1)}, bf16[432,512]{1,0:T(8,128)(2,1)}, u32[]{:S(2)}, u32[]{:S(2)}) collective-permute-start(bf16[432,512]{1,0:T(8,128)(2,1)S(1)} %add_convert_fusion.refs_4_), channel_id=1, source_target_pairs={{0,8},{8,0},{16,24},{24,16},{1,9},{9,1},{17,25},{25,17},{2,10},{10... | collective-permute-start | bytes 1327112 | tf_op jit(solution)/shard_map/ppermute | solution.py:1229
  407.3 24.7 %all-to-all-start.6 = ((bf16[8,2,32,2,128]{4,2,3,1,0:T(8,128)(2,1)}), bf16[8,2,32,2,128]{4,2,3,1,0:T(8,128)(2,1)S(1)}, u32[]{:S(2)}, u32[]{:S(2)}) async-start(bf16[8,2,32,2,128]{4,2,3,1,0:T(8,128)(2,1)} %bitcast.183), calls=%async_computation.6 | async-start | bytes 524288 | tf_op jit(solution)/shard_map/all_to_all | solution.py:964
  (109 other events, 749.0 us)
Sparse Core Ops, SparseCore 0:
  23.9 31.1 all-gather.6
  62.5 24.6 all-gather.14
  92.7 37.0 all-gather.8
  271.9 92.0 all-reduce.5
  365.7 37.8 all-gather.10
  405.2 34.0 all-gather.12

commit v3 on v2

--- a/solution.py
+++ b/solution.py
@@ -1056,8 +1056,7 @@
             (grown_own, grown_twin, table, dec_convs),
         )
     )
-    ahead, (maps,) = scatter_pieces(shares, (maps,))
-    maps = lax.all_gather(maps.reshape(spaces, 2, bits, -1), "section", axis=0)
+    ahead, _ = scatter_pieces(shares)
     enc_keep, enc_send, enc_act, enc_stats, enc_mine = call(
         partial(first_conv_kernel, (False, across, group, members, 0, 4, 0)),
         "enc_conv_one",
@@ -1066,7 +1065,7 @@
         [spec, spec, hbm],
         (video, table, enc_convs),
     )
-    dec_act_two, dec_inner, dec_sums_two, enc_send = call(
+    dec_act_two, dec_inner, dec_sums_two, enc_send, maps = call(
         partial(mid_both_kernel, (group, members, 3, 9, 10, chips)),
         "dec_mid",
         (piece_b, piece_b, sums_f),
@@ -1075,8 +1074,9 @@
         (*ahead, behind[:, 0], table),
         1,
         8,
-        (enc_send,),
-    )
+        (enc_send, maps),
+    )
+    maps = lax.all_gather(maps.reshape(spaces, 2, bits, -1), "section", axis=0)
     inner_hops = z_hops(dec_inner)
     enc_pieces, _ = scatter_swap([(enc_keep, to_twin(enc_send))])
     enc_act_two, enc_kept, dec_inner = call(
@@ -1199,7 +1199,7 @@
     enc_pieces, _ = scatter_pieces(shares)
     (enc_grad_two,) = kernel_grad_of(enc_act_two_full, enc_cot, "enc_grad_two")
     (enc_grad_one,) = kernel_grad_of(enc_act, enc_inner_full, "enc_grad_one")
-    video_back, enc_sums_one, enc_grad_one = call(
+    video_back, enc_sums_one, enc_grad_one, enc_grad_two = call(
         partial(last_back_kernel, (group, members, 0, 4, chips)),
         "enc_last",
         (piece_b, sums_f),
@@ -1208,11 +1208,10 @@
         (*enc_pieces, enc_mine, cot_mine, enc_stats, table),
         1,
         8,
-        (enc_grad_one,),
+        (enc_grad_one, enc_grad_two),
         (dec_two,),
     )
     dec_two = lax.all_gather(dec_two, "section", axis=0, tiled=True)
-    enc_two = lax.psum(enc_grad_two, "section")
     swapped, _ = scatter_swap([grad_shares, recon_shares, encoded_shares])
     totals = jnp.sum(swapped.astype(F32), axis=0)
     own_bias = own_channels(table[11])
@@ -1248,7 +1247,7 @@
         return every.reshape((sections,) + value.shape)
 
     enc_one_sum = quarter_sum(enc_grad_one)
-    enc_one = by_section(enc_one_sum).reshape(row_count, channels)
+    enc_two = lax.all_gather(parts_of(enc_grad_two), "section", axis=0, tiled=True)
 
     own = lax.dynamic_slice_in_dim(video, space * own_cubes, own_cubes, 0).astype(F32)
     encoded = as_cubes(totals[2]) + table[7] + own
@@ -1268,7 +1267,7 @@
     projected = jnp.concatenate(
         [through(sign_grad, encoded, down_weight), through(signs_own, decoded_grad, up_weight)]
     )
-    both, projected, pieces = call(
+    both, projected, pieces, enc_one_sum = call(
         lambda where: None,
         "latent",
         (),
@@ -1277,9 +1276,9 @@
         (),
         1,
         8,
-        (both, projected, pieces),
-        (enc_one_sum,),
-    )
+        (both, projected, pieces, enc_one_sum),
+    )
+    enc_one = by_section(enc_one_sum).reshape(row_count, channels)
     both = by_section(both)
     recon_out, video_out = to_output(pieces)
     for hop in z_hops(projected):

time: 462 us -> 447 us (0.968)
  waiting for transfers between devices: 142 us -> 120 us
    all_to_all x2 -> x3, waiting for transfers between devices: 12.4 us -> 0.12 us  [parts_of(): parts = lax.all_to_all(parts, 'section', 0, 0, tiled=True)]
    ppermute x9, waiting for transfers between devices: 42.8 us -> 32 us  [section_swap(): lax.ppermute(value, 'section', [(i, i ^ step) for i in range(sections)])]
    ppermute x2, waiting for transfers between devices: 1.79 us -> 7.82 us  [fast_body(): small_grads = small_grads + lax.ppermute(small_grads, 'section', route)]
    all_to_all x1, waiting for transfers between devices: 0.01 us -> 5.07 us  [to_output(): lax.all_to_all(slab.transpose(4, 0, 1, 2, 3, 5), 'section', 0, 0, tiled=T...]
    all_to_all x2 -> x3, starting transfers between devices: 9.11 us -> 12.9 us  [parts_of(): parts = lax.all_to_all(parts, 'section', 0, 0, tiled=True)]
    unnamed x140 -> x130, local copies, waits for them, and re-layouts: 24.5 us -> 24.7 us
  transfers between devices with their start and end apart: 67 -> 68, of which waited for: 33 -> 29; matrix products, arithmetic and copies ran while one was open for 15% -> 15% of each run, Pallas kernels for 15% -> 18%
where the time goes in v3:
time: 447 us; the launch traced here: 438 us
  waiting for transfers between devices  120 us (27%)
  Pallas kernels  97.3 us (22%)
  starting transfers between devices  96.3 us (22%)
  local copies, waits for them, and re-layouts  58.2 us (13%)
  other arithmetic  32.3 us (7%)
  matrix products  18.1 us (4%)
  between operations  16 us (4%)
    pallas_call x24, Pallas kernels, call(): pl.pallas_call(ordered, grid=(1,), out_shape=(arr(where.shape, jnp.int32)...  97.3 us
    ppermute x27, waiting for transfers between devices, along_chips(): return lax.ppermute(value, 'space', route)  61.4 us
    ppermute x27, starting transfers between devices, along_chips(): return lax.ppermute(value, 'space', route)  40.9 us
    ppermute x9, waiting for transfers between devices, section_swap(): lax.ppermute(value, 'section', [(i, i ^ step) for i in range(sections)])  32 us
    unnamed x130, local copies, waits for them, and re-layouts  24.7 us
    all_to_all x4, starting transfers between devices, swap_chips(): lax.all_to_all(value, 'space', 0, 0, axis_index_groups=line, tiled=True)  16.8 us
    all_to_all x3, starting transfers between devices, parts_of(): parts = lax.all_to_all(parts, 'section', 0, 0, tiled=True)  12.9 us
    ppermute x9, starting transfers between devices, section_swap(): lax.ppermute(value, 'section', [(i, i ^ step) for i in range(sections)])  10.5 us
  transfers between devices with their start and end apart: 68, of which 29 were waited for; matrix products, arithmetic and copies ran while one was open for 15% of the time, Pallas kernels for 18%

profile of v3, /device:TPU:0, one launch (start us, length us, event | category | flops | bytes accessed | tf_op | source)
XLA Modules:
  0.0 437.8 jit_solution(11067342843652409449)
XLA Ops:
  40.7 11.6 %collective-permute-done.5 = bf16[8,16,512]{2,1,0:T(8,128)(2,1)S(1)} collective-permute-done((bf16[8,16,512]{2,1,0:T(8,128)(2,1)S(1)}, bf16[8,16,512]{2,1,0:T(8,128)(2,1)S(1)}, u32[]{:S(2)}, u32[]{:S(2)}) %collective-permute-start.5) | collective-permute-done | bytes 131104 | tf_op jit(solution)/shard_map/ppermute | solution.py:28
  62.4 7.3 %dec_back_two.1 = (s32[4]{0:T(128)S(1)}, f32[4,32,16,128]{3,2,1,0:T(8,128)S(1)}, bf16[4,32,16,128]{3,2,1,0:T(8,128)(2,1)}) custom-call(s32[4]{0:T(128)S(1)} %get-tuple-element.118.refs_0_, bf16[64,16,512]{2,1,0:T(8,128)(2,1)S(1)} %copy.129.refs_5_.refs_1_.refs_7_.refs_4_, bf16[2,1728,512]{2,1,0:T(8,128)(2,1)} %refs_3_.9), custom_call_target="tpu_custom_call" | custom-call | flops 1879048192 | bytes 6291456 | tf_op jit(solution)/shard_map/dec_back_two/pallas_call | solution.py:898
  73.3 7.8 %dec_conv_one.1 = (s32[4]{0:T(128)S(1)}, f32[4,32,16,128]{3,2,1,0:T(8,128)S(1)}, bf16[4,32,16,128]{3,2,1,0:T(8,128)(2,1)S(1)}, bf16[64,16,512]{2,1,0:T(8,128)(2,...) custom-call(s32[4]{0:T(128)S(1)} %get-tuple-element.122.refs_0_, ...), custom_call_target="tpu_custom_call" | custom-call | flops 1879048192 | bytes 6291456 | tf_op jit(solution)/shard_map/dec_conv_one/pallas_call | solution.py:898
  102.1 7.2 %enc_conv_one.1 = (s32[4]{0:T(128)S(1)}, f32[4,32,16,128]{3,2,1,0:T(8,128)S(1)}, bf16[4,32,16,128]{3,2,1,0:T(8,128)(2,1)S(1)}, bf16[64,16,512]{2,1,0:T(8,128)(2,...) custom-call(s32[4]{0:T(128)S(1)} %get-tuple-element.126.refs_0_, ...), custom_call_target="tpu_custom_call" | custom-call | flops 1879048192 | bytes 6291456 | tf_op jit(solution)/shard_map/enc_conv_one/pallas_call | solution.py:898
  131.5 7.6 %collective-permute-done.16 = bf16[32,16,128]{2,1,0:T(8,128)(2,1)S(1)} collective-permute-done((bf16[32,16,128]{2,1,0:T(8,128)(2,1)S(1)}, bf16[32,16,128]{2,1,0:T(8,128)(2,1)S(1)}, u32[]{:S(2)}, u32[]{:S(2)}) %collective-permute-start.16) | collective-permute-done | bytes 131104 | tf_op jit(solution)/shard_map/ppermute | solution.py:28
  139.1 13.4 %collective-permute-done.15 = bf16[32,16,128]{2,1,0:T(8,128)(2,1)S(1)} collective-permute-done((bf16[32,16,128]{2,1,0:T(8,128)(2,1)S(1)}, bf16[32,16,128]{2,1,0:T(8,128)(2,1)S(1)}, u32[]{:S(2)}, u32[]{:S(2)}) %collective-permute-start.15) | collective-permute-done | bytes 131104 | tf_op jit(solution)/shard_map/ppermute | solution.py:28
  165.6 11.1 %dec_back_one.1 = (s32[4]{0:T(128)S(1)}, f32[4,8,16,512]{3,2,1,0:T(8,128)S(1)}, bf16[4,8,16,512]{3,2,1,0:T(8,128)(2,1)S(1)}, f32[24,128]{1,0:T(8,128)S(1)}, bf16[64,16,512]{2,1,0:T(8,128)(2,1)S(1)}) custom-call(s32[4]{0:T(128)S(1)} %get-tuple-element.143.refs_0_, bf16[4,32,16,128]{3,2,1,0:T(8,128)(2,1)} %pad_maximum_fusion.3.refs_1_, ...), custom_call_target="tpu_custom_call" | custom-call | flops 1879048192 | bytes 6291456 | tf_op jit(solution)/shard_map/dec_back_one/pallas_call | solution.py:898
  192.4 7.3 %enc_back_two.1 = (s32[4]{0:T(128)S(1)}, f32[4,32,16,128]{3,2,1,0:T(8,128)S(1)}, bf16[4,32,16,128]{3,2,1,0:T(8,128)(2,1)S(1)}, bf16[64,16,512]{2,1,0:T(8,128)(2,...) custom-call(s32[4]{0:T(128)S(1)} %get-tuple-element.151.refs_0_, ...), custom_call_target="tpu_custom_call", output_to_operand_aliasing={{5}: (4, {}), {6}: (5, {})} | custom-call | flops 1879048192 | bytes 6291456 | tf_op jit(solution)/shard_map/enc_back_two/pallas_call | solution.py:898
  213.1 10.2 %dec_conv_two.1 = (s32[4]{0:T(128)S(1)}, f32[4,32,16,128]{3,2,1,0:T(8,128)S(1)}, bf16[4,32,16,128]{3,2,1,0:T(8,128)(2,1)S(1)}, bf16[1728,512]{1,0:T(8,128)(2,1)}, bf16[64,16,512]{2,1,0:T(8,128)(2,1)}) custom-call(s32[4]{0:T(128)S(1)} %get-tuple-element.160.refs_0_, bf16[4,2,32,16,128]{4,3,2,1,0:T(8,128)(2,1)} %get-tuple-element.161.refs_1_, ...), custom_call_target="tpu_custom_call" | custom-call | flops 1879048192 | bytes 6291456 | tf_op jit(solution)/shard_map/dec_conv_two/pallas_call | solution.py:898
  233.8 6.7 %collective-permute-done.28 = bf16[32,16,128]{2,1,0:T(8,128)(2,1)S(1)} collective-permute-done((bf16[32,16,128]{2,1,0:T(8,128)(2,1)S(1)}, bf16[32,16,128]{2,1,0:T(8,128)(2,1)S(1)}, u32[]{:S(2)}, u32[]{:S(2)}) %collective-permute-start.28) | collective-permute-done | bytes 131104 | tf_op jit(solution)/shard_map/ppermute | solution.py:28
  240.5 6.7 %enc_conv_two.1 = (s32[4]{0:T(128)S(1)}, f32[4,8,16,512]{3,2,1,0:T(8,128)S(1)}, bf16[4,8,16,512]{3,2,1,0:T(8,128)(2,1)S(1)}, bf16[64,16,512]{2,1,0:T(8,128)(2,1)...) custom-call(s32[4]{0:T(128)S(1)} %get-tuple-element.170.refs_0_, ...), custom_call_target="tpu_custom_call", output_to_operand_aliasing={{4}: (4, {}), {5}: (5, {}), {6}: (6, {})} | custom-call | flops 1879048192 | bytes 6291456 | tf_op jit(solution)/shard_map/enc_conv_two/pallas_call | solution.py:898
  256.3 7.3 %enc_back_one.1 = (s32[4]{0:T(128)S(1)}, f32[4,32,16,128]{3,2,1,0:T(8,128)S(1)}, bf16[4,32,16,128]{3,2,1,0:T(8,128)(2,1)}, bf16[64,16,512]{2,1,0:T(8,128)(2,1)S(1)}) custom-call(s32[4]{0:T(128)S(1)} %get-tuple-element.174.refs_0_, bf16[4,32,16,128]{3,2,1,0:T(8,128)(2,1)S(1)} %pad_maximum_fusion.4.refs_1_, bf16[4,32,16,128]{3,2,1,0:T(8,128)(2,1)S(1)} %copy-done.42, ...), custom_call_target="tpu_custom_call" | custom-call | flops 1879048192 | bytes 6291456 | tf_op jit(solution)/shard_map/enc_back_one/pallas_call | solution.py:898
  274.1 4.8 %enc_grad_two.1 = (s32[4]{0:T(128)S(1)}, bf16[1728,512]{1,0:T(8,128)(2,1)}) custom-call(s32[4]{0:T(128)S(1)} %get-tuple-element.179.refs_0_, bf16[64,16,512]{2,1,0:T(8,128)(2,1)S(1)} %copy-done.38, bf16[64,16,512]{2,1,0:T(8,128)(2,1)S(1)} %copy-done.19), custom_call_target="tpu_custom_call" | custom-call | flops 1879048192 | bytes 6291456 | tf_op jit(solution)/shard_map/enc_grad_two/pallas_call | solution.py:898
  292.3 4.8 %all-to-all-start.5 = ((bf16[4,3,32,16,128]{4,3,2,1,0:T(8,128)(2,1)}), bf16[4,3,32,16,128]{4,3,2,1,0:T(8,128)(2,1)}, u32[]{:S(2)}, u32[]{:S(2)}) async-start(bf16[4,3,32,16,128]{4,3,2,1,0:T(8,128)(2,1)} %get-tuple-element.204), calls=%async_computation.5 | async-start | bytes 3145728 | tf_op jit(solution)/shard_map/all_to_all | solution.py:935
  304.7 9.5 %collective-permute-done.38 = bf16[432,512]{1,0:T(8,128)(2,1)S(1)} collective-permute-done((bf16[432,512]{1,0:T(8,128)(2,1)}, bf16[432,512]{1,0:T(8,128)(2,1)S(1)}, u32[]{:S(2)}, u32[]{:S(2)}) %collective-permute-start.38) | collective-permute-done | bytes 442400 | tf_op jit(solution)/shard_map/ppermute | solution.py:1228
  314.2 14.2 %collective-permute-done.40 = bf16[432,512]{1,0:T(8,128)(2,1)S(1)} collective-permute-done((bf16[432,512]{1,0:T(8,128)(2,1)}, bf16[432,512]{1,0:T(8,128)(2,1)S(1)}, u32[]{:S(2)}, u32[]{:S(2)}) %collective-permute-start.40) | collective-permute-done | bytes 442400 | tf_op jit(solution)/shard_map/ppermute | solution.py:1228
  358.9 7.8 %collective-permute-done.48 = f32[49,64]{1,0:T(8,128)S(1)} collective-permute-done((f32[49,64]{1,0:T(8,128)S(1)}, f32[49,64]{1,0:T(8,128)S(1)}, u32[]{:S(2)}, u32[]{:S(2)}) %collective-permute-start.48) | collective-permute-done | bytes 12576 | tf_op jit(solution)/shard_map/ppermute | solution.py:1334
  373.7 4.6 %all-to-all-start.6 = ((bf16[8,2,32,2,128]{4,2,3,1,0:T(8,128)(2,1)}), bf16[8,2,32,2,128]{4,2,3,1,0:T(8,128)(2,1)S(1)}, u32[]{:S(2)}, u32[]{:S(2)}) async-start(bf16[8,2,32,2,128]{4,2,3,1,0:T(8,128)(2,1)} %bitcast.184), calls=%async_computation.6 | async-start | bytes 524288 | tf_op jit(solution)/shard_map/all_to_all | solution.py:964
  384.1 6.4 %collective-permute-done.51 = bf16[17,16,512]{2,1,0:T(8,128)(2,1)S(1)} collective-permute-done((bf16[17,16,512]{2,1,0:T(8,128)(2,1)S(1)}, bf16[17,16,512]{2,1,0:T(8,128)(2,1)S(1)}, u32[]{:S(2)}, u32[]{:S(2)}) %collective-permute-start.51) | collective-permute-done | bytes 278560 | tf_op jit(solution)/shard_map/ppermute | solution.py:1228
  392.7 4.7 %fusion.34 = f32[4096,512]{1,0:T(8,128)} fusion(bf16[64,4096]{1,0:T(8,128)(2,1)S(1)} %bitcast.210, bf16[64,512]{1,0:T(8,128)(2,1)S(1)} %copy-done.51), kind=kOutput, calls=%fused_computation.106 | convolution fusion | flops 268435456 | bytes 8978432 | tf_op jit(solution)/shard_map/dot_general | solution.py:1300
  397.4 4.7 %fusion.33 = f32[4096,512]{1,0:T(8,128)} fusion(bf16[64,4096]{1,0:T(8,128)(2,1)S(1)} %bitcast.211, bf16[64,512]{1,0:T(8,128)(2,1)S(1)} %convolution_convert_fusion.2), kind=kOutput, calls=%fused_computation.105 | convolution fusion | flops 268435456 | bytes 8978432 | tf_op jit(solution)/shard_map/dot_general | solution.py:1300
  403.4 5.4 %maximum_convert_fusion.1 = f32[2,1728,512]{2,1,0:T(8,128)} fusion(bf16[1,1728,512]{2,1,0:T(8,128)(2,1)} %bitcast.216, bf16[1,1728,512]{2,1,0:T(8,128)(2,1)} %bitcast.215), kind=kLoop, calls=%fused_computation.3 | loop fusion | flops 3538944 | bytes 10616832 | tf_op jit(solution)/shard_map/convert_element_type | solution.py:1350
  418.9 5.1 %all-to-all-done.7 = bf16[4,2,4,4,8,128]{5,4,3,2,1,0:T(8,128)(2,1)} async-done(((bf16[4,2,4,4,8,128]{5,4,3,2,1,0:T(8,128)(2,1)}), bf16[4,2,4,4,8,128]{5,4,3,2,1,0:T(8,128)(2,1)}, u32[]{:S(2)}, u32[]{:S(2)}) %all-to-all-start.7) | async-done | bytes 262176 | tf_op jit(solution)/shard_map/all_to_all | solution.py:969
  425.6 4.9 %maximum_convert_fusion = f32[2,1728,512]{2,1,0:T(8,128)} fusion(bf16[1,1728,512]{2,1,0:T(8,128)(2,1)} %bitcast.217, bf16[1,1728,512]{2,1,0:T(8,128)(2,1)S(1)} %bitcast.204), kind=kLoop, calls=%fused_computation.2 | loop fusion | flops 3538944 | bytes 10616832 | tf_op jit(solution)/shard_map/convert_element_type | solution.py:1340
  (405 shorter events, 240.8 us)
Async XLA Ops:
  7.2 47.9 %all-gather.8.cloned.1.call-start = ((), (), s32[]{:S(2)}) async-start(), calls=%async_computation.9 | async-start | bytes 1179648 | tf_op jit(solution)/shard_map/all_gather | solution.py:1004
  23.8 71.3 %all-gather.18.cloned.1.call-start = ((), (), s32[]{:S(2)}) async-start(), calls=%async_computation.14 | async-start | bytes 1843200 | tf_op jit(solution)/shard_map/all_gather | solution.py:1035
  84.0 28.5 %all-to-all-start = ((bf16[4,1,32,16,128]{4,3,2,1,0:T(8,128)(2,1)}), bf16[4,1,32,16,128]{4,3,2,1,0:T(8,128)(2,1)S(1)}, u32[]{:S(2)}, u32[]{:S(2)}) async-start(bf16[4,1,32,16,128]{4,3,2,1,0:T(8,128)(2,1)} %get-tuple-element.135), calls=%async_computation | async-start | bytes 1048576 | tf_op jit(solution)/shard_map/all_to_all | solution.py:935
  87.4 72.6 %all-gather.10.cloned.1.call-start = ((), (), s32[]{:S(2)}) async-start(), calls=%async_computation.10 | async-start | bytes 2949120 | tf_op jit(solution)/shard_map/all_gather | solution.py:1079
  88.8 23.6 %collective-permute-start.10 = (bf16[32,16,128]{2,1,0:T(8,128)(2,1)}, bf16[32,16,128]{2,1,0:T(8,128)(2,1)}, u32[]{:S(2)}, u32[]{:S(2)}) collective-permute-start(bf16[32,16,128]{2,1,0:T(8,128)(2,1)} %get-tuple-element.132), channel_id=1, source_target_pairs={{0,2},{1,3},{2,4},{3,5},{4,6},{5,7},{6,0},{7,1},{8,10},{9,11},{10,... | collective-permute-start | bytes 393224 | tf_op jit(solution)/shard_map/ppermute | solution.py:28
  122.2 30.3 %all-to-all-start.1 = ((bf16[4,1,32,16,128]{4,3,2,1,0:T(8,128)(2,1)}), bf16[4,1,32,16,128]{4,3,2,1,0:T(8,128)(2,1)S(1)}, u32[]{:S(2)}, u32[]{:S(2)}) async-start(bf16[4,1,32,16,128]{4,3,2,1,0:T(8,128)(2,1)} %get-tuple-element.141), calls=%async_computation.1 | async-start | bytes 1048576 | tf_op jit(solution)/shard_map/all_to_all | solution.py:935
  130.3 22.2 %collective-permute-start.15 = (bf16[32,16,128]{2,1,0:T(8,128)(2,1)S(1)}, bf16[32,16,128]{2,1,0:T(8,128)(2,1)S(1)}, u32[]{:S(2)}, u32[]{:S(2)}) collective-permute-start(bf16[32,16,128]{2,1,0:T(8,128)(2,1)S(1)} %get-tuple-element.142.refs_3_), channel_id=1, source_target_pairs={{0,4},{1,5},{2,6},{3,7},{4,0},{5,1},{6,2},{7,3},{8,12},{9,13},{10,... | collective-permute-start | bytes 393224 | tf_op jit(solution)/shard_map/ppermute | solution.py:28
  154.9 36.0 %all-to-all-start.2 = ((bf16[4,2,32,16,128]{4,3,2,1,0:T(8,128)(2,1)}), bf16[4,2,32,16,128]{4,3,2,1,0:T(8,128)(2,1)}, u32[]{:S(2)}, u32[]{:S(2)}) async-start(bf16[4,2,32,16,128]{4,3,2,1,0:T(8,128)(2,1)} %broadcast_in_dim.33), calls=%async_computation.2 | async-start | bytes 2097152 | tf_op jit(solution)/shard_map/all_to_all | solution.py:935
  204.4 26.8 %all-to-all-start.3 = ((bf16[4,432,512]{2,1,0:T(8,128)(2,1)}), bf16[4,432,512]{2,1,0:T(8,128)(2,1)}, u32[]{:S(2)}, u32[]{:S(2)}) async-start(bf16[4,432,512]{2,1,0:T(8,128)(2,1)} %bitcast.188), calls=%async_computation.3 | async-start | bytes 3538944 | tf_op jit(solution)/shard_map/all_to_all | solution.py:1136
  250.0 35.3 %all-to-all-start.4 = ((bf16[4,432,512]{2,1,0:T(8,128)(2,1)}), bf16[4,432,512]{2,1,0:T(8,128)(2,1)}, u32[]{:S(2)}, u32[]{:S(2)}) async-start(bf16[4,432,512]{2,1,0:T(8,128)(2,1)} %bitcast.48), calls=%async_computation.4 | async-start | bytes 3538944 | tf_op jit(solution)/shard_map/all_to_all | solution.py:1136
  254.4 148.9 %all-gather.14.cloned.1.call-start = ((), (), s32[]{:S(2)}) async-start(), calls=%async_computation.12 | async-start | bytes 2211840 | tf_op jit(solution)/shard_map/all_gather | solution.py:1185
  266.2 23.3 %collective-permute-start.35 = (bf16[4,8,16,512]{3,2,1,0:T(8,128)(2,1)}, bf16[4,8,16,512]{3,2,1,0:T(8,128)(2,1)}, u32[]{:S(2)}, u32[]{:S(2)}) collective-permute-start(bf16[4,8,16,512]{3,2,1,0:T(8,128)(2,1)} %copy-done.39), channel_id=1, source_target_pairs={{0,1},{1,0},{2,3},{3,2},{4,5},{5,4},{6,7},{7,6},{8,9},{9,8},{10,11... | collective-permute-start | bytes 1572872 | tf_op jit(solution)/shard_map/ppermute | solution.py:32
  266.2 23.2 %collective-permute-start.36 = (bf16[4,32,16,128]{3,2,1,0:T(8,128)(2,1)}, bf16[4,32,16,128]{3,2,1,0:T(8,128)(2,1)}, u32[]{:S(2)}, u32[]{:S(2)}) collective-permute-start(bf16[4,32,16,128]{3,2,1,0:T(8,128)(2,1)} %copy-done.26), channel_id=1, source_target_pairs={{0,1},{1,0},{2,3},{3,2},{4,5},{5,4},{6,7},{7,6},{8,9},{9,8},{10,11... | collective-permute-start | bytes 1572872 | tf_op jit(solution)/shard_map/ppermute | solution.py:32
  266.7 22.7 %collective-permute-start.37 = (bf16[4,8,16,512]{3,2,1,0:T(8,128)(2,1)}, bf16[4,8,16,512]{3,2,1,0:T(8,128)(2,1)}, u32[]{:S(2)}, u32[]{:S(2)}) collective-permute-start(bf16[4,8,16,512]{3,2,1,0:T(8,128)(2,1)} %copy-done.40), channel_id=1, source_target_pairs={{0,1},{1,0},{2,3},{3,2},{4,5},{5,4},{6,7},{7,6},{8,9},{9,8},{10,11... | collective-permute-start | bytes 1572872 | tf_op jit(solution)/shard_map/ppermute | solution.py:32
  292.3 42.0 %all-to-all-start.5 = ((bf16[4,3,32,16,128]{4,3,2,1,0:T(8,128)(2,1)}), bf16[4,3,32,16,128]{4,3,2,1,0:T(8,128)(2,1)}, u32[]{:S(2)}, u32[]{:S(2)}) async-start(bf16[4,3,32,16,128]{4,3,2,1,0:T(8,128)(2,1)} %get-tuple-element.204), calls=%async_computation.5 | async-start | bytes 3145728 | tf_op jit(solution)/shard_map/all_to_all | solution.py:935
  297.1 106.3 %all-gather.16.cloned.1.call-start = ((), (), s32[]{:S(2)}) async-start(), calls=%async_computation.13 | async-start | bytes 2211840 | tf_op jit(solution)/shard_map/all_gather | solution.py:1214
  302.8 25.6 %collective-permute-start.40 = (bf16[432,512]{1,0:T(8,128)(2,1)}, bf16[432,512]{1,0:T(8,128)(2,1)S(1)}, u32[]{:S(2)}, u32[]{:S(2)}) collective-permute-start(bf16[432,512]{1,0:T(8,128)(2,1)} %get-tuple-element.250), channel_id=1, source_target_pairs={{0,24},{8,16},{16,8},{24,0},{1,25},{9,17},{17,9},{25,1},{2,26},{10... | collective-permute-start | bytes 1327112 | tf_op jit(solution)/shard_map/ppermute | solution.py:1228
  304.3 24.9 %collective-permute-start.39 = (bf16[432,512]{1,0:T(8,128)(2,1)}, bf16[432,512]{1,0:T(8,128)(2,1)}, u32[]{:S(2)}, u32[]{:S(2)}) collective-permute-start(bf16[432,512]{1,0:T(8,128)(2,1)} %get-tuple-element.251), channel_id=1, source_target_pairs={{0,16},{8,24},{16,0},{24,8},{1,17},{9,25},{17,1},{25,9},{2,18},{10... | collective-permute-start | bytes 1327112 | tf_op jit(solution)/shard_map/ppermute | solution.py:1228
  334.3 33.9 %all-to-all-start.8 = ((bf16[4,432,512]{2,1,0:T(8,128)(2,1)}), bf16[4,432,512]{2,1,0:T(8,128)(2,1)S(1)}, u32[]{:S(2)}, u32[]{:S(2)}) async-start(bf16[4,432,512]{2,1,0:T(8,128)(2,1)} %bitcast.73), calls=%async_computation.8 | async-start | bytes 3538944 | tf_op jit(solution)/shard_map/all_to_all | solution.py:1136
  338.3 87.4 %all-gather.12.cloned.1.call-start = ((), (), s32[]{:S(2)}) async-start(), calls=%async_computation.11 | async-start | bytes 2211840 | tf_op jit(solution)/shard_map/all_gather | solution.py:1250
  373.7 38.9 %all-to-all-start.6 = ((bf16[8,2,32,2,128]{4,2,3,1,0:T(8,128)(2,1)}), bf16[8,2,32,2,128]{4,2,3,1,0:T(8,128)(2,1)S(1)}, u32[]{:S(2)}, u32[]{:S(2)}) async-start(bf16[8,2,32,2,128]{4,2,3,1,0:T(8,128)(2,1)} %bitcast.184), calls=%async_computation.6 | async-start | bytes 524288 | tf_op jit(solution)/shard_map/all_to_all | solution.py:964
  378.3 30.5 %collective-permute-start.43 = (bf16[432,512]{1,0:T(8,128)(2,1)S(1)}, bf16[432,512]{1,0:T(8,128)(2,1)}, u32[]{:S(2)}, u32[]{:S(2)}) collective-permute-start(bf16[432,512]{1,0:T(8,128)(2,1)S(1)} %get-tuple-element.209), channel_id=1, source_target_pairs={{0,24},{8,16},{16,8},{24,0},{1,25},{9,17},{17,9},{25,1},{2,26},{10... | collective-permute-start | bytes 1327112 | tf_op jit(solution)/shard_map/ppermute | solution.py:1228
  378.6 31.3 %collective-permute-start.42 = (bf16[432,512]{1,0:T(8,128)(2,1)S(1)}, bf16[432,512]{1,0:T(8,128)(2,1)}, u32[]{:S(2)}, u32[]{:S(2)}) collective-permute-start(bf16[432,512]{1,0:T(8,128)(2,1)S(1)} %get-tuple-element.209), channel_id=1, source_target_pairs={{0,16},{8,24},{16,0},{24,8},{1,17},{9,25},{17,1},{25,9},{2,18},{10... | collective-permute-start | bytes 1327112 | tf_op jit(solution)/shard_map/ppermute | solution.py:1228
  382.6 28.2 %collective-permute-start.41 = (bf16[432,512]{1,0:T(8,128)(2,1)S(1)}, bf16[432,512]{1,0:T(8,128)(2,1)}, u32[]{:S(2)}, u32[]{:S(2)}) collective-permute-start(bf16[432,512]{1,0:T(8,128)(2,1)S(1)} %get-tuple-element.209), channel_id=1, source_target_pairs={{0,8},{8,0},{16,24},{24,16},{1,9},{9,1},{17,25},{25,17},{2,10},{10... | collective-permute-start | bytes 1327112 | tf_op jit(solution)/shard_map/ppermute | solution.py:1228
  (105 other events, 676.7 us)
Sparse Core Ops, SparseCore 0:
  23.9 31.1 all-gather.7
  62.5 24.5 all-gather.17
  118.9 38.3 all-gather.9
  266.9 32.5 all-gather.13
  304.9 58.9 all-gather.15
  369.5 47.2 all-gather.11
